TPU v7x, 32 devices: a whole 2x2x4 slice. The times are simulated.
32 devices in a mesh: grid: 8 (over z, y), member: 4 (over x, core).
Axes of the slice: x: 2, y: 2, z: 4, core: 2. Of those that a mesh axis runs over, the one named last changes fastest.
Arguments:
- latent: bfloat16 [8, 2560, 1024], P('member', 'grid'), may hold values from -6 to 6
- grid_feat: bfloat16 [1024, 1024], P('grid'), may hold values from -6 to 6
- w_query: bfloat16 [1024, 1024], replicated, may hold values from -0.1875 to 0.1875
- w_key: bfloat16 [1024, 1024], replicated, may hold values from -0.1875 to 0.1875
- w_value: bfloat16 [1024, 1024], replicated, may hold values from -0.1875 to 0.1875
- w_out: bfloat16 [96, 1024], replicated, may hold values from -0.1875 to 0.1875
- truth: float32 [96, 1024], P(None, 'grid'), may hold values from -6 to 6
- area: float32 [1024], P('grid'), may hold values from 1 to 10
- var_weight: float32 [96], replicated, may hold values from 1 to 10
- send_rows: int32 [8, 8, 24], P('grid'), may hold values from 0 to 319, as said below
- neighbours: int32 [1024, 16], P('grid'), may hold values from 0 to 191, as said below
- live_count: int32 [1024], P('grid'), may hold values from 8 to 16
Outputs:
- latent_grad: float32 [8, 2560, 1024], P('member', 'grid')
Inputs may be any that keep to these rules, and one draw needn't show every extreme that they name: send_rows[s, d, c] is the row, local to owner s, that owner s sends to grid device d in place c; the 24 entries of one s and d are distinct. neighbours[g, k] = s * 24 + c names place c of what owner s sends to the grid device of point g; every place named is one that some point of that device uses, and on some device every place of every owner is used; slots k >= live_count[g] are ignored.
All inputs are finite; a program needn't handle non-finite values.
Results may differ from a plain program's by a relative error of at most 0.0078.
Values may be sent and summed in bfloat16 or wider, within the bound.
No kernel may reach another device: no remote copies, remote signals or barrier semaphores. Data moves between devices by JAX's collectives and lax.ppermute only.
A program may use at most 128 MiB of HBM per device.

v0:
```python
import jax
import jax.numpy as jnp
from jax import lax
from jax.sharding import PartitionSpec as P

H = 16


def ensemble_gradient(everyone, mine, truth, area, var_weight):
    total = everyone.shape[0]
    miss = mine - truth[None]
    first = miss / jnp.sqrt(1.0 + miss * miss) / total
    paired = mine[:, None] - everyone[None]
    second = jnp.sum(paired / jnp.sqrt(1.0 + paired * paired), axis=1) / (total * (total - 1))
    return area[None, None, :] * var_weight[None, :, None] * (first - second)


def on_device(
    latent,
    grid_feat,
    w_query,
    w_key,
    w_value,
    w_out,
    truth,
    area,
    var_weight,
    send_rows,
    neighbours,
    live_count,
):
    f32 = jnp.float32
    bf16 = jnp.bfloat16
    highest = lax.Precision.HIGHEST
    members_here = latent.shape[0]
    own_rows = latent.shape[1]
    width = latent.shape[2]
    points = grid_feat.shape[0]
    slots = neighbours.shape[1]
    head_size = width // H
    scale = head_size ** (-0.5)
    owners = send_rows.shape[1]
    capacity = send_rows.shape[2]
    received = owners * capacity
    rows_out = send_rows[0].reshape(-1)
    query = jnp.dot(grid_feat, w_query, preferred_element_type=f32).astype(bf16)
    query_heads = query.reshape(points, H, head_size)
    outgoing = latent[:, rows_out, :].reshape(members_here, owners, capacity, width)
    arrived = lax.all_to_all(outgoing, "grid", split_axis=1, concat_axis=1, tiled=True)
    rows_in = arrived.reshape(arrived.shape[0], -1, width)
    keys_in = jnp.einsum("mrd,de->mre", rows_in, w_key, preferred_element_type=f32).astype(bf16)
    values_in = jnp.einsum("mrd,de->mre", rows_in, w_value, preferred_element_type=f32).astype(bf16)
    live = jnp.arange(slots)[None, :] < live_count[:, None]
    row_ids = jnp.arange(received, dtype=jnp.int32)
    matches = (neighbours[:, :, None] == row_ids[None, None, :]) & live[:, :, None]
    mult = jnp.sum(matches.astype(f32), axis=1)
    named = (mult > 0.0)[:, None, :]
    mult_heads = mult[:, None, :]
    kept_probs, kept_values, predictions = ([], [], [])
    for member in range(members_here):
        keys_heads = keys_in[member].reshape(received, H, head_size)
        values_heads = values_in[member].reshape(received, H, head_size)
        scores = (
            jnp.einsum("ghd,rhd->ghr", query_heads, keys_heads, preferred_element_type=f32) * scale
        )
        raised = jnp.where(named, jnp.exp(jnp.where(named, scores, 0.0)), 0.0)
        denom = jnp.sum(mult_heads * raised, axis=2, keepdims=True)
        probs = (raised / denom).astype(bf16)
        weights = mult_heads * probs.astype(f32)
        attended = jnp.einsum(
            "ghr,rhd->ghd", weights, values_heads.astype(f32), precision=highest
        ).astype(bf16)
        predictions.append(
            jnp.einsum(
                "vd,gd->vg", w_out, attended.reshape(points, width), preferred_element_type=f32
            )
        )
        kept_probs.append(probs)
        kept_values.append(values_heads)
    predicted = jnp.stack(predictions)
    everyone = lax.all_gather(predicted, "member", axis=0, tiled=True)
    score_grads = ensemble_gradient(everyone, predicted, truth, area, var_weight).astype(bf16)
    query_wide = query_heads.astype(f32)
    key_terms, value_terms = ([], [])
    for member in range(members_here):
        probs_wide = kept_probs[member].astype(f32)
        d_attended = jnp.einsum(
            "vg,vd->gd", score_grads[member], w_out, preferred_element_type=f32
        ).astype(bf16)
        d_attended = d_attended.reshape(points, H, head_size)
        d_probs = jnp.einsum(
            "ghd,rhd->ghr", d_attended, kept_values[member], preferred_element_type=f32
        )
        weights = mult_heads * probs_wide
        inner = jnp.sum(weights * d_probs, axis=2, keepdims=True)
        d_scores = probs_wide * (d_probs - inner) * scale
        key_weights = mult_heads * d_scores
        d_keys = jnp.einsum("ghr,ghd->rhd", key_weights, query_wide, precision=highest).reshape(
            received, width
        )
        d_values = jnp.einsum(
            "ghr,ghd->rhd", weights, d_attended.astype(f32), precision=highest
        ).reshape(received, width)
        key_terms.append(d_keys)
        value_terms.append(d_values)
    key_terms = jnp.stack(key_terms)
    value_terms = jnp.stack(value_terms)
    key_wide = w_key.astype(f32)
    value_wide = w_value.astype(f32)
    results = []
    row_terms = jnp.einsum("mre,de->mrd", key_terms, key_wide, precision=highest)
    row_terms = row_terms + jnp.einsum("mre,de->mrd", value_terms, value_wide, precision=highest)
    returned = lax.all_to_all(
        row_terms.reshape(members_here, owners, capacity, width),
        "grid",
        split_axis=1,
        concat_axis=1,
        tiled=True,
    )
    for member in range(members_here):
        results.append(
            jax.ops.segment_sum(
                returned[member].reshape(-1, width), rows_out, num_segments=own_rows
            )
        )
    return jnp.stack(results)


def solution(mesh):
    return jax.shard_map(
        on_device,
        mesh=mesh,
        in_specs=(
            P("member", "grid", None),
            P("grid", None),
            P(),
            P(),
            P(),
            P(),
            P(None, "grid"),
            P("grid"),
            P(),
            P("grid", None, None),
            P("grid", None),
            P("grid"),
        ),
        out_specs=P("member", "grid", None),
        check_vma=False,
    )
```

profile of v0, /device:TPU:0, one launch (start us, length us, event | category | flops | bytes accessed | tf_op | source)
XLA Modules:
  0.0 158.7 jit_solution(11553747500265202055)
XLA Ops:
  0.9 6.1 %gather_fusion = bf16[192,2,1024]{2,0,1:T(8,128)(2,1)S(1)} fusion(bf16[2,320,1024]{2,1,0:T(8,128)(2,1)} %param.12, s32[1024]{0:T(1024)S(1)} %pad_clamp_fusion), kind=kCustom, calls=%fused_computation | custom fusion | bytes 1573632 | tf_op jit(solution)/shard_map/gather | solution.py:48
  8.0 7.3 %all-to-all-start = ((bf16[2,8,24,1024]{3,2,0,1:T(8,128)(2,1)}), bf16[2,8,24,1024]{3,2,0,1:T(8,128)(2,1)S(1)}, u32[]{:S(2)}, u32[]{:S(2)}) async-start(bf16[2,8,24,1024]{3,2,0,1:T(8,128)(2,1)} %copy.60), calls=%async_computation | async-start | bytes 1572864 | tf_op jit(solution)/shard_map/all_to_all | solution.py:49
  15.3 2.0 %convolution_convert_fusion.2 = bf16[128,1024]{1,0:T(8,128)(2,1)S(1)} fusion(bf16[128,1024]{1,0:T(8,128)(2,1)S(1)} %copy-done.20, bf16[1024,1024]{1,0:T(8,128)(2,1)} %param.14), kind=kOutput, calls=%fused_computation.58 | convolution fusion | flops 268566528 | bytes 2621440 | tf_op jit(solution)/shard_map/dot_general | solution.py:46
  19.3 16.2 %all-to-all-done = bf16[2,8,24,1024]{3,2,0,1:T(8,128)(2,1)S(1)} async-done(((bf16[2,8,24,1024]{3,2,0,1:T(8,128)(2,1)}), bf16[2,8,24,1024]{3,2,0,1:T(8,128)(2,1)S(1)}, u32[]{:S(2)}, u32[]{:S(2)}) %all-to-all-start) | async-done | bytes 786464 | tf_op jit(solution)/shard_map/all_to_all | solution.py:49
  35.5 2.9 %fusion.46 = bf16[2,192,1024]{2,1,0:T(8,128)(2,1)S(1)} fusion(bf16[2,192,1024]{2,1,0:T(8,128)(2,1)S(1)} %bitcast.135, bf16[1024,1024]{1,0:T(8,128)(2,1)} %param.15), kind=kOutput, calls=%fused_computation.54 | convolution fusion | flops 805699584 | bytes 3670016 | tf_op jit(solution)/shard_map/mrd,de->mre/dot_general | solution.py:51
  40.2 1.6 fusion.33
  44.8 2.0 %copy.63 = bf16[1,192,1024]{1,2,0:T(8,128)(2,1)} copy(bf16[1,192,1024]{2,1,0:T(8,128)(2,1)} %get-tuple-element.11) | data formatting | bytes 786432 | tf_op jit(solution)/shard_map/slice | solution.py:62
  46.8 2.0 %copy.65 = bf16[1,192,1024]{1,2,0:T(8,128)(2,1)} copy(bf16[1,192,1024]{2,1,0:T(8,128)(2,1)} %get-tuple-element.10) | data formatting | bytes 786432 | tf_op jit(solution)/shard_map/slice | solution.py:61
  48.8 1.6 fusion.31
  52.8 2.2 %fusion.52 = bf16[16,64,128]{2,1,0:T(8,128)(2,1)S(1)} fusion(bf16[192,16,64]{0,2,1:T(8,128)(2,1)} %bitcast.118, bf16[128,16,192]{0,2,1:T(8,128)(2,1)S(1)} %divide_convert_fusion.1, f32[128,192]{0,1:T(8,128)S(1)} %convert_reduce_fusion), kind=kOutput, calls=%fused_computation.59 | convolution fusion | flops 302907392 | bytes 1540096 | tf_op jit(solution)/shard_map/ghr,rhd->ghd/dot_general | solution.py:70
  56.6 6.6 %all_gather.3 = f32[8,96,128]{2,1,0:T(8,128)S(1)} all-gather(f32[2,96,128]{2,1,0:T(8,128)S(1)} %pad_maximum_fusion.1), channel_id=1, replica_groups=mesh['grid'=8,'member'=4] {'member'}, dimensions={0}, use_global_device_ids=true | all-gather | bytes 491520 | tf_op jit(solution)/shard_map/all_gather | solution.py:81
  65.4 1.8 %copy.67 = bf16[128,1024]{0,1:T(8,128)(2,1)} copy(bf16[128,1024]{1,0:T(8,128)(2,1)} %convolution_convert_fusion) | data formatting | bytes 524288 | tf_op jit(solution)/shard_map/convert_element_type | solution.py:89
  67.2 2.6 %fusion.76 = f32[16,192,128]{2,1,0:T(8,128)} fusion(bf16[192,16,64]{0,2,1:T(8,128)(2,1)S(1)} %bitcast.117, bf16[128,16,64]{0,2,1:T(8,128)(2,1)} %bitcast.131), kind=kOutput, calls=%fused_computation.97 | convolution fusion | flops 50331648 | bytes 2228224 | tf_op jit(solution)/shard_map/ghd,rhd->ghr/dot_general | solution.py:91
  69.8 2.6 %fusion.10 = f32[16,64,192]{2,1,0:T(8,128)} fusion(bf16[128,16,64]{0,2,1:T(8,128)(2,1)S(1)} %bitcast.132, bf16[128,16,192]{0,2,1:T(8,128)(2,1)S(1)} %copy-done.3, f32[128,192]{0,1:T(8,128)S(1)} %convert_reduce_fusion), kind=kOutput, calls=%fused_computation.16 | convolution fusion | flops 302776320 | bytes 1933312 | tf_op jit(solution)/shard_map/ghr,ghd->rhd/dot_general | solution.py:101
  72.4 1.9 %copy.66 = bf16[128,1024]{0,1:T(8,128)(2,1)} copy(bf16[128,1024]{1,0:T(8,128)(2,1)} %convolution_convert_fusion.1) | data formatting | bytes 524288 | tf_op jit(solution)/shard_map/convert_element_type | solution.py:89
  74.3 3.7 %fusion.13 = f32[16,64,192]{2,1,0:T(8,128)} fusion(bf16[128,16,64]{0,2,1:T(8,128)(2,1)} %bitcast.129, bf16[128,16,192]{0,2,1:T(8,128)(2,1)S(1)} %divide_convert_fusion.1, f32[128,192]{0,1:T(8,128)S(1)} %convert_reduce_fusion), kind=kOutput, calls=%fused_computation.21 | convolution fusion | flops 302776320 | bytes 1933312 | tf_op jit(solution)/shard_map/ghr,ghd->rhd/dot_general | solution.py:101
  78.0 1.9 %fusion.16 = (f32[128,16]{0,1:T(8,128)S(1)}, f32[128,16]{0,1:T(8,128)S(1)}, f32[16,192,128]{2,1,0:T(8,128)S(1)}) fusion(bf16[128,16,192]{0,2,1:T(8,128)(2,1)S(1)} %divide_convert_fusion.1, f32[128,192]{0,1:T(8,128)S(1)} %convert_reduce_fusion, f32[16,192,128]{2,1,0:T(8,128)S(1)} %copy-done.1, bf16[128,16,192]{0,2,1:T(8,128)(2,1)} %divide_convert_fusion, ...), kind=kOutput, calls=%fused_computation.24 | convolution fusion | flops 53473280 | bytes 5488640 | tf_op jit(solution)/shard_map/ghd,rhd->ghr/dot_general | solution.py:91
  80.0 2.7 %fusion.18 = f32[16,64,192]{2,1,0:T(8,128)} fusion(bf16[128,16,64]{0,2,1:T(8,128)(2,1)S(1)} %bitcast.127, bf16[128,16,192]{0,2,1:T(8,128)(2,1)S(1)} %divide_convert_fusion.1, f32[16,192,128]{2,1,0:T(8,128)S(1)} %get-tuple-element.13, f32[128,192]{0,1:T(8,128)S(1)} %copy-done.16, f32[128,16]{0,1:T(8,128)S(1)} %get-tuple-element.5), kind=kOutput, calls=%fused_computation.26 | convolution fusion | flops 303562752 | bytes 3514368 | tf_op jit(solution)/shard_map/ghr,ghd->rhd/dot_general | solution.py:98
  82.7 2.5 %copy.68 = f32[1,192,1024]{2,1,0:T(8,128)} copy(f32[1,192,1024]{1,2,0:T(8,128)} %bitcast.121) | data formatting | bytes 1572864 | tf_op jit(solution)/shard_map/stack;reshape | solution.py:106
  85.3 4.1 %fusion.22 = f32[16,64,192]{2,1,0:T(8,128)} fusion(bf16[128,16,64]{0,2,1:T(8,128)(2,1)S(1)} %bitcast.128, bf16[128,16,192]{0,2,1:T(8,128)(2,1)S(1)} %copy-done.4, f32[16,192,128]{2,1,0:T(8,128)} %fusion.76, f32[128,16]{0,1:T(8,128)S(1)} %get-tuple-element.6, f32[128,192]{0,1:T(8,128)S(1)} %copy-done.17), kind=kOutput, calls=%fused_computation.29 | convolution fusion | flops 303562752 | bytes 3514368 | tf_op jit(solution)/shard_map/ghr,ghd->rhd/dot_general | solution.py:98
  89.3 2.5 %copy.69 = f32[1,192,1024]{2,1,0:T(8,128)} copy(f32[1,192,1024]{1,2,0:T(8,128)} %bitcast.120) | data formatting | bytes 1572864 | tf_op jit(solution)/shard_map/stack;reshape | solution.py:106
  91.9 2.4 %copy.70 = f32[1,192,1024]{2,1,0:T(8,128)} copy(f32[1,192,1024]{1,2,0:T(8,128)} %bitcast.123) | data formatting | bytes 1572864 | tf_op jit(solution)/shard_map/stack;reshape | solution.py:107
  94.3 1.2 copy.71
  95.5 4.2 %fusion.2 = f32[2,192,1024]{2,1,0:T(8,128)S(1)} fusion(bf16[1024,1024]{1,0:T(8,128)(2,1)S(1)} %copy-done, f32[1,192,1024]{2,1,0:T(8,128)} %copy.71, f32[1,192,1024]{2,1,0:T(8,128)} %copy.70), kind=kOutput, calls=%fused_computation.6 | convolution fusion | flops 4832231424 | bytes 5242880 | tf_op jit(solution)/shard_map/mre,de->mrd/dot_general | solution.py:112
  99.7 2.9 %fusion.41 = f32[2,192,1024]{2,1,0:T(8,128)S(1)} fusion(f32[2,192,1024]{2,1,0:T(8,128)S(1)} %fusion.2, bf16[1024,1024]{1,0:T(8,128)(2,1)S(1)} %copy-done.15, f32[1,192,1024]{2,1,0:T(8,128)S(1)} %copy-done.8, f32[1,192,1024]{2,1,0:T(8,128)S(1)} %copy-done.7), kind=kOutput, calls=%fused_computation.53 | convolution fusion | flops 4832624640 | bytes 6815744 | tf_op jit(solution)/shard_map/mre,de->mrd/dot_general | solution.py:111
  102.6 1.2 copy.72
  103.9 4.4 %all-to-all-start.1 = ((f32[2,8,24,1024]{3,2,0,1:T(8,128)}), f32[2,8,24,1024]{3,2,0,1:T(8,128)}, u32[]{:S(2)}, u32[]{:S(2)}) async-start(f32[2,8,24,1024]{3,2,0,1:T(8,128)} %copy.72), calls=%async_computation.1 | async-start | bytes 3145728 | tf_op jit(solution)/shard_map/all_to_all | solution.py:113
  108.4 37.7 %all-to-all-done.1 = f32[2,8,24,1024]{3,2,0,1:T(8,128)} async-done(((f32[2,8,24,1024]{3,2,0,1:T(8,128)}), f32[2,8,24,1024]{3,2,0,1:T(8,128)}, u32[]{:S(2)}, u32[]{:S(2)}) %all-to-all-start.1) | async-done | bytes 1572896 | tf_op jit(solution)/shard_map/all_to_all | solution.py:113
  146.1 2.7 %fusion.73 = (f32[1,8,24,1024]{3,2,0,1:T(8,128)}, f32[1,8,24,1024]{3,2,0,1:T(8,128)}) fusion(f32[2,8,24,1024]{3,2,0,1:T(8,128)} %all-to-all-done.1), kind=kLoop, calls=%fused_computation.94 | loop fusion | bytes 3145728 | tf_op jit(solution)/shard_map/slice | solution.py:123
  148.8 3.0 %scatter_custom_fusion = f32[320,1024]{1,0:T(8,128)S(1)} fusion(s32[192]{0:T(256)S(1)} %reshape.135, f32[192,1024]{1,0:T(8,128)} %bitcast.138, f32[]{:T(128)} %constant.6.clone.1), kind=kCustom, calls=%fused_computation.80 | custom fusion | flops 196608 | bytes 1311232 | tf_op jit(solution)/shard_map/scatter-add | solution.py:122
  151.8 3.8 %scatter_custom_fusion.1 = f32[320,1024]{1,0:T(8,128)} fusion(s32[192]{0:T(256)S(1)} %reshape.135, f32[192,1024]{1,0:T(8,128)} %bitcast.137, f32[]{:T(128)} %constant.6.clone.1), kind=kCustom, calls=%fused_computation.78 | custom fusion | flops 196608 | bytes 1311232 | tf_op jit(solution)/shard_map/scatter-add | solution.py:122
  155.6 3.1 %pad_maximum_fusion = f32[2,320,1024]{2,1,0:T(8,128)} fusion(f32[1,320,1024]{2,1,0:T(8,128)} %bitcast.115, f32[1,320,1024]{2,1,0:T(8,128)S(1)} %bitcast.114), kind=kLoop, calls=%fused_computation.5 | loop fusion | flops 655360 | bytes 5242880 | tf_op jit(solution)/shard_map/stack | solution.py:126
  (77 shorter events, 14.8 us)
Async XLA Ops:
  0.0 42.1 %copy-start = (bf16[1024,1024]{1,0:T(8,128)(2,1)S(1)}, bf16[1024,1024]{1,0:T(8,128)(2,1)}, u32[]{:S(2)}) copy-start(bf16[1024,1024]{1,0:T(8,128)(2,1)} %param.16) | copy-start | bytes 6291460
  7.0 8.2 %copy-start.20 = (bf16[128,1024]{1,0:T(8,128)(2,1)S(1)}, bf16[128,1024]{1,0:T(8,128)(2,1)}, u32[]{:S(2)}) copy-start(bf16[128,1024]{1,0:T(8,128)(2,1)} %param.13) | copy-start | bytes 786436
  8.0 27.5 %all-to-all-start = ((bf16[2,8,24,1024]{3,2,0,1:T(8,128)(2,1)}), bf16[2,8,24,1024]{3,2,0,1:T(8,128)(2,1)S(1)}, u32[]{:S(2)}, u32[]{:S(2)}) async-start(bf16[2,8,24,1024]{3,2,0,1:T(8,128)(2,1)} %copy.60), calls=%async_computation | async-start | bytes 1572864 | tf_op jit(solution)/shard_map/all_to_all | solution.py:49
  15.3 2.3 %copy-start.24 = (s32[128]{0:T(128)S(1)}, s32[128]{0:T(128)}, u32[]{:S(2)}) copy-start(s32[128]{0:T(128)} %param.23) | copy-start | bytes 1540
  15.3 2.3 %copy-start.23 = (s32[128,16]{0,1:T(8,128)S(1)}, s32[128,16]{0,1:T(8,128)}, u32[]{:S(2)}) copy-start(s32[128,16]{0,1:T(8,128)} %param.22) | copy-start | bytes 24580
  17.5 31.3 %copy-start.10 = (bf16[128,1024]{0,1:T(8,128)(2,1)}, bf16[128,1024]{0,1:T(8,128)(2,1)S(1)}, u32[]{:S(2)}) copy-start(bf16[128,1024]{0,1:T(8,128)(2,1)S(1)} %copy.59) | copy-start | bytes 786436
  35.5 2.9 %copy-start.18 = (bf16[2,8,24,1024]{3,2,1,0:T(8,128)(2,1)}, bf16[2,8,24,1024]{3,2,1,0:T(8,128)(2,1)S(1)}, u32[]{:S(2)}) copy-start(bf16[2,8,24,1024]{3,2,1,0:T(8,128)(2,1)S(1)} %copy.61) | copy-start | bytes 2359300
  41.8 1.1 copy-start.19
  52.8 2.3 %copy-start.9 = (bf16[96,1024]{1,0:T(8,128)(2,1)S(1)}, bf16[96,1024]{1,0:T(8,128)(2,1)}, u32[]{:S(2)}) copy-start(bf16[96,1024]{1,0:T(8,128)(2,1)} %param.17) | copy-start | bytes 589828
  52.8 2.5 %copy-start.2 = (bf16[128,16,192]{0,2,1:T(8,128)(2,1)S(1)}, bf16[128,16,192]{0,2,1:T(8,128)(2,1)}, u32[]{:S(2)}) copy-start(bf16[128,16,192]{0,2,1:T(8,128)(2,1)} %divide_convert_fusion) | copy-start | bytes 2359300
  55.3 8.1 %copy-start.21 = (f32[96,128]{1,0:T(8,128)S(1)}, f32[96,128]{1,0:T(8,128)}, u32[]{:S(2)}) copy-start(f32[96,128]{1,0:T(8,128)} %param.18) | copy-start | bytes 147460
  67.2 2.6 %copy-start.3 = (bf16[128,16,192]{0,2,1:T(8,128)(2,1)S(1)}, bf16[128,16,192]{0,2,1:T(8,128)(2,1)}, u32[]{:S(2)}) copy-start(bf16[128,16,192]{0,2,1:T(8,128)(2,1)} %divide_convert_fusion) | copy-start | bytes 2359300
  67.2 2.6 %copy-start.14 = (bf16[128,1024]{0,1:T(8,128)(2,1)S(1)}, bf16[128,1024]{0,1:T(8,128)(2,1)}, u32[]{:S(2)}) copy-start(bf16[128,1024]{0,1:T(8,128)(2,1)} %copy.67) | copy-start | bytes 786436
  72.4 5.6 %copy-start.5 = (bf16[1,192,1024]{1,2,0:T(8,128)(2,1)S(1)}, bf16[1,192,1024]{1,2,0:T(8,128)(2,1)}, u32[]{:S(2)}) copy-start(bf16[1,192,1024]{1,2,0:T(8,128)(2,1)} %copy.63) | copy-start | bytes 1179652
  74.3 3.7 %copy-start.1 = (f32[16,192,128]{2,1,0:T(8,128)S(1)}, f32[16,192,128]{2,1,0:T(8,128)}, u32[]{:S(2)}) copy-start(f32[16,192,128]{2,1,0:T(8,128)} %fusion.76) | copy-start | bytes 4718596
  74.3 3.7 %copy-start.13 = (bf16[128,1024]{0,1:T(8,128)(2,1)S(1)}, bf16[128,1024]{0,1:T(8,128)(2,1)}, u32[]{:S(2)}) copy-start(bf16[128,1024]{0,1:T(8,128)(2,1)} %copy.66) | copy-start | bytes 786436
  78.0 2.0 %copy-start.11 = (bf16[128,1024]{0,1:T(8,128)(2,1)S(1)}, bf16[128,1024]{0,1:T(8,128)(2,1)}, u32[]{:S(2)}) copy-start(bf16[128,1024]{0,1:T(8,128)(2,1)} %copy-done.10) | copy-start | bytes 786436
  78.0 2.0 %copy-start.16 = (f32[128,192]{0,1:T(8,128)S(1)}, f32[128,192]{0,1:T(8,128)}, u32[]{:S(2)}) copy-start(f32[128,192]{0,1:T(8,128)} %broadcast_multiply_fusion) | copy-start | bytes 294916
  82.7 2.5 %copy-start.4 = (bf16[128,16,192]{0,2,1:T(8,128)(2,1)S(1)}, bf16[128,16,192]{0,2,1:T(8,128)(2,1)}, u32[]{:S(2)}) copy-start(bf16[128,16,192]{0,2,1:T(8,128)(2,1)} %divide_convert_fusion) | copy-start | bytes 2359300
  82.7 2.5 %copy-start.12 = (bf16[128,1024]{0,1:T(8,128)(2,1)S(1)}, bf16[128,1024]{0,1:T(8,128)(2,1)}, u32[]{:S(2)}) copy-start(bf16[128,1024]{0,1:T(8,128)(2,1)} %copy-done.10) | copy-start | bytes 786436
  82.7 2.5 %copy-start.17 = (f32[128,192]{0,1:T(8,128)S(1)}, f32[128,192]{0,1:T(8,128)}, u32[]{:S(2)}) copy-start(f32[128,192]{0,1:T(8,128)} %broadcast_multiply_fusion) | copy-start | bytes 294916
  89.3 4.9 %copy-start.6 = (f32[16,64,192]{2,1,0:T(8,128)S(1)}, f32[16,64,192]{2,1,0:T(8,128)}, u32[]{:S(2)}) copy-start(f32[16,64,192]{2,1,0:T(8,128)} %fusion.10) | copy-start | bytes 2359300
  95.5 4.2 %copy-start.7 = (f32[1,192,1024]{2,1,0:T(8,128)S(1)}, f32[1,192,1024]{2,1,0:T(8,128)}, u32[]{:S(2)}) copy-start(f32[1,192,1024]{2,1,0:T(8,128)} %copy.68) | copy-start | bytes 2359300
  95.5 4.2 %copy-start.8 = (f32[1,192,1024]{2,1,0:T(8,128)S(1)}, f32[1,192,1024]{2,1,0:T(8,128)}, u32[]{:S(2)}) copy-start(f32[1,192,1024]{2,1,0:T(8,128)} %copy.69) | copy-start | bytes 2359300
  95.5 4.2 %copy-start.15 = (bf16[1024,1024]{1,0:T(8,128)(2,1)S(1)}, bf16[1024,1024]{1,0:T(8,128)(2,1)}, u32[]{:S(2)}) copy-start(bf16[1024,1024]{1,0:T(8,128)(2,1)} %param.15) | copy-start | bytes 6291460
  103.9 4.4 %copy-start.22 = (s32[1,8,24]{2,1,0:T(8,128)S(1)}, s32[1,8,24]{2,1,0:T(8,128)}, u32[]{:S(2)}) copy-start(s32[1,8,24]{2,1,0:T(8,128)} %param.21) | copy-start | bytes 2308
  103.9 42.2 %all-to-all-start.1 = ((f32[2,8,24,1024]{3,2,0,1:T(8,128)}), f32[2,8,24,1024]{3,2,0,1:T(8,128)}, u32[]{:S(2)}, u32[]{:S(2)}) async-start(f32[2,8,24,1024]{3,2,0,1:T(8,128)} %copy.72), calls=%async_computation.1 | async-start | bytes 3145728 | tf_op jit(solution)/shard_map/all_to_all | solution.py:113
where the time goes:
time: 160 us; the launch traced here: 159 us
  waiting for transfers between devices  53.9 us (34%)
  matrix products  39.5 us (25%)
  local copies, waits for them, and re-layouts  33.3 us (21%)
  other arithmetic  13.3 us (8%)
  starting transfers between devices  11.7 us (7%)
  blocking collectives  6.64 us (4%)
    all_to_all x1, waiting for transfers between devices, on_device(): lax.all_to_all(row_terms.reshape(members_here, owners, capacity, width),...  37.7 us
    all_to_all x1, waiting for transfers between devices, on_device(): lax.all_to_all(outgoing, 'grid', split_axis=1, concat_axis=1, tiled=True)  16.2 us
    all_to_all x1, starting transfers between devices, on_device(): lax.all_to_all(outgoing, 'grid', split_axis=1, concat_axis=1, tiled=True)  7.28 us
    scatter-add x2, other arithmetic, on_device(): jax.ops.segment_sum(returned[member].reshape(-1, width), rows_out, num_se...  6.85 us
    dot_general x2, matrix products, on_device(): jnp.einsum('ghr,ghd->rhd', key_weights, query_wide, precision=highest)  6.81 us
    all_gather x1, blocking collectives, on_device(): everyone = lax.all_gather(predicted, 'member', axis=0, tiled=True)  6.64 us
    dot_general x2, matrix products, on_device(): jnp.einsum('ghr,ghd->rhd', weights, d_attended.astype(f32), precision=hig...  6.31 us
    gather x1, local copies, waits for them, and re-layouts, on_device(): latent[:, rows_out, :].reshape(members_here, owners, capacity, width)  6.07 us
  transfers between devices with their start and end apart: 2, of which 2 were waited for; matrix products, arithmetic and copies ran while one was open for 3% of the time, Pallas kernels for 0%

commit v1 on v0

v1 whole, which is shorter than its diff:
```python
import functools

import jax
import jax.numpy as jnp
from jax import lax
from jax.experimental import pallas as pl
from jax.experimental.pallas import tpu as pltpu
from jax.sharding import PartitionSpec as P

H = 16
LANES = 128
F32 = jnp.float32
BF16 = jnp.bfloat16
NN = (((1,), (0,)), ((), ()))
NT = (((1,), (1,)), ((), ()))
TN = (((0,), (0,)), ((), ()))
VMEM = pl.BlockSpec(memory_space=pltpu.VMEM)


def dot(a, b, dims=NN):
    return lax.dot_general(a, b, dims, preferred_element_type=F32)


def call(kernel, out_shape, operands, scratch=(), flops=0, limit=40):
    single = not isinstance(out_shape, (list, tuple))
    bytes_accessed = sum(x.size * x.dtype.itemsize for x in operands)
    return pl.pallas_call(
        kernel,
        out_shape=out_shape,
        in_specs=[VMEM] * len(operands),
        out_specs=VMEM if single else [VMEM] * len(out_shape),
        scratch_shapes=list(scratch),
        compiler_params=pltpu.CompilerParams(vmem_limit_bytes=limit * 1024 * 1024),
        cost_estimate=pl.CostEstimate(
            flops=flops, bytes_accessed=bytes_accessed, transcendentals=0
        ),
    )(*operands)


def of_member(block, member, members, chunks, capacity):
    step = members * capacity
    first = member * capacity
    return jnp.concatenate(
        [block[c * step + first : c * step + first + capacity] for c in range(chunks)], axis=0
    )


def by_chunk(blocks, chunks, capacity):
    return jnp.concatenate(
        [b[c * capacity : (c + 1) * capacity] for c in range(chunks) for b in blocks], axis=0
    )


def gather_kernel(members, chunks, capacity, latent_ref, rows_ref, *out_refs):
    own_rows = latent_ref.shape[1]
    total = chunks * capacity
    ids = lax.broadcasted_iota(jnp.int32, (total, own_rows), 1)
    pick = (rows_ref[...] == ids).astype(F32).astype(BF16)
    picked = [dot(pick, latent_ref[m]) for m in range(members)]
    step = members * capacity
    rows = by_chunk(picked, chunks, capacity).astype(BF16)
    for c in range(chunks):
        out_refs[c][...] = rows[c * step : (c + 1) * step]


def query_kernel(head_size, feat_ref, w_ref, out_ref):
    points, width = feat_ref.shape
    per = LANES // head_size
    query = dot(feat_ref[...], w_ref[...]).astype(BF16)
    head = lax.broadcasted_iota(jnp.int32, (points, width), 1) // head_size % per
    for p in range(per):
        out_ref[p * points : (p + 1) * points, :] = jnp.where(
            head == p, query, jnp.zeros_like(query)
        )


def forward_kernel(
    members, chunks, capacity, head_size, qm_ref, wk_ref, wv_ref, wout_ref, mult_ref, *refs
):
    chunk_refs = refs[:chunks]
    pred_ref, weight_ref, v_ref, rows_scr, k_scr = refs[chunks:]
    width = wk_ref.shape[0]
    points = mult_ref.shape[1]
    per = LANES // head_size
    groups = width // LANES
    scale = head_size ** (-0.5)
    step = members * capacity
    for c in range(chunks):
        rows_scr[c * step : (c + 1) * step, :] = chunk_refs[c][...]
    tile = 2 * LANES

    @pl.loop(0, width // tile)
    def project(t):
        cols = pl.ds(pl.multiple_of(t * tile, tile), tile)
        keys = dot(rows_scr[...], wk_ref[:, cols])
        values = dot(rows_scr[...], wv_ref[:, cols])
        for m in range(members):
            k_scr[m, :, cols] = of_member(keys, m, members, chunks, capacity).astype(BF16)
            v_ref[m, :, cols] = of_member(values, m, members, chunks, capacity).astype(BF16)

    mult = jnp.concatenate([mult_ref[...]] * per, axis=1)
    named = mult > 0.0
    head = lax.broadcasted_iota(jnp.int32, (points, LANES), 1) // head_size
    for m in range(members):
        pred = jnp.zeros(pred_ref.shape[1:], F32)
        for j in range(groups):
            cols = slice(j * LANES, (j + 1) * LANES)
            scores = dot(k_scr[m, :, cols], qm_ref[:, cols], NT) * scale
            raised = jnp.where(named, jnp.exp(scores), 0.0)
            denom = jnp.sum(mult * raised, axis=0, keepdims=True)
            probs = (raised * (1.0 / denom)).astype(BF16)
            weights = (mult * probs.astype(F32)).astype(BF16)
            weight_ref[m, j] = weights
            both = dot(weights, v_ref[m, :, cols], TN)
            attended = both[:points]
            for p in range(1, per):
                attended = jnp.where(head == p, both[p * points : (p + 1) * points], attended)
            pred = pred + dot(wout_ref[:, cols], attended.astype(BF16), NT)
        pred_ref[m] = pred


def backward_kernel(
    members,
    chunks,
    capacity,
    head_size,
    qm_ref,
    wk_ref,
    wv_ref,
    wout_ref,
    every_ref,
    mine_ref,
    truth_ref,
    area_ref,
    var_ref,
    weight_ref,
    v_ref,
    *refs,
):
    out_refs = refs[:chunks]
    da_scr, dk_scr, dv_scr = refs[chunks:]
    width = wk_ref.shape[0]
    points = truth_ref.shape[1]
    total = every_ref.shape[0]
    per = LANES // head_size
    groups = width // LANES
    scale = head_size ** (-0.5)
    step = members * capacity
    factor = area_ref[...] * var_ref[...]
    head = lax.broadcasted_iota(jnp.int32, (points, width), 1) // head_size % per
    for m in range(members):
        mine = mine_ref[m]
        miss = mine - truth_ref[...]
        first = miss / jnp.sqrt(1.0 + miss * miss) / total
        second = jnp.zeros_like(mine)
        for f in range(total):
            paired = mine - every_ref[f]
            second = second + paired / jnp.sqrt(1.0 + paired * paired)
        dpred = (factor * (first - second / (total * (total - 1)))).astype(BF16)
        d_attended = dot(dpred, wout_ref[...], TN).astype(BF16)
        for p in range(per):
            da_scr[m, p * points : (p + 1) * points, :] = jnp.where(
                head == p, d_attended, jnp.zeros_like(d_attended)
            )
    for j in range(groups):
        cols = slice(j * LANES, (j + 1) * LANES)
        d_keys, d_values = [], []
        for m in range(members):
            d_probs = dot(v_ref[m, :, cols], da_scr[m, :, cols], NT)
            weights = weight_ref[m, j].astype(F32)
            inner = jnp.sum(weights * d_probs, axis=0, keepdims=True)
            d_scores = (weights * (d_probs - inner) * scale).astype(BF16)
            d_keys.append(dot(d_scores, qm_ref[:, cols]))
            d_values.append(dot(weight_ref[m, j], da_scr[m, :, cols]))
        dk_scr[:, cols] = by_chunk(d_keys, chunks, capacity).astype(BF16)
        dv_scr[:, cols] = by_chunk(d_values, chunks, capacity).astype(BF16)
    tile = 2 * LANES

    @pl.loop(0, width // tile)
    def project(t):
        cols = pl.ds(pl.multiple_of(t * tile, tile), tile)
        rows = dot(dk_scr[...], wk_ref[cols, :], NT) + dot(dv_scr[...], wv_ref[cols, :], NT)
        rows = rows.astype(BF16)
        for c in range(chunks):
            out_refs[c][:, cols] = rows[c * step : (c + 1) * step]


def scatter_kernel(members, chunks, capacity, rows_ref, *refs):
    chunk_refs = refs[:chunks]
    out_ref = refs[chunks]
    own_rows = out_ref.shape[1]
    total = chunks * capacity
    ids = lax.broadcasted_iota(jnp.int32, (own_rows, total), 0)
    place = (rows_ref[...] == ids).astype(F32).astype(BF16)
    back = jnp.concatenate([r[...] for r in chunk_refs], axis=0).astype(F32)
    for m in range(members):
        mine = of_member(back, m, members, chunks, capacity).astype(BF16)
        out_ref[m] = dot(place, mine)


def on_device(
    chunks,
    latent,
    grid_feat,
    w_query,
    w_key,
    w_value,
    w_out,
    truth,
    area,
    var_weight,
    send_rows,
    neighbours,
    live_count,
):
    members, own_rows, width = latent.shape
    points, slots = neighbours.shape
    variables = w_out.shape[0]
    capacity = send_rows.shape[2]
    head_size = width // H
    per = LANES // head_size
    groups = width // LANES
    step = members * capacity
    received = chunks * capacity
    me = lax.axis_index("grid")
    shifts = jnp.arange(chunks, dtype=jnp.int32)
    targets = lax.rem(me + shifts, chunks)
    sources = lax.rem(me + chunks - shifts, chunks)

    def sent(blocks, sign):
        pairs = lambda s: [(i, (i + sign * s) % chunks) for i in range(chunks)]
        return [blocks[0]] + [
            lax.ppermute(blocks[s], "grid", pairs(s)) for s in range(1, chunks)
        ]

    rows_out = send_rows[0][targets].reshape(-1)
    chunk_shape = jax.ShapeDtypeStruct((step, width), BF16)
    outgoing = call(
        functools.partial(gather_kernel, members, chunks, capacity),
        [chunk_shape] * chunks,
        [latent, rows_out[:, None]],
        flops=2 * members * received * own_rows * width,
    )
    arrived = sent(outgoing, 1)
    query = call(
        functools.partial(query_kernel, head_size),
        jax.ShapeDtypeStruct((per * points, width), BF16),
        [grid_feat, w_query],
        flops=2 * points * width * width,
    )
    row_ids = (sources[:, None] * capacity + jnp.arange(capacity, dtype=jnp.int32)).reshape(-1)
    live = jnp.arange(slots)[:, None] < live_count[None, :]
    names = jnp.where(live, neighbours.T, -1)
    mult = jnp.sum((row_ids[None, :, None] == names[:, None, :]).astype(F32), axis=0)

    predicted, weights, values = call(
        functools.partial(forward_kernel, members, chunks, capacity, head_size),
        [
            jax.ShapeDtypeStruct((members, variables, points), F32),
            jax.ShapeDtypeStruct((members, groups, received, per * points), BF16),
            jax.ShapeDtypeStruct((members, received, width), BF16),
        ],
        [query, w_key, w_value, w_out, mult, *arrived],
        scratch=[
            pltpu.VMEM((chunks * step, width), BF16),
            pltpu.VMEM((members, received, width), BF16),
        ],
        flops=4 * members * received * width * width,
    )
    everyone = lax.all_gather(predicted, "member", axis=0, tiled=True)
    leaving = call(
        functools.partial(backward_kernel, members, chunks, capacity, head_size),
        [chunk_shape] * chunks,
        [
            query,
            w_key,
            w_value,
            w_out,
            everyone,
            predicted,
            truth,
            area[None, :],
            var_weight[:, None],
            weights,
            values,
        ],
        scratch=[
            pltpu.VMEM((members, per * points, width), BF16),
            pltpu.VMEM((chunks * step, width), BF16),
            pltpu.VMEM((chunks * step, width), BF16),
        ],
        flops=4 * members * received * width * width,
    )
    returned = sent(leaving, -1)
    return call(
        functools.partial(scatter_kernel, members, chunks, capacity),
        jax.ShapeDtypeStruct((members, own_rows, width), F32),
        [rows_out[None, :], *returned],
        flops=2 * members * received * own_rows * width,
    )


def solution(mesh):
    return jax.shard_map(
        functools.partial(on_device, mesh.shape["grid"]),
        mesh=mesh,
        in_specs=(
            P("member", "grid", None),
            P("grid", None),
            P(),
            P(),
            P(),
            P(),
            P(None, "grid"),
            P("grid"),
            P(),
            P("grid", None, None),
            P("grid", None),
            P("grid"),
        ),
        out_specs=P("member", "grid", None),
        check_vma=False,
    )
```

time: 160 us -> 73 us (0.46)
  matrix products: 39.5 us -> 0 us
  waiting for transfers between devices: 53.9 us -> 18.2 us
  local copies, waits for them, and re-layouts: 33.3 us -> 6.07 us
  Pallas kernels: 0 us -> 16.3 us
  starting transfers between devices: 11.7 us -> 25.2 us
  other arithmetic: 13.3 us -> 0.32 us
    all_to_all x2 -> x0, waiting for transfers between devices: 53.9 us -> none  [the longest x1 37.7 us: on_device(): lax.all_to_all(row_terms.reshape(members_here, owners, capacity, width),...]
    dot_general x19 -> x0, matrix products: 39.5 us -> none  [the longest x2 6.81 us: on_device(): jnp.einsum('ghr,ghd->rhd', key_weights, query_wide, precision=highest)]
    ppermute x0 -> x14, starting transfers between devices: none -> 25.2 us  [sent(): lax.ppermute(blocks[s], 'grid', pairs(s))]
    ppermute x0 -> x14, waiting for transfers between devices: none -> 18.2 us  [sent(): lax.ppermute(blocks[s], 'grid', pairs(s))]
    pallas_call x0 -> x5, Pallas kernels: none -> 16.3 us  [call(): pl.pallas_call(kernel, out_shape=out_shape, in_specs=[VMEM] * len(operand...]
    all_to_all x2 -> x0, starting transfers between devices: 11.7 us -> none  [the longest x1 7.28 us: on_device(): lax.all_to_all(outgoing, 'grid', split_axis=1, concat_axis=1, tiled=True)]
    slice x7 -> x0, local copies, waits for them, and re-layouts: 10.6 us -> none  [the longest x3 4.12 us: on_device(): values_heads = values_in[member].reshape(received, H, head_size)]
    another operation x6 -> x2, local copies, waits for them, and re-layouts: 9.66 us -> 0.17 us  [the longest x1 0.09 us: on_device(): rows_out[:, None]]
  transfers between devices with their start and end apart: 2 -> 14, of which waited for: 2 -> 6; matrix products, arithmetic and copies ran while one was open for 3% -> 1% of each run, Pallas kernels for 0% -> 1%
where the time goes in v1:
time: 73 us; the launch traced here: 72.7 us
  starting transfers between devices  25.2 us (35%)
  waiting for transfers between devices  18.2 us (25%)
  Pallas kernels  16.3 us (22%)
  blocking collectives  6.48 us (9%)
  local copies, waits for them, and re-layouts  6.07 us (8%)
    ppermute x14, starting transfers between devices, sent(): lax.ppermute(blocks[s], 'grid', pairs(s))  25.2 us
    ppermute x14, waiting for transfers between devices, sent(): lax.ppermute(blocks[s], 'grid', pairs(s))  18.2 us
    pallas_call x5, Pallas kernels, call(): pl.pallas_call(kernel, out_shape=out_shape, in_specs=[VMEM] * len(operand...  16.3 us
    all_gather x1, blocking collectives, on_device(): everyone = lax.all_gather(predicted, 'member', axis=0, tiled=True)  6.48 us
    unnamed x24, local copies, waits for them, and re-layouts  5.16 us
  transfers between devices with their start and end apart: 14, of which 6 were waited for; matrix products, arithmetic and copies ran while one was open for 1% of the time, Pallas kernels for 1%

profile of v1, /device:TPU:0, one launch (start us, length us, event | category | flops | bytes accessed | tf_op | source)
XLA Modules:
  0.0 72.7 jit_solution(14168791365503712800)
XLA Ops:
  0.0 0.6 copy-done
  0.7 0.6 gather_fusion
  1.2 0.1 broadcast_in_dim_reshape.9.rows_ref
  1.4 1.3 %copy-done.4 = bf16[2,320,1024]{2,1,0:T(8,128)(2,1)S(1)} copy-done((bf16[2,320,1024]{2,1,0:T(8,128)(2,1)S(1)}, bf16[2,320,1024]{2,1,0:T(8,128)(2,1)}, u32[]{:S(2)}) %copy-start.4) | copy-done | bytes 1310744
  2.7 0.6 shard_map.119
  3.3 3.0 %collective-permute-start = (bf16[48,1024]{1,0:T(8,128)(2,1)S(1)}, bf16[48,1024]{1,0:T(8,128)(2,1)S(1)}, u32[]{:S(2)}, u32[]{:S(2)}) collective-permute-start(bf16[48,1024]{1,0:T(8,128)(2,1)S(1)} %get-tuple-element.25), channel_id=1, source_target_pairs={{0,4},{4,8},{8,12},{12,16},{16,20},{20,24},{24,28},{28,0},{1,5},{5... | collective-permute-start | bytes 294920 | tf_op jit(solution)/shard_map/ppermute | solution.py:233
  6.3 1.6 %collective-permute-start.1 = (bf16[48,1024]{1,0:T(8,128)(2,1)S(1)}, bf16[48,1024]{1,0:T(8,128)(2,1)S(1)}, u32[]{:S(2)}, u32[]{:S(2)}) collective-permute-start(bf16[48,1024]{1,0:T(8,128)(2,1)S(1)} %get-tuple-element.26), channel_id=1, source_target_pairs={{0,8},{4,12},{8,16},{12,20},{16,24},{20,28},{24,0},{28,4},{1,9},{5... | collective-permute-start | bytes 294920 | tf_op jit(solution)/shard_map/ppermute | solution.py:233
  7.9 2.5 %collective-permute-start.2 = (bf16[48,1024]{1,0:T(8,128)(2,1)S(1)}, bf16[48,1024]{1,0:T(8,128)(2,1)S(1)}, u32[]{:S(2)}, u32[]{:S(2)}) collective-permute-start(bf16[48,1024]{1,0:T(8,128)(2,1)S(1)} %get-tuple-element.27), channel_id=1, source_target_pairs={{0,12},{4,16},{8,20},{12,24},{16,28},{20,0},{24,4},{28,8},{1,13},{... | collective-permute-start | bytes 294920 | tf_op jit(solution)/shard_map/ppermute | solution.py:233
  10.4 1.2 %collective-permute-start.3 = (bf16[48,1024]{1,0:T(8,128)(2,1)S(1)}, bf16[48,1024]{1,0:T(8,128)(2,1)S(1)}, u32[]{:S(2)}, u32[]{:S(2)}) collective-permute-start(bf16[48,1024]{1,0:T(8,128)(2,1)S(1)} %get-tuple-element.28), channel_id=1, source_target_pairs={{0,16},{4,20},{8,24},{12,28},{16,0},{20,4},{24,8},{28,12},{1,17},{... | collective-permute-start | bytes 294920 | tf_op jit(solution)/shard_map/ppermute | solution.py:233
  11.6 2.6 %collective-permute-start.4 = (bf16[48,1024]{1,0:T(8,128)(2,1)S(1)}, bf16[48,1024]{1,0:T(8,128)(2,1)S(1)}, u32[]{:S(2)}, u32[]{:S(2)}) collective-permute-start(bf16[48,1024]{1,0:T(8,128)(2,1)S(1)} %get-tuple-element.29), channel_id=1, source_target_pairs={{0,20},{4,24},{8,28},{12,0},{16,4},{20,8},{24,12},{28,16},{1,21},{... | collective-permute-start | bytes 294920 | tf_op jit(solution)/shard_map/ppermute | solution.py:233
  14.5 0.1 copy.19.var_ref
  14.6 1.6 %copy-done.1 = bf16[1024,1024]{1,0:T(8,128)(2,1)S(1)} copy-done((bf16[1024,1024]{1,0:T(8,128)(2,1)S(1)}, bf16[1024,1024]{1,0:T(8,128)(2,1)}, u32[]{:S(2)}) %copy-start.1) | copy-done | bytes 2097176
  16.2 0.5 shard_map.118.qm_ref
  16.7 1.4 %collective-permute-start.5 = (bf16[48,1024]{1,0:T(8,128)(2,1)S(1)}, bf16[48,1024]{1,0:T(8,128)(2,1)S(1)}, u32[]{:S(2)}, u32[]{:S(2)}) collective-permute-start(bf16[48,1024]{1,0:T(8,128)(2,1)S(1)} %get-tuple-element.30), channel_id=1, source_target_pairs={{0,24},{4,28},{8,0},{12,4},{16,8},{20,12},{24,16},{28,20},{1,25},{... | collective-permute-start | bytes 294920 | tf_op jit(solution)/shard_map/ppermute | solution.py:233
  18.1 1.4 %collective-permute-start.6 = (bf16[48,1024]{1,0:T(8,128)(2,1)S(1)}, bf16[48,1024]{1,0:T(8,128)(2,1)S(1)}, u32[]{:S(2)}, u32[]{:S(2)}) collective-permute-start(bf16[48,1024]{1,0:T(8,128)(2,1)S(1)} %get-tuple-element.31), channel_id=1, source_target_pairs={{0,28},{4,0},{8,4},{12,8},{16,12},{20,16},{24,20},{28,24},{1,29},{... | collective-permute-start | bytes 294920 | tf_op jit(solution)/shard_map/ppermute | solution.py:233
  19.5 0.2 convert_reduce_fusion.mult_ref
  19.7 1.1 %collective-permute-done.2.refs_3_ = bf16[48,1024]{1,0:T(8,128)(2,1)S(1)} collective-permute-done((bf16[48,1024]{1,0:T(8,128)(2,1)S(1)}, bf16[48,1024]{1,0:T(8,128)(2,1)S(1)}, u32[]{:S(2)}, u32[]{:S(2)}) %collective-permute-start.2) | collective-permute-done | bytes 98336 | tf_op jit(solution)/shard_map/ppermute | solution.py:233
  20.8 0.6 collective-permute-done.3.refs_4_
  21.3 3.6 %collective-permute-done.5.refs_6_ = bf16[48,1024]{1,0:T(8,128)(2,1)S(1)} collective-permute-done((bf16[48,1024]{1,0:T(8,128)(2,1)S(1)}, bf16[48,1024]{1,0:T(8,128)(2,1)S(1)}, u32[]{:S(2)}, u32[]{:S(2)}) %collective-permute-start.5) | collective-permute-done | bytes 98336 | tf_op jit(solution)/shard_map/ppermute | solution.py:233
  25.0 1.6 %copy-done.3 = bf16[1024,1024]{1,0:T(8,128)(2,1)S(1)} copy-done((bf16[1024,1024]{1,0:T(8,128)(2,1)S(1)}, bf16[1024,1024]{1,0:T(8,128)(2,1)}, u32[]{:S(2)}) %copy-start.3) | copy-done | bytes 2097176
  26.6 6.3 %shard_map.120 = (f32[2,96,128]{2,1,0:T(8,128)S(1)}, bf16[2,8,192,256]{3,2,1,0:T(8,128)(2,1)S(1)}, bf16[2,192,1024]{2,1,0:T(8,128)(2,1)S(1)}) custom-call(bf16[256,1024]{1,0:T(8,128)(2,1)S(1)} %shard_map.118.qm_ref, bf16[1024,1024]{1,0:T(8,128)(2,1)S(1)} %copy-done.2, bf16[1024,1024]{1,0:T(8,128)(2,1)S(1)} %copy-done.3, bf16[96,1024]{1,0:T(8,128)(2,1)S(1)} %copy-done.6, ...), custom_call_target="tpu_custom_call" | custom-call | flops 1610612736 | bytes 5799936 | tf_op jit(solution)/shard_map/pallas_call | solution.py:27
  32.9 6.5 %all_gather.3.every_ref = f32[8,96,128]{2,1,0:T(8,128)S(1)} all-gather(f32[2,96,128]{2,1,0:T(8,128)S(1)} %get-tuple-element.32.mine_ref), channel_id=1, replica_groups=mesh['grid'=8,'member'=4] {'member'}, dimensions={0}, use_global_device_ids=true | all-gather | bytes 491520 | tf_op jit(solution)/shard_map/all_gather | solution.py:270
  39.4 6.9 %shard_map.121 = (bf16[48,1024]{1,0:T(8,128)(2,1)S(1)}, bf16[48,1024]{1,0:T(8,128)(2,1)S(1)}, bf16[48,1024]{1,0:T(8,128)(2,1)S(1)}, bf16[48,1024]{1,0:T(8,128)(2...) custom-call(bf16[256,1024]{1,0:T(8,128)(2,1)S(1)} %shard_map.118.qm_, ...), custom_call_target="tpu_custom_call" | custom-call | flops 1610612736 | bytes 7816064 | tf_op jit(solution)/shard_map/pallas_call | solution.py:27
  46.3 4.8 %collective-permute-start.7 = (bf16[48,1024]{1,0:T(8,128)(2,1)S(1)}, bf16[48,1024]{1,0:T(8,128)(2,1)S(1)}, u32[]{:S(2)}, u32[]{:S(2)}) collective-permute-start(bf16[48,1024]{1,0:T(8,128)(2,1)S(1)} %get-tuple-element.36), channel_id=1, source_target_pairs={{0,28},{4,0},{8,4},{12,8},{16,12},{20,16},{24,20},{28,24},{1,29},{... | collective-permute-start | bytes 294920 | tf_op jit(solution)/shard_map/ppermute | solution.py:233
  51.1 1.6 %collective-permute-start.8 = (bf16[48,1024]{1,0:T(8,128)(2,1)S(1)}, bf16[48,1024]{1,0:T(8,128)(2,1)S(1)}, u32[]{:S(2)}, u32[]{:S(2)}) collective-permute-start(bf16[48,1024]{1,0:T(8,128)(2,1)S(1)} %get-tuple-element.37), channel_id=1, source_target_pairs={{0,24},{4,28},{8,0},{12,4},{16,8},{20,12},{24,16},{28,20},{1,25},{... | collective-permute-start | bytes 294920 | tf_op jit(solution)/shard_map/ppermute | solution.py:233
  52.7 1.4 %collective-permute-start.10 = (bf16[48,1024]{1,0:T(8,128)(2,1)S(1)}, bf16[48,1024]{1,0:T(8,128)(2,1)S(1)}, u32[]{:S(2)}, u32[]{:S(2)}) collective-permute-start(bf16[48,1024]{1,0:T(8,128)(2,1)S(1)} %get-tuple-element.39), channel_id=1, source_target_pairs={{0,16},{4,20},{8,24},{12,28},{16,0},{20,4},{24,8},{28,12},{1,17},{... | collective-permute-start | bytes 294920 | tf_op jit(solution)/shard_map/ppermute | solution.py:233
  54.1 1.5 %collective-permute-start.11 = (bf16[48,1024]{1,0:T(8,128)(2,1)S(1)}, bf16[48,1024]{1,0:T(8,128)(2,1)S(1)}, u32[]{:S(2)}, u32[]{:S(2)}) collective-permute-start(bf16[48,1024]{1,0:T(8,128)(2,1)S(1)} %get-tuple-element.40), channel_id=1, source_target_pairs={{0,12},{4,16},{8,20},{12,24},{16,28},{20,0},{24,4},{28,8},{1,13},{... | collective-permute-start | bytes 294920 | tf_op jit(solution)/shard_map/ppermute | solution.py:233
  55.6 2.1 %collective-permute-start.12 = (bf16[48,1024]{1,0:T(8,128)(2,1)S(1)}, bf16[48,1024]{1,0:T(8,128)(2,1)S(1)}, u32[]{:S(2)}, u32[]{:S(2)}) collective-permute-start(bf16[48,1024]{1,0:T(8,128)(2,1)S(1)} %get-tuple-element.41), channel_id=1, source_target_pairs={{0,8},{4,12},{8,16},{12,20},{16,24},{20,28},{24,0},{28,4},{1,9},{5... | collective-permute-start | bytes 294920 | tf_op jit(solution)/shard_map/ppermute | solution.py:233
  57.8 0.9 %collective-permute-done.9.refs_3_ = bf16[48,1024]{1,0:T(8,128)(2,1)S(1)} collective-permute-done((bf16[48,1024]{1,0:T(8,128)(2,1)S(1)}, bf16[48,1024]{1,0:T(8,128)(2,1)S(1)}, u32[]{:S(2)}, u32[]{:S(2)}) %collective-permute-start.9) | collective-permute-done | bytes 98336 | tf_op jit(solution)/shard_map/ppermute | solution.py:233
  58.7 10.9 %collective-permute-done.10.refs_4_ = bf16[48,1024]{1,0:T(8,128)(2,1)S(1)} collective-permute-done((bf16[48,1024]{1,0:T(8,128)(2,1)S(1)}, bf16[48,1024]{1,0:T(8,128)(2,1)S(1)}, u32[]{:S(2)}, u32[]{:S(2)}) %collective-permute-start.10) | collective-permute-done | bytes 98336 | tf_op jit(solution)/shard_map/ppermute | solution.py:233
  69.6 1.1 %collective-permute-done.11.refs_5_ = bf16[48,1024]{1,0:T(8,128)(2,1)S(1)} collective-permute-done((bf16[48,1024]{1,0:T(8,128)(2,1)S(1)}, bf16[48,1024]{1,0:T(8,128)(2,1)S(1)}, u32[]{:S(2)}, u32[]{:S(2)}) %collective-permute-start.11) | collective-permute-done | bytes 98336 | tf_op jit(solution)/shard_map/ppermute | solution.py:233
  70.7 2.0 %shard_map.122 = f32[2,320,1024]{2,1,0:T(8,128)} custom-call(s32[1,192]{1,0:T(1,128)S(1)} %broadcast_in_dim_reshape.7.rows_ref, bf16[48,1024]{1,0:T(8,128)(2,1)S(1)} %get-tuple-element.35.refs_0_, bf16[48,1024]{1,0:T(8,128)(2,1)S(1)} %collective-permute-done.7.refs_1_, bf16[48,1024]{1,0:T(8,128)(2,1)S(1)} %collective-permute-done.8.refs_2_, ...), custom_call_target="tpu_custom_call" | custom-call | flops 251658240 | bytes 787200 | tf_op jit(solution)/shard_map/pallas_call | solution.py:27
  (37 shorter events, 0.3 us)
Async XLA Ops:
  0.0 0.7 copy-start
  0.0 14.3 %copy-start.11 = (s32[128]{0:T(128)S(1)}, s32[128]{0:T(128)}, u32[]{:S(2)}) copy-start(s32[128]{0:T(128)} %param.23) | copy-start | bytes 1540
  0.0 14.3 %copy-start.9 = (s32[128,16]{0,1:T(8,128)S(1)}, s32[128,16]{0,1:T(8,128)}, u32[]{:S(2)}) copy-start(s32[128,16]{0,1:T(8,128)} %param.22) | copy-start | bytes 24580
  0.0 14.5 %copy-start.10 = (f32[96]{0:T(128)S(1)}, f32[96]{0:T(128)}, u32[]{:S(2)}) copy-start(f32[96]{0:T(128)} %param.20) | copy-start | bytes 1156
  1.3 1.3 %copy-start.4 = (bf16[2,320,1024]{2,1,0:T(8,128)(2,1)S(1)}, bf16[2,320,1024]{2,1,0:T(8,128)(2,1)}, u32[]{:S(2)}) copy-start(bf16[2,320,1024]{2,1,0:T(8,128)(2,1)} %latent_ref.1) | copy-start | bytes 3932164
  2.7 11.9 %copy-start.5 = (bf16[128,1024]{1,0:T(8,128)(2,1)S(1)}, bf16[128,1024]{1,0:T(8,128)(2,1)}, u32[]{:S(2)}) copy-start(bf16[128,1024]{1,0:T(8,128)(2,1)} %feat_ref.1) | copy-start | bytes 786436
  2.7 22.3 %copy-start.6 = (bf16[96,1024]{1,0:T(8,128)(2,1)S(1)}, bf16[96,1024]{1,0:T(8,128)(2,1)}, u32[]{:S(2)}) copy-start(bf16[96,1024]{1,0:T(8,128)(2,1)} %wout_ref.3) | copy-start | bytes 589828
  3.3 13.4 %collective-permute-start = (bf16[48,1024]{1,0:T(8,128)(2,1)S(1)}, bf16[48,1024]{1,0:T(8,128)(2,1)S(1)}, u32[]{:S(2)}, u32[]{:S(2)}) collective-permute-start(bf16[48,1024]{1,0:T(8,128)(2,1)S(1)} %get-tuple-element.25), channel_id=1, source_target_pairs={{0,4},{4,8},{8,12},{12,16},{16,20},{20,24},{24,28},{28,0},{1,5},{5... | collective-permute-start | bytes 294920 | tf_op jit(solution)/shard_map/ppermute | solution.py:233
  6.3 11.8 %collective-permute-start.1 = (bf16[48,1024]{1,0:T(8,128)(2,1)S(1)}, bf16[48,1024]{1,0:T(8,128)(2,1)S(1)}, u32[]{:S(2)}, u32[]{:S(2)}) collective-permute-start(bf16[48,1024]{1,0:T(8,128)(2,1)S(1)} %get-tuple-element.26), channel_id=1, source_target_pairs={{0,8},{4,12},{8,16},{12,20},{16,24},{20,28},{24,0},{28,4},{1,9},{5... | collective-permute-start | bytes 294920 | tf_op jit(solution)/shard_map/ppermute | solution.py:233
  7.9 12.9 %collective-permute-start.2 = (bf16[48,1024]{1,0:T(8,128)(2,1)S(1)}, bf16[48,1024]{1,0:T(8,128)(2,1)S(1)}, u32[]{:S(2)}, u32[]{:S(2)}) collective-permute-start(bf16[48,1024]{1,0:T(8,128)(2,1)S(1)} %get-tuple-element.27), channel_id=1, source_target_pairs={{0,12},{4,16},{8,20},{12,24},{16,28},{20,0},{24,4},{28,8},{1,13},{... | collective-permute-start | bytes 294920 | tf_op jit(solution)/shard_map/ppermute | solution.py:233
  10.4 10.9 %collective-permute-start.3 = (bf16[48,1024]{1,0:T(8,128)(2,1)S(1)}, bf16[48,1024]{1,0:T(8,128)(2,1)S(1)}, u32[]{:S(2)}, u32[]{:S(2)}) collective-permute-start(bf16[48,1024]{1,0:T(8,128)(2,1)S(1)} %get-tuple-element.28), channel_id=1, source_target_pairs={{0,16},{4,20},{8,24},{12,28},{16,0},{20,4},{24,8},{28,12},{1,17},{... | collective-permute-start | bytes 294920 | tf_op jit(solution)/shard_map/ppermute | solution.py:233
  11.6 9.7 %collective-permute-start.4 = (bf16[48,1024]{1,0:T(8,128)(2,1)S(1)}, bf16[48,1024]{1,0:T(8,128)(2,1)S(1)}, u32[]{:S(2)}, u32[]{:S(2)}) collective-permute-start(bf16[48,1024]{1,0:T(8,128)(2,1)S(1)} %get-tuple-element.29), channel_id=1, source_target_pairs={{0,20},{4,24},{8,28},{12,0},{16,4},{20,8},{24,12},{28,16},{1,21},{... | collective-permute-start | bytes 294920 | tf_op jit(solution)/shard_map/ppermute | solution.py:233
  14.6 1.6 %copy-start.1 = (bf16[1024,1024]{1,0:T(8,128)(2,1)S(1)}, bf16[1024,1024]{1,0:T(8,128)(2,1)}, u32[]{:S(2)}) copy-start(bf16[1024,1024]{1,0:T(8,128)(2,1)} %w_ref.1) | copy-start | bytes 6291460
  16.2 8.8 %copy-start.2 = (bf16[1024,1024]{1,0:T(8,128)(2,1)S(1)}, bf16[1024,1024]{1,0:T(8,128)(2,1)}, u32[]{:S(2)}) copy-start(bf16[1024,1024]{1,0:T(8,128)(2,1)} %wk_ref.3) | copy-start | bytes 6291460
  16.7 8.3 %collective-permute-start.5 = (bf16[48,1024]{1,0:T(8,128)(2,1)S(1)}, bf16[48,1024]{1,0:T(8,128)(2,1)S(1)}, u32[]{:S(2)}, u32[]{:S(2)}) collective-permute-start(bf16[48,1024]{1,0:T(8,128)(2,1)S(1)} %get-tuple-element.30), channel_id=1, source_target_pairs={{0,24},{4,28},{8,0},{12,4},{16,8},{20,12},{24,16},{28,20},{1,25},{... | collective-permute-start | bytes 294920 | tf_op jit(solution)/shard_map/ppermute | solution.py:233
  18.1 6.9 %collective-permute-start.6 = (bf16[48,1024]{1,0:T(8,128)(2,1)S(1)}, bf16[48,1024]{1,0:T(8,128)(2,1)S(1)}, u32[]{:S(2)}, u32[]{:S(2)}) collective-permute-start(bf16[48,1024]{1,0:T(8,128)(2,1)S(1)} %get-tuple-element.31), channel_id=1, source_target_pairs={{0,28},{4,0},{8,4},{12,8},{16,12},{20,16},{24,20},{28,24},{1,29},{... | collective-permute-start | bytes 294920 | tf_op jit(solution)/shard_map/ppermute | solution.py:233
  25.0 1.6 %copy-start.3 = (bf16[1024,1024]{1,0:T(8,128)(2,1)S(1)}, bf16[1024,1024]{1,0:T(8,128)(2,1)}, u32[]{:S(2)}) copy-start(bf16[1024,1024]{1,0:T(8,128)(2,1)} %wv_ref.3) | copy-start | bytes 6291460
  26.6 12.8 %copy-start.7 = (f32[96,128]{1,0:T(8,128)S(1)}, f32[96,128]{1,0:T(8,128)}, u32[]{:S(2)}) copy-start(f32[96,128]{1,0:T(8,128)} %truth_ref.1) | copy-start | bytes 147460
  26.6 12.8 %copy-start.8 = (f32[128]{0:T(128)S(1)}, f32[128]{0:T(128)}, u32[]{:S(2)}) copy-start(f32[128]{0:T(128)} %param.19) | copy-start | bytes 1540
  46.3 9.3 %collective-permute-start.7 = (bf16[48,1024]{1,0:T(8,128)(2,1)S(1)}, bf16[48,1024]{1,0:T(8,128)(2,1)S(1)}, u32[]{:S(2)}, u32[]{:S(2)}) collective-permute-start(bf16[48,1024]{1,0:T(8,128)(2,1)S(1)} %get-tuple-element.36), channel_id=1, source_target_pairs={{0,28},{4,0},{8,4},{12,8},{16,12},{20,16},{24,20},{28,24},{1,29},{... | collective-permute-start | bytes 294920 | tf_op jit(solution)/shard_map/ppermute | solution.py:233
  51.1 6.6 %collective-permute-start.8 = (bf16[48,1024]{1,0:T(8,128)(2,1)S(1)}, bf16[48,1024]{1,0:T(8,128)(2,1)S(1)}, u32[]{:S(2)}, u32[]{:S(2)}) collective-permute-start(bf16[48,1024]{1,0:T(8,128)(2,1)S(1)} %get-tuple-element.37), channel_id=1, source_target_pairs={{0,24},{4,28},{8,0},{12,4},{16,8},{20,12},{24,16},{28,20},{1,25},{... | collective-permute-start | bytes 294920 | tf_op jit(solution)/shard_map/ppermute | solution.py:233
  52.7 6.0 %collective-permute-start.9 = (bf16[48,1024]{1,0:T(8,128)(2,1)S(1)}, bf16[48,1024]{1,0:T(8,128)(2,1)S(1)}, u32[]{:S(2)}, u32[]{:S(2)}) collective-permute-start(bf16[48,1024]{1,0:T(8,128)(2,1)S(1)} %get-tuple-element.38), channel_id=1, source_target_pairs={{0,20},{4,24},{8,28},{12,0},{16,4},{20,8},{24,12},{28,16},{1,21},{... | collective-permute-start | bytes 294920 | tf_op jit(solution)/shard_map/ppermute | solution.py:233
  52.7 16.9 %collective-permute-start.10 = (bf16[48,1024]{1,0:T(8,128)(2,1)S(1)}, bf16[48,1024]{1,0:T(8,128)(2,1)S(1)}, u32[]{:S(2)}, u32[]{:S(2)}) collective-permute-start(bf16[48,1024]{1,0:T(8,128)(2,1)S(1)} %get-tuple-element.39), channel_id=1, source_target_pairs={{0,16},{4,20},{8,24},{12,28},{16,0},{20,4},{24,8},{28,12},{1,17},{... | collective-permute-start | bytes 294920 | tf_op jit(solution)/shard_map/ppermute | solution.py:233
  54.1 16.6 %collective-permute-start.11 = (bf16[48,1024]{1,0:T(8,128)(2,1)S(1)}, bf16[48,1024]{1,0:T(8,128)(2,1)S(1)}, u32[]{:S(2)}, u32[]{:S(2)}) collective-permute-start(bf16[48,1024]{1,0:T(8,128)(2,1)S(1)} %get-tuple-element.40), channel_id=1, source_target_pairs={{0,12},{4,16},{8,20},{12,24},{16,28},{20,0},{24,4},{28,8},{1,13},{... | collective-permute-start | bytes 294920 | tf_op jit(solution)/shard_map/ppermute | solution.py:233
  55.6 15.1 %collective-permute-start.12 = (bf16[48,1024]{1,0:T(8,128)(2,1)S(1)}, bf16[48,1024]{1,0:T(8,128)(2,1)S(1)}, u32[]{:S(2)}, u32[]{:S(2)}) collective-permute-start(bf16[48,1024]{1,0:T(8,128)(2,1)S(1)} %get-tuple-element.41), channel_id=1, source_target_pairs={{0,8},{4,12},{8,16},{12,20},{16,24},{20,28},{24,0},{28,4},{1,9},{5... | collective-permute-start | bytes 294920 | tf_op jit(solution)/shard_map/ppermute | solution.py:233
  57.7 13.1 %collective-permute-start.13 = (bf16[48,1024]{1,0:T(8,128)(2,1)S(1)}, bf16[48,1024]{1,0:T(8,128)(2,1)S(1)}, u32[]{:S(2)}, u32[]{:S(2)}) collective-permute-start(bf16[48,1024]{1,0:T(8,128)(2,1)S(1)} %get-tuple-element.42), channel_id=1, source_target_pairs={{0,4},{4,8},{8,12},{12,16},{16,20},{20,24},{24,28},{28,0},{1,5},{5... | collective-permute-start | bytes 294920 | tf_op jit(solution)/shard_map/ppermute | solution.py:233

commit v2 on v1

v2 whole, which is shorter than its diff:
```python
import functools
import math

import jax
import jax.numpy as jnp
from jax import lax
from jax.experimental import pallas as pl
from jax.experimental.pallas import tpu as pltpu
from jax.sharding import PartitionSpec as P

H = 16
LANES = 128
ROOM = 4 * 1024 * 1024
F32 = jnp.float32
BF16 = jnp.bfloat16
NN = (((1,), (0,)), ((), ()))
NT = (((1,), (1,)), ((), ()))
TN = (((0,), (0,)), ((), ()))
VMEM = pl.BlockSpec(memory_space=pltpu.VMEM)
SMEM = pl.BlockSpec(memory_space=pltpu.SMEM)


def dot(a, b, dims=NN):
    return lax.dot_general(a, b, dims, preferred_element_type=F32)


def call(kernel, out_shape, operands, scratch=(), flops=0, scalars=(), limit=None):
    single = not isinstance(out_shape, (list, tuple))
    outs = [out_shape] if single else out_shape
    moved = sum(x.size * x.dtype.itemsize for x in [*operands, *outs])
    held = sum(math.prod(s.shape) * jnp.dtype(s.dtype).itemsize for s in scratch)
    return pl.pallas_call(
        kernel,
        out_shape=out_shape,
        in_specs=[SMEM if i in scalars else VMEM for i in range(len(operands))],
        out_specs=VMEM if single else [VMEM] * len(outs),
        scratch_shapes=list(scratch),
        compiler_params=pltpu.CompilerParams(vmem_limit_bytes=limit or moved + 2 * held + ROOM),
        cost_estimate=pl.CostEstimate(flops=flops, bytes_accessed=moved, transcendentals=0),
    )(*operands)


def of_member(block, member, members, chunks, capacity):
    step = members * capacity
    first = member * capacity
    return jnp.concatenate(
        [block[c * step + first : c * step + first + capacity] for c in range(chunks)], axis=0
    )


def by_chunk(blocks, chunks, capacity):
    return jnp.concatenate(
        [b[c * capacity : (c + 1) * capacity] for c in chunks for b in blocks], axis=0
    )


def named_rows(send_ref, me_ref, order):
    return jnp.concatenate(
        [send_ref[0, pl.ds(me_ref[0] ^ mask, 1), :] for mask in order], axis=1
    )


def one_hot(send_ref, me_ref, order, own_rows):
    rows = named_rows(send_ref, me_ref, order)
    ids = lax.broadcasted_iota(jnp.int32, (own_rows, rows.shape[1]), 0)
    return (rows == ids).astype(F32).astype(BF16)


def gather_kernel(members, order, capacity, latent_ref, send_ref, me_ref, *out_refs):
    chunks = len(order)
    pick = one_hot(send_ref, me_ref, order, latent_ref.shape[1])
    picked = [dot(pick, latent_ref[m], TN) for m in range(members)]
    step = members * capacity
    rows = by_chunk(picked, range(chunks), capacity).astype(BF16)
    for c in range(chunks):
        out_refs[c][...] = rows[c * step : (c + 1) * step]


def query_kernel(head_size, feat_ref, w_ref, out_ref):
    points, width = feat_ref.shape
    per = LANES // head_size
    query = dot(feat_ref[...], w_ref[...]).astype(BF16)
    head = lax.broadcasted_iota(jnp.int32, (points, width), 1) // head_size % per
    for p in range(per):
        out_ref[p * points : (p + 1) * points, :] = jnp.where(
            head == p, query, jnp.zeros_like(query)
        )


def project(rows, wk_ref, wv_ref, k_scr, v_ref, offset, members, chunks, capacity):
    width = wk_ref.shape[0]
    tile = 2 * LANES
    rows_here = pl.ds(offset, chunks * capacity)
    for t in range(width // tile):
        cols = slice(t * tile, (t + 1) * tile)
        keys = dot(rows, wk_ref[:, cols])
        values = dot(rows, wv_ref[:, cols])
        for m in range(members):
            k_scr[m, :, cols] = of_member(keys, m, members, chunks, capacity).astype(BF16)
            v_ref[m, rows_here, cols] = of_member(values, m, members, chunks, capacity).astype(
                BF16
            )


def raised_scores(k_scr, qm_ref, m, j, factor, bias):
    cols = slice(j * LANES, (j + 1) * LANES)
    return jnp.exp2(dot(k_scr[m, :, cols], qm_ref[:, cols], NT) * factor + bias)


def exponent(head_size):
    return head_size ** (-0.5) * math.log2(math.e)


def near_kernel(members, chunks, capacity, head_size, qm_ref, wk_ref, wv_ref, mult_ref, *refs):
    raised_ref, v_ref, k_scr = refs[chunks:]
    groups = wk_ref.shape[0] // LANES
    rows = jnp.concatenate([r[...] for r in refs[:chunks]], axis=0)
    project(rows, wk_ref, wv_ref, k_scr, v_ref, 0, members, chunks, capacity)
    mult = jnp.concatenate([mult_ref[...]] * (LANES // head_size), axis=1)
    bias = jnp.where(mult > 0.0, 0.0, -jnp.inf)
    for m in range(members):
        for j in range(groups):
            raised_ref[m, j] = raised_scores(k_scr, qm_ref, m, j, exponent(head_size), bias)


def forward_kernel(
    members,
    chunks,
    capacity,
    head_size,
    qm_ref,
    wk_ref,
    wv_ref,
    wout_ref,
    mult_ref,
    raised_ref,
    v_near_ref,
    *refs,
):
    pred_ref, weight_ref, v_ref, k_scr, att_scr = refs[chunks:]
    points = mult_ref.shape[1]
    per = LANES // head_size
    groups = wk_ref.shape[0] // LANES
    done = v_near_ref.shape[1]
    rows = jnp.concatenate([r[...] for r in refs[:chunks]], axis=0)
    v_ref[:, :done, :] = v_near_ref[...]
    project(rows, wk_ref, wv_ref, k_scr, v_ref, done, members, chunks, capacity)
    mult = jnp.concatenate([mult_ref[...]] * per, axis=1)
    bias = jnp.where(mult[done:] > 0.0, 0.0, -jnp.inf)
    steps = [(m, j) for m in range(members) for j in range(groups)]
    ahead = raised_scores(k_scr, qm_ref, *steps[0], exponent(head_size), bias)
    for i, (m, j) in enumerate(steps):
        raised = jnp.concatenate([raised_ref[m, j], ahead], axis=0)
        if i + 1 < len(steps):
            ahead = raised_scores(k_scr, qm_ref, *steps[i + 1], exponent(head_size), bias)
        root = lax.rsqrt(jnp.sum(mult * raised, axis=0, keepdims=True))
        weights = (raised * root * root * mult).astype(BF16)
        weight_ref[m, j] = weights
        both = dot(v_ref[m, :, j * LANES : (j + 1) * LANES], weights, TN)
        for p in range(per):
            first = p * head_size
            att_scr[pl.ds(j * LANES + first, head_size), :] = both[
                first : first + head_size, p * points : (p + 1) * points
            ].astype(BF16)
        if j == groups - 1:
            pred_ref[m] = dot(wout_ref[...], att_scr[...])


def return_rows(dk, dv, wk_ref, wv_ref, out_refs):
    width = wk_ref.shape[0]
    tile = 2 * LANES
    step = out_refs[0].shape[0]
    for t in range(width // tile):
        cols = slice(t * tile, (t + 1) * tile)
        rows = dot(dk, wk_ref[cols, :], NT) + dot(dv, wv_ref[cols, :], NT)
        rows = rows.astype(BF16)
        for c, out_ref in enumerate(out_refs):
            out_ref[:, cols] = rows[c * step : (c + 1) * step]


def backward_kernel(
    members,
    early,
    late,
    capacity,
    head_size,
    qm_ref,
    wk_ref,
    wv_ref,
    wout_ref,
    every_ref,
    mine_ref,
    truth_ref,
    area_ref,
    var_ref,
    weight_ref,
    v_ref,
    *refs,
):
    out_refs = refs[: len(early)]
    dk_ref, dv_ref, da_scr, dk_scr, dv_scr = refs[len(early) :]
    width = wk_ref.shape[0]
    points = truth_ref.shape[1]
    total = every_ref.shape[0]
    per = LANES // head_size
    groups = width // LANES
    scale = head_size ** (-0.5)
    factor = area_ref[...] * var_ref[...]
    head = lax.broadcasted_iota(jnp.int32, (points, width), 1) // head_size % per
    for m in range(members):
        mine = mine_ref[m]
        miss = mine - truth_ref[...]
        first = miss * lax.rsqrt(1.0 + miss * miss) / total
        second = jnp.zeros_like(mine)
        for f in range(total):
            paired = mine - every_ref[f]
            second = second + paired * lax.rsqrt(1.0 + paired * paired)
        dpred = (factor * (first - second / (total * (total - 1)))).astype(BF16)
        d_attended = dot(dpred, wout_ref[...], TN).astype(BF16)
        for p in range(per):
            da_scr[m, p * points : (p + 1) * points, :] = jnp.where(
                head == p, d_attended, jnp.zeros_like(d_attended)
            )

    def probs_grad(m, j):
        cols = slice(j * LANES, (j + 1) * LANES)
        return dot(v_ref[m, :, cols], da_scr[m, :, cols], NT)

    steps = [(m, j) for j in range(groups) for m in range(members)]
    ahead = probs_grad(*steps[0])
    d_keys, d_values = [], []
    for i, (m, j) in enumerate(steps):
        cols = slice(j * LANES, (j + 1) * LANES)
        d_probs = ahead
        if i + 1 < len(steps):
            ahead = probs_grad(*steps[i + 1])
        weights = weight_ref[m, j].astype(F32)
        inner = jnp.sum(weights * d_probs, axis=0, keepdims=True)
        d_scores = (weights * scale * (d_probs - inner)).astype(BF16)
        d_keys.append(dot(d_scores, qm_ref[:, cols]))
        d_values.append(dot(weight_ref[m, j], da_scr[m, :, cols]))
        if m == members - 1:
            dk_scr[:, cols] = by_chunk(d_keys, early, capacity).astype(BF16)
            dv_scr[:, cols] = by_chunk(d_values, early, capacity).astype(BF16)
            dk_ref[:, cols] = by_chunk(d_keys, late, capacity).astype(BF16)
            dv_ref[:, cols] = by_chunk(d_values, late, capacity).astype(BF16)
            d_keys, d_values = [], []
    return_rows(dk_scr[...], dv_scr[...], wk_ref, wv_ref, out_refs)


def late_rows_kernel(wk_ref, wv_ref, dk_ref, dv_ref, *out_refs):
    return_rows(dk_ref[...], dv_ref[...], wk_ref, wv_ref, out_refs)


def first_sum_kernel(members, order, capacity, send_ref, me_ref, *refs):
    chunks = len(order)
    out_ref = refs[chunks]
    place = one_hot(send_ref, me_ref, order, out_ref.shape[1])
    back = jnp.concatenate([r[...] for r in refs[:chunks]], axis=0).astype(F32)
    for m in range(members):
        mine = of_member(back, m, members, chunks, capacity).astype(BF16)
        out_ref[m] = dot(place, mine)


def last_sum_kernel(members, order, capacity, send_ref, me_ref, before_ref, *refs):
    chunks = len(order)
    out_ref, sum_scr, sems = refs[chunks:]
    own_rows, width = out_ref.shape[1:]
    parts = sems.shape[1]
    part = width // parts
    place = one_hot(send_ref, me_ref, order, own_rows)
    back = jnp.concatenate([r[...] for r in refs[:chunks]], axis=0).astype(F32)
    mine = [
        of_member(back, m, members, chunks, capacity).astype(BF16) for m in range(members)
    ]
    sends = []
    for m in range(members):
        for p in range(parts):
            cols = slice(p * part, (p + 1) * part)
            sum_scr[m, :, cols] = before_ref[m, :, cols] + dot(place, mine[m][:, cols])
            there = pl.ds(p * part, part)
            send = pltpu.make_async_copy(
                sum_scr.at[m, :, there], out_ref.at[m, :, there], sems.at[m, p]
            )
            send.start()
            sends.append(send)
    for send in sends:
        send.wait()


def last_sum(members, order, capacity, send_rows, me, before, blocks):
    step, width = blocks[0].shape
    own_rows = before.shape[1]
    parts = 4 if width % (4 * LANES) == 0 else 1
    moved = len(order) * step * width * 2 + 2 * members * own_rows * width * 4
    return pl.pallas_call(
        functools.partial(last_sum_kernel, members, order, capacity),
        out_shape=jax.ShapeDtypeStruct((members, own_rows, width), F32),
        in_specs=[VMEM, SMEM] + [VMEM] * (1 + len(order)),
        out_specs=pl.BlockSpec(memory_space=pltpu.HBM),
        scratch_shapes=[
            pltpu.VMEM((members, own_rows, width), F32),
            pltpu.SemaphoreType.DMA((members, parts)),
        ],
        compiler_params=pltpu.CompilerParams(vmem_limit_bytes=2 * moved + 2 * ROOM),
        cost_estimate=pl.CostEstimate(
            flops=2 * len(order) * step * own_rows * width,
            bytes_accessed=moved,
            transcendentals=0,
        ),
    )(send_rows, me, before, *blocks)


def on_device(
    chunks,
    latent,
    grid_feat,
    w_query,
    w_key,
    w_value,
    w_out,
    truth,
    area,
    var_weight,
    send_rows,
    neighbours,
    live_count,
):
    members, own_rows, width = latent.shape
    points, slots = neighbours.shape
    variables = w_out.shape[0]
    capacity = send_rows.shape[2]
    head_size = width // H
    per = LANES // head_size
    groups = width // LANES
    step = members * capacity
    received = chunks * capacity
    me = lax.axis_index("grid")
    half, quarter = chunks // 2, chunks // 4
    order = tuple(range(chunks))
    near, far = order[:half], order[half:]
    early = (0, *far[:quarter], *near[1 : max(quarter, 1)])
    late = tuple(s for s in [*far, *near] if s not in early)
    here = me[None]
    partners = jnp.bitwise_xor(me, jnp.arange(chunks, dtype=jnp.int32))

    def exchanged(blocks, masks):
        return [
            b if s == 0 else lax.ppermute(b, "grid", [(i, i ^ s) for i in range(chunks)])
            for s, b in zip(masks, blocks)
        ]

    chunk_shape = jax.ShapeDtypeStruct((step, width), BF16)
    outgoing = call(
        functools.partial(gather_kernel, members, order, capacity),
        [chunk_shape] * chunks,
        [latent, send_rows, here],
        flops=2 * members * received * own_rows * width,
        scalars=(2,),
        limit=40 * 1024 * 1024,
    )
    arrived_near = exchanged(outgoing[:half], near)
    arrived_far = exchanged(outgoing[half:], far)
    query = call(
        functools.partial(query_kernel, head_size),
        jax.ShapeDtypeStruct((per * points, width), BF16),
        [grid_feat, w_query],
        flops=2 * points * width * width,
    )
    row_ids = (partners[:, None] * capacity + jnp.arange(capacity, dtype=jnp.int32)).reshape(-1)
    live = jnp.arange(slots)[:, None] < live_count[None, :]
    names = jnp.where(live, neighbours.T, -1)
    mult = jnp.sum((row_ids[None, :, None] == names[:, None, :]).astype(F32), axis=0)

    raised, values_near = call(
        functools.partial(near_kernel, members, half, capacity, head_size),
        [
            jax.ShapeDtypeStruct((members, groups, half * capacity, per * points), F32),
            jax.ShapeDtypeStruct((members, half * capacity, width), BF16),
        ],
        [query, w_key, w_value, mult[: half * capacity], *arrived_near],
        scratch=[pltpu.VMEM((members, half * capacity, width), BF16)],
        flops=4 * members * half * capacity * width * width,
    )
    predicted, weights, values = call(
        functools.partial(forward_kernel, members, (chunks - half), capacity, head_size),
        [
            jax.ShapeDtypeStruct((members, variables, points), F32),
            jax.ShapeDtypeStruct((members, groups, received, per * points), BF16),
            jax.ShapeDtypeStruct((members, received, width), BF16),
        ],
        [query, w_key, w_value, w_out, mult, raised, values_near, *arrived_far],
        scratch=[
            pltpu.VMEM((members, (chunks - half) * capacity, width), BF16),
            pltpu.VMEM((width, points), BF16),
        ],
        flops=4 * members * (chunks - half) * capacity * width * width,
    )
    everyone = lax.all_gather(predicted, "member", axis=0, tiled=True)
    late_grad = jax.ShapeDtypeStruct((len(late) * step, width), BF16)
    *leaving_early, d_keys, d_values = call(
        functools.partial(
            backward_kernel, members, early, late, capacity, head_size
        ),
        [chunk_shape] * len(early) + [late_grad] * 2,
        [
            query,
            w_key,
            w_value,
            w_out,
            everyone,
            predicted,
            truth,
            area[None, :],
            var_weight[:, None],
            weights,
            values,
        ],
        scratch=[
            pltpu.VMEM((members, per * points, width), BF16),
            pltpu.VMEM((len(early) * step, width), BF16),
            pltpu.VMEM((len(early) * step, width), BF16),
        ],
        flops=4 * members * received * width * width,
    )
    returned_early = exchanged(leaving_early, early)
    leaving_late = call(
        late_rows_kernel,
        [chunk_shape] * len(late),
        [w_key, w_value, d_keys, d_values],
        flops=4 * len(late) * step * width * width,
    )
    returned_late = exchanged(leaving_late, late)
    before = call(
        functools.partial(first_sum_kernel, members, early, capacity),
        jax.ShapeDtypeStruct((members, own_rows, width), F32),
        [send_rows, here, *returned_early],
        flops=2 * len(early) * step * own_rows * width,
        scalars=(1,),
    )
    return last_sum(members, late, capacity, send_rows, here, before, returned_late)


def solution(mesh):
    return jax.shard_map(
        functools.partial(on_device, mesh.shape["grid"]),
        mesh=mesh,
        in_specs=(
            P("member", "grid", None),
            P("grid", None),
            P(),
            P(),
            P(),
            P(),
            P(None, "grid"),
            P("grid"),
            P(),
            P("grid", None, None),
            P("grid", None),
            P("grid"),
        ),
        out_specs=P("member", "grid", None),
        check_vma=False,
    )
```

time: 73 us -> 66.1 us (0.905)
  waiting for transfers between devices: 18.2 us -> 15.3 us
  Pallas kernels: 16.3 us -> 13.6 us
  starting transfers between devices: 25.2 us -> 23.1 us
    ppermute x14, waiting for transfers between devices: 18.2 us -> 15.3 us  [exchanged(): lax.ppermute(b, 'grid', [(i, i ^ s) for i in range(chunks)])]
    pallas_call x5 -> x8, Pallas kernels: 16.3 us -> 13.6 us  [the longest x7 11.7 us: call(): pl.pallas_call(kernel, out_shape=out_shape, in_specs=[SMEM if i in scalar...]
    ppermute x14, starting transfers between devices: 25.2 us -> 23.1 us  [exchanged(): lax.ppermute(b, 'grid', [(i, i ^ s) for i in range(chunks)])]
    broadcast_in_dim x1, local copies, waits for them, and re-layouts: 0.1 us -> 0.9 us  [on_device(): var_weight[:, None]]
    unnamed x24 -> x22, local copies, waits for them, and re-layouts: 5.16 us -> 5.21 us
  transfers between devices with their start and end apart: 14 -> 14, of which waited for: 6 -> 5; matrix products, arithmetic and copies ran while one was open for 1% -> 3% of each run, Pallas kernels for 1% -> 6%
where the time goes in v2:
time: 66.1 us; the launch traced here: 65.8 us
  starting transfers between devices  23.1 us (35%)
  waiting for transfers between devices  15.3 us (23%)
  Pallas kernels  13.6 us (21%)
  blocking collectives  6.45 us (10%)
  local copies, waits for them, and re-layouts  6.2 us (9%)
  other arithmetic  1 us (2%)
    ppermute x14, starting transfers between devices, exchanged(): lax.ppermute(b, 'grid', [(i, i ^ s) for i in range(chunks)])  23.1 us
    ppermute x14, waiting for transfers between devices, exchanged(): lax.ppermute(b, 'grid', [(i, i ^ s) for i in range(chunks)])  15.3 us
    pallas_call x7, Pallas kernels, call(): pl.pallas_call(kernel, out_shape=out_shape, in_specs=[SMEM if i in scalar...  11.7 us
    all_gather x1, blocking collectives, on_device(): everyone = lax.all_gather(predicted, 'member', axis=0, tiled=True)  6.45 us
    unnamed x22, local copies, waits for them, and re-layouts  5.21 us
    pallas_call x1, Pallas kernels, last_sum(): pl.pallas_call(functools.partial(last_sum_kernel, members, order, capacit...  1.86 us
  transfers between devices with their start and end apart: 14, of which 5 were waited for; matrix products, arithmetic and copies ran while one was open for 3% of the time, Pallas kernels for 6%

profile of v2, /device:TPU:0, one launch (start us, length us, event | category | flops | bytes accessed | tf_op | source)
XLA Modules:
  0.0 65.8 jit_solution(10498088912880801211)
XLA Ops:
  0.0 1.3 %copy-done.4 = bf16[2,320,1024]{2,1,0:T(8,128)(2,1)S(1)} copy-done((bf16[2,320,1024]{2,1,0:T(8,128)(2,1)S(1)}, bf16[2,320,1024]{2,1,0:T(8,128)(2,1)}, u32[]{:S(2)}) %copy-start.4) | copy-done | bytes 1310744
  1.3 0.7 %copy-done.8 = s32[1,8,24]{2,1,0:T(8,128)S(1)} copy-done((s32[1,8,24]{2,1,0:T(8,128)S(1)}, s32[1,8,24]{2,1,0:T(8,128)}, u32[]{:S(2)}) %copy-start.8) | copy-done | bytes 792
  2.0 1.3 %shard_map.119 = (bf16[48,1024]{1,0:T(8,128)(2,1)S(1)}, bf16[48,1024]{1,0:T(8,128)(2,1)}, bf16[48,1024]{1,0:T(8,128)(2,1)}, bf16[48,1024]{1,0:T(8,128)(2,1)S(1)}...) custom-call(bf16[2,320,1024]{2,1,0:T(8,128)(2,1)S(1)} %copy-done.4, ...), custom_call_target="tpu_custom_call" | custom-call | flops 251658240 | bytes 2097924 | tf_op jit(solution)/shard_map/pallas_call | solution.py:32
  3.3 3.0 %collective-permute-start = (bf16[48,1024]{1,0:T(8,128)(2,1)}, bf16[48,1024]{1,0:T(8,128)(2,1)S(1)}, u32[]{:S(2)}, u32[]{:S(2)}) collective-permute-start(bf16[48,1024]{1,0:T(8,128)(2,1)} %get-tuple-element.29), channel_id=1, source_target_pairs={{0,4},{4,0},{8,12},{12,8},{16,20},{20,16},{24,28},{28,24},{1,5},{5... | collective-permute-start | bytes 294920 | tf_op jit(solution)/shard_map/ppermute | solution.py:349
  6.3 1.6 %collective-permute-start.1 = (bf16[48,1024]{1,0:T(8,128)(2,1)}, bf16[48,1024]{1,0:T(8,128)(2,1)S(1)}, u32[]{:S(2)}, u32[]{:S(2)}) collective-permute-start(bf16[48,1024]{1,0:T(8,128)(2,1)} %get-tuple-element.30), channel_id=1, source_target_pairs={{0,8},{4,12},{8,0},{12,4},{16,24},{20,28},{24,16},{28,20},{1,9},{5... | collective-permute-start | bytes 294920 | tf_op jit(solution)/shard_map/ppermute | solution.py:349
  7.8 3.0 %collective-permute-start.3 = (bf16[48,1024]{1,0:T(8,128)(2,1)S(1)}, bf16[48,1024]{1,0:T(8,128)(2,1)S(1)}, u32[]{:S(2)}, u32[]{:S(2)}) collective-permute-start(bf16[48,1024]{1,0:T(8,128)(2,1)S(1)} %get-tuple-element.34), channel_id=1, source_target_pairs={{0,16},{4,20},{8,24},{12,28},{16,0},{20,4},{24,8},{28,12},{1,17},{... | collective-permute-start | bytes 294920 | tf_op jit(solution)/shard_map/ppermute | solution.py:349
  10.8 1.3 %collective-permute-start.4 = (bf16[48,1024]{1,0:T(8,128)(2,1)S(1)}, bf16[48,1024]{1,0:T(8,128)(2,1)S(1)}, u32[]{:S(2)}, u32[]{:S(2)}) collective-permute-start(bf16[48,1024]{1,0:T(8,128)(2,1)S(1)} %get-tuple-element.35), channel_id=1, source_target_pairs={{0,20},{4,16},{8,28},{12,24},{16,4},{20,0},{24,12},{28,8},{1,21},{... | collective-permute-start | bytes 294920 | tf_op jit(solution)/shard_map/ppermute | solution.py:349
  12.1 0.1 iota_add_fusion
  12.2 0.1 add.23
  12.3 0.9 %copy.15.var_ref = f32[96,1]{1,0:T(8,128)S(1)} copy(f32[96,1]{0,1:T(1,128)} %bitcast.6) | data formatting | bytes 768 | tf_op jit(solution)/shard_map/broadcast_in_dim | solution.py:415
  13.2 0.7 %bitcast_select_fusion = s32[16,128]{1,0:T(8,128)S(1)} fusion(s32[128,16]{0,1:T(8,128)} %param.22, s32[128]{0:T(128)} %param.23), kind=kLoop, calls=%fused_computation.1 | loop fusion | flops 4096 | bytes 16896 | tf_op jit(solution)/shard_map/jit(_where)/select_n | solution.py:372
  13.9 0.2 convert_reduce_fusion.mult_ref
  14.1 3.7 %collective-permute-start.5 = (bf16[48,1024]{1,0:T(8,128)(2,1)S(1)}, bf16[48,1024]{1,0:T(8,128)(2,1)S(1)}, u32[]{:S(2)}, u32[]{:S(2)}) collective-permute-start(bf16[48,1024]{1,0:T(8,128)(2,1)S(1)} %get-tuple-element.36), channel_id=1, source_target_pairs={{0,24},{4,28},{8,16},{12,20},{16,8},{20,12},{24,0},{28,4},{1,25},{... | collective-permute-start | bytes 294920 | tf_op jit(solution)/shard_map/ppermute | solution.py:349
  17.8 1.6 %copy-done.3 = bf16[1024,1024]{1,0:T(8,128)(2,1)S(1)} copy-done((bf16[1024,1024]{1,0:T(8,128)(2,1)S(1)}, bf16[1024,1024]{1,0:T(8,128)(2,1)}, u32[]{:S(2)}) %copy-start.3) | copy-done | bytes 2097176
  19.4 0.5 shard_map.118.qm_ref
  19.9 1.6 %copy-done.1 = bf16[1024,1024]{1,0:T(8,128)(2,1)S(1)} copy-done((bf16[1024,1024]{1,0:T(8,128)(2,1)S(1)}, bf16[1024,1024]{1,0:T(8,128)(2,1)}, u32[]{:S(2)}) %copy-start.1) | copy-done | bytes 2097176
  21.5 1.3 %shard_map.120 = (f32[2,8,96,256]{3,2,1,0:T(8,128)S(1)}, bf16[2,96,1024]{2,1,0:T(8,128)(2,1)S(1)}) custom-call(bf16[256,1024]{1,0:T(8,128)(2,1)S(1)} %shard_map.118.qm_ref, bf16[1024,1024]{1,0:T(8,128)(2,1)S(1)} %copy-done, bf16[1024,1024]{1,0:T(8,128)(2,1)S(1)} %copy-done.1, f32[96,128]{1,0:T(8,128)S(1)} %slice.4.mult_ref, ...), custom_call_target="tpu_custom_call" | custom-call | flops 805306368 | bytes 7127040 | tf_op jit(solution)/shard_map/pallas_call | solution.py:32
  22.9 3.2 %collective-permute-done.4.refs_1_ = bf16[48,1024]{1,0:T(8,128)(2,1)S(1)} collective-permute-done((bf16[48,1024]{1,0:T(8,128)(2,1)S(1)}, bf16[48,1024]{1,0:T(8,128)(2,1)S(1)}, u32[]{:S(2)}, u32[]{:S(2)}) %collective-permute-start.4) | collective-permute-done | bytes 98336 | tf_op jit(solution)/shard_map/ppermute | solution.py:349
  26.1 2.6 %shard_map.121 = (f32[2,96,128]{2,1,0:T(8,128)S(1)}, bf16[2,8,192,256]{3,2,1,0:T(8,128)(2,1)S(1)}, bf16[2,192,1024]{2,1,0:T(8,128)(2,1)S(1)}) custom-call(bf16[256,1024]{1,0:T(8,128)(2,1)S(1)} %shard_map.118.qm_ref, bf16[1024,1024]{1,0:T(8,128)(2,1)S(1)} %copy-done, bf16[1024,1024]{1,0:T(8,128)(2,1)S(1)} %copy-done.2, bf16[96,1024]{1,0:T(8,128)(2,1)S(1)} %copy-done.5, ...), custom_call_target="tpu_custom_call" | custom-call | flops 805306368 | bytes 9830400 | tf_op jit(solution)/shard_map/pallas_call | solution.py:32
  28.7 6.4 %all_gather.3.every_ref = f32[8,96,128]{2,1,0:T(8,128)S(1)} all-gather(f32[2,96,128]{2,1,0:T(8,128)S(1)} %get-tuple-element.38.mine_ref), channel_id=1, replica_groups=mesh['grid'=8,'member'=4] {'member'}, dimensions={0}, use_global_device_ids=true | all-gather | bytes 491520 | tf_op jit(solution)/shard_map/all_gather | solution.py:399
  35.2 3.9 %shard_map.122 = (bf16[48,1024]{1,0:T(8,128)(2,1)S(1)}, bf16[48,1024]{1,0:T(8,128)(2,1)S(1)}, bf16[48,1024]{1,0:T(8,128)(2,1)S(1)}, bf16[48,1024]{1,0:T(8,128)(2...) custom-call(bf16[256,1024]{1,0:T(8,128)(2,1)S(1)} %shard_map.118.qm_ref, ...), custom_call_target="tpu_custom_call" | custom-call | flops 1610612736 | bytes 8995712 | tf_op jit(solution)/shard_map/pallas_call | solution.py:32
  39.1 5.2 %collective-permute-start.7 = (bf16[48,1024]{1,0:T(8,128)(2,1)S(1)}, bf16[48,1024]{1,0:T(8,128)(2,1)S(1)}, u32[]{:S(2)}, u32[]{:S(2)}) collective-permute-start(bf16[48,1024]{1,0:T(8,128)(2,1)S(1)} %get-tuple-element.42), channel_id=1, source_target_pairs={{0,16},{4,20},{8,24},{12,28},{16,0},{20,4},{24,8},{28,12},{1,17},{... | collective-permute-start | bytes 294920 | tf_op jit(solution)/shard_map/ppermute | solution.py:349
  44.4 1.5 %collective-permute-start.9 = (bf16[48,1024]{1,0:T(8,128)(2,1)S(1)}, bf16[48,1024]{1,0:T(8,128)(2,1)S(1)}, u32[]{:S(2)}, u32[]{:S(2)}) collective-permute-start(bf16[48,1024]{1,0:T(8,128)(2,1)S(1)} %get-tuple-element.44), channel_id=1, source_target_pairs={{0,4},{4,0},{8,12},{12,8},{16,20},{20,16},{24,28},{28,24},{1,5},{5... | collective-permute-start | bytes 294920 | tf_op jit(solution)/shard_map/ppermute | solution.py:349
  45.8 1.5 %shard_map.124 = (bf16[48,1024]{1,0:T(8,128)(2,1)S(1)}, bf16[48,1024]{1,0:T(8,128)(2,1)S(1)}, bf16[48,1024]{1,0:T(8,128)(2,1)S(1)}, bf16[48,1024]{1,0:T(8,128)(2,1)S(1)}) custom-call(bf16[1024,1024]{1,0:T(8,128)(2,1)S(1)} %copy-done, bf16[1024,1024]{1,0:T(8,128)(2,1)S(1)} %copy-done.2, bf16[192,1024]{1,0:T(8,128)(2,1)S(1)} %get-tuple-element.45.dk_ref, ...), custom_call_target="tpu_custom_call" | custom-call | flops 805306368 | bytes 5373952 | tf_op jit(solution)/shard_map/pallas_call | solution.py:32
  47.4 1.2 %collective-permute-start.10 = (bf16[48,1024]{1,0:T(8,128)(2,1)S(1)}, bf16[48,1024]{1,0:T(8,128)(2,1)S(1)}, u32[]{:S(2)}, u32[]{:S(2)}) collective-permute-start(bf16[48,1024]{1,0:T(8,128)(2,1)S(1)} %get-tuple-element.47), channel_id=1, source_target_pairs={{0,24},{4,28},{8,16},{12,20},{16,8},{20,12},{24,0},{28,4},{1,25},{... | collective-permute-start | bytes 294920 | tf_op jit(solution)/shard_map/ppermute | solution.py:349
  48.6 2.6 %collective-permute-start.11 = (bf16[48,1024]{1,0:T(8,128)(2,1)S(1)}, bf16[48,1024]{1,0:T(8,128)(2,1)S(1)}, u32[]{:S(2)}, u32[]{:S(2)}) collective-permute-start(bf16[48,1024]{1,0:T(8,128)(2,1)S(1)} %get-tuple-element.48), channel_id=1, source_target_pairs={{0,28},{4,24},{8,20},{12,16},{16,12},{20,8},{24,4},{28,0},{1,29},{... | collective-permute-start | bytes 294920 | tf_op jit(solution)/shard_map/ppermute | solution.py:349
  51.2 4.6 %collective-permute-done.7.refs_1_ = bf16[48,1024]{1,0:T(8,128)(2,1)S(1)} collective-permute-done((bf16[48,1024]{1,0:T(8,128)(2,1)S(1)}, bf16[48,1024]{1,0:T(8,128)(2,1)S(1)}, u32[]{:S(2)}, u32[]{:S(2)}) %collective-permute-start.7) | collective-permute-done | bytes 98336 | tf_op jit(solution)/shard_map/ppermute | solution.py:349
  55.8 2.6 %collective-permute-done.8.refs_2_ = bf16[48,1024]{1,0:T(8,128)(2,1)S(1)} collective-permute-done((bf16[48,1024]{1,0:T(8,128)(2,1)S(1)}, bf16[48,1024]{1,0:T(8,128)(2,1)S(1)}, u32[]{:S(2)}, u32[]{:S(2)}) %collective-permute-start.8) | collective-permute-done | bytes 98336 | tf_op jit(solution)/shard_map/ppermute | solution.py:349
  58.4 0.5 shard_map.123.before_ref
  59.0 1.4 %collective-permute-done.12.refs_2_ = bf16[48,1024]{1,0:T(8,128)(2,1)S(1)} collective-permute-done((bf16[48,1024]{1,0:T(8,128)(2,1)S(1)}, bf16[48,1024]{1,0:T(8,128)(2,1)S(1)}, u32[]{:S(2)}, u32[]{:S(2)}) %collective-permute-start.12) | collective-permute-done | bytes 98336 | tf_op jit(solution)/shard_map/ppermute | solution.py:349
  60.4 3.5 %collective-permute-done.13.refs_3_ = bf16[48,1024]{1,0:T(8,128)(2,1)S(1)} collective-permute-done((bf16[48,1024]{1,0:T(8,128)(2,1)S(1)}, bf16[48,1024]{1,0:T(8,128)(2,1)S(1)}, u32[]{:S(2)}, u32[]{:S(2)}) %collective-permute-start.13) | collective-permute-done | bytes 98336 | tf_op jit(solution)/shard_map/ppermute | solution.py:349
  63.9 1.9 %shard_map.125 = f32[2,320,1024]{2,1,0:T(8,128)} custom-call(s32[1,8,24]{2,1,0:T(8,128)S(1)} %copy-done.9, s32[1]{0:T(128)} %bitcast.me_ref, f32[2,320,1024]{2,1,0:T(8,128)S(1)} %shard_map.123.before_ref, bf16[48,1024]{1,0:T(8,128)(2,1)S(1)} %collective-permute-done.10.refs_0_, bf16[48,1024]{1,0:T(8,128)(2,1)S(1)} %collective-permute-done.11.refs_1_, ...), custom_call_target="tpu_custom_call" | custom-call | flops 125829120 | bytes 5636096 | tf_op jit(solution)/shard_map/pallas_call | solution.py:296
  (34 shorter events, 0.2 us)
Async XLA Ops:
  0.0 1.3 %copy-start.4 = (bf16[2,320,1024]{2,1,0:T(8,128)(2,1)S(1)}, bf16[2,320,1024]{2,1,0:T(8,128)(2,1)}, u32[]{:S(2)}) copy-start(bf16[2,320,1024]{2,1,0:T(8,128)(2,1)} %latent_ref.1) | copy-start | bytes 3932164
  1.3 0.7 %copy-start.8 = (s32[1,8,24]{2,1,0:T(8,128)S(1)}, s32[1,8,24]{2,1,0:T(8,128)}, u32[]{:S(2)}) copy-start(s32[1,8,24]{2,1,0:T(8,128)} %send_ref.5) | copy-start | bytes 2308
  2.0 15.8 %copy-start.6 = (bf16[128,1024]{1,0:T(8,128)(2,1)S(1)}, bf16[128,1024]{1,0:T(8,128)(2,1)}, u32[]{:S(2)}) copy-start(bf16[128,1024]{1,0:T(8,128)(2,1)} %feat_ref.1) | copy-start | bytes 786436
  3.3 10.8 %collective-permute-start = (bf16[48,1024]{1,0:T(8,128)(2,1)}, bf16[48,1024]{1,0:T(8,128)(2,1)S(1)}, u32[]{:S(2)}, u32[]{:S(2)}) collective-permute-start(bf16[48,1024]{1,0:T(8,128)(2,1)} %get-tuple-element.29), channel_id=1, source_target_pairs={{0,4},{4,0},{8,12},{12,8},{16,20},{20,16},{24,28},{28,24},{1,5},{5... | collective-permute-start | bytes 294920 | tf_op jit(solution)/shard_map/ppermute | solution.py:349
  6.3 11.5 %collective-permute-start.1 = (bf16[48,1024]{1,0:T(8,128)(2,1)}, bf16[48,1024]{1,0:T(8,128)(2,1)S(1)}, u32[]{:S(2)}, u32[]{:S(2)}) collective-permute-start(bf16[48,1024]{1,0:T(8,128)(2,1)} %get-tuple-element.30), channel_id=1, source_target_pairs={{0,8},{4,12},{8,0},{12,4},{16,24},{20,28},{24,16},{28,20},{1,9},{5... | collective-permute-start | bytes 294920 | tf_op jit(solution)/shard_map/ppermute | solution.py:349
  7.8 12.1 %collective-permute-start.2 = (bf16[48,1024]{1,0:T(8,128)(2,1)S(1)}, bf16[48,1024]{1,0:T(8,128)(2,1)S(1)}, u32[]{:S(2)}, u32[]{:S(2)}) collective-permute-start(bf16[48,1024]{1,0:T(8,128)(2,1)S(1)} %get-tuple-element.31), channel_id=1, source_target_pairs={{0,12},{4,8},{8,4},{12,0},{16,28},{20,24},{24,20},{28,16},{1,13},{... | collective-permute-start | bytes 294920 | tf_op jit(solution)/shard_map/ppermute | solution.py:349
  7.8 15.0 %collective-permute-start.3 = (bf16[48,1024]{1,0:T(8,128)(2,1)S(1)}, bf16[48,1024]{1,0:T(8,128)(2,1)S(1)}, u32[]{:S(2)}, u32[]{:S(2)}) collective-permute-start(bf16[48,1024]{1,0:T(8,128)(2,1)S(1)} %get-tuple-element.34), channel_id=1, source_target_pairs={{0,16},{4,20},{8,24},{12,28},{16,0},{20,4},{24,8},{28,12},{1,17},{... | collective-permute-start | bytes 294920 | tf_op jit(solution)/shard_map/ppermute | solution.py:349
  10.8 15.2 %collective-permute-start.4 = (bf16[48,1024]{1,0:T(8,128)(2,1)S(1)}, bf16[48,1024]{1,0:T(8,128)(2,1)S(1)}, u32[]{:S(2)}, u32[]{:S(2)}) collective-permute-start(bf16[48,1024]{1,0:T(8,128)(2,1)S(1)} %get-tuple-element.35), channel_id=1, source_target_pairs={{0,20},{4,16},{8,28},{12,24},{16,4},{20,0},{24,12},{28,8},{1,21},{... | collective-permute-start | bytes 294920 | tf_op jit(solution)/shard_map/ppermute | solution.py:349
  12.3 7.6 %copy-start = (bf16[1024,1024]{1,0:T(8,128)(2,1)S(1)}, bf16[1024,1024]{1,0:T(8,128)(2,1)}, u32[]{:S(2)}) copy-start(bf16[1024,1024]{1,0:T(8,128)(2,1)} %wk_ref.7) | copy-start | bytes 6291460
  14.1 11.9 %collective-permute-start.5 = (bf16[48,1024]{1,0:T(8,128)(2,1)S(1)}, bf16[48,1024]{1,0:T(8,128)(2,1)S(1)}, u32[]{:S(2)}, u32[]{:S(2)}) collective-permute-start(bf16[48,1024]{1,0:T(8,128)(2,1)S(1)} %get-tuple-element.36), channel_id=1, source_target_pairs={{0,24},{4,28},{8,16},{12,20},{16,8},{20,12},{24,0},{28,4},{1,25},{... | collective-permute-start | bytes 294920 | tf_op jit(solution)/shard_map/ppermute | solution.py:349
  17.8 8.2 %collective-permute-start.6 = (bf16[48,1024]{1,0:T(8,128)(2,1)S(1)}, bf16[48,1024]{1,0:T(8,128)(2,1)S(1)}, u32[]{:S(2)}, u32[]{:S(2)}) collective-permute-start(bf16[48,1024]{1,0:T(8,128)(2,1)S(1)} %get-tuple-element.37), channel_id=1, source_target_pairs={{0,28},{4,24},{8,20},{12,16},{16,12},{20,8},{24,4},{28,0},{1,29},{... | collective-permute-start | bytes 294920 | tf_op jit(solution)/shard_map/ppermute | solution.py:349
  17.8 1.6 %copy-start.3 = (bf16[1024,1024]{1,0:T(8,128)(2,1)S(1)}, bf16[1024,1024]{1,0:T(8,128)(2,1)}, u32[]{:S(2)}) copy-start(bf16[1024,1024]{1,0:T(8,128)(2,1)} %w_ref.1) | copy-start | bytes 6291460
  19.9 1.6 %copy-start.1 = (bf16[1024,1024]{1,0:T(8,128)(2,1)S(1)}, bf16[1024,1024]{1,0:T(8,128)(2,1)}, u32[]{:S(2)}) copy-start(bf16[1024,1024]{1,0:T(8,128)(2,1)} %wv_ref.7) | copy-start | bytes 6291460
  21.5 4.5 %copy-start.2 = (bf16[1024,1024]{1,0:T(8,128)(2,1)S(1)}, bf16[1024,1024]{1,0:T(8,128)(2,1)}, u32[]{:S(2)}) copy-start(bf16[1024,1024]{1,0:T(8,128)(2,1)} %wv_ref.7) | copy-start | bytes 6291460
  21.5 4.5 %copy-start.5 = (bf16[96,1024]{1,0:T(8,128)(2,1)S(1)}, bf16[96,1024]{1,0:T(8,128)(2,1)}, u32[]{:S(2)}) copy-start(bf16[96,1024]{1,0:T(8,128)(2,1)} %wout_ref.3) | copy-start | bytes 589828
  26.1 9.1 %copy-start.7 = (f32[96,128]{1,0:T(8,128)S(1)}, f32[96,128]{1,0:T(8,128)}, u32[]{:S(2)}) copy-start(f32[96,128]{1,0:T(8,128)} %truth_ref.1) | copy-start | bytes 147460
  26.1 9.1 %copy-start.10 = (f32[128]{0:T(128)S(1)}, f32[128]{0:T(128)}, u32[]{:S(2)}) copy-start(f32[128]{0:T(128)} %param.19) | copy-start | bytes 1540
  39.1 16.7 %collective-permute-start.7 = (bf16[48,1024]{1,0:T(8,128)(2,1)S(1)}, bf16[48,1024]{1,0:T(8,128)(2,1)S(1)}, u32[]{:S(2)}, u32[]{:S(2)}) collective-permute-start(bf16[48,1024]{1,0:T(8,128)(2,1)S(1)} %get-tuple-element.42), channel_id=1, source_target_pairs={{0,16},{4,20},{8,24},{12,28},{16,0},{20,4},{24,8},{28,12},{1,17},{... | collective-permute-start | bytes 294920 | tf_op jit(solution)/shard_map/ppermute | solution.py:349
  44.3 14.1 %collective-permute-start.8 = (bf16[48,1024]{1,0:T(8,128)(2,1)S(1)}, bf16[48,1024]{1,0:T(8,128)(2,1)S(1)}, u32[]{:S(2)}, u32[]{:S(2)}) collective-permute-start(bf16[48,1024]{1,0:T(8,128)(2,1)S(1)} %get-tuple-element.43), channel_id=1, source_target_pairs={{0,20},{4,16},{8,28},{12,24},{16,4},{20,0},{24,12},{28,8},{1,21},{... | collective-permute-start | bytes 294920 | tf_op jit(solution)/shard_map/ppermute | solution.py:349
  44.4 14.1 %collective-permute-start.9 = (bf16[48,1024]{1,0:T(8,128)(2,1)S(1)}, bf16[48,1024]{1,0:T(8,128)(2,1)S(1)}, u32[]{:S(2)}, u32[]{:S(2)}) collective-permute-start(bf16[48,1024]{1,0:T(8,128)(2,1)S(1)} %get-tuple-element.44), channel_id=1, source_target_pairs={{0,4},{4,0},{8,12},{12,8},{16,20},{20,16},{24,28},{28,24},{1,5},{5... | collective-permute-start | bytes 294920 | tf_op jit(solution)/shard_map/ppermute | solution.py:349
  45.8 12.6 %copy-start.9 = (s32[1,8,24]{2,1,0:T(8,128)S(1)}, s32[1,8,24]{2,1,0:T(8,128)}, u32[]{:S(2)}) copy-start(s32[1,8,24]{2,1,0:T(8,128)} %send_ref.5) | copy-start | bytes 2308
  47.4 11.6 %collective-permute-start.10 = (bf16[48,1024]{1,0:T(8,128)(2,1)S(1)}, bf16[48,1024]{1,0:T(8,128)(2,1)S(1)}, u32[]{:S(2)}, u32[]{:S(2)}) collective-permute-start(bf16[48,1024]{1,0:T(8,128)(2,1)S(1)} %get-tuple-element.47), channel_id=1, source_target_pairs={{0,24},{4,28},{8,16},{12,20},{16,8},{20,12},{24,0},{28,4},{1,25},{... | collective-permute-start | bytes 294920 | tf_op jit(solution)/shard_map/ppermute | solution.py:349
  48.6 10.4 %collective-permute-start.11 = (bf16[48,1024]{1,0:T(8,128)(2,1)S(1)}, bf16[48,1024]{1,0:T(8,128)(2,1)S(1)}, u32[]{:S(2)}, u32[]{:S(2)}) collective-permute-start(bf16[48,1024]{1,0:T(8,128)(2,1)S(1)} %get-tuple-element.48), channel_id=1, source_target_pairs={{0,28},{4,24},{8,20},{12,16},{16,12},{20,8},{24,4},{28,0},{1,29},{... | collective-permute-start | bytes 294920 | tf_op jit(solution)/shard_map/ppermute | solution.py:349
  55.8 4.6 %collective-permute-start.12 = (bf16[48,1024]{1,0:T(8,128)(2,1)S(1)}, bf16[48,1024]{1,0:T(8,128)(2,1)S(1)}, u32[]{:S(2)}, u32[]{:S(2)}) collective-permute-start(bf16[48,1024]{1,0:T(8,128)(2,1)S(1)} %get-tuple-element.49), channel_id=1, source_target_pairs={{0,8},{4,12},{8,0},{12,4},{16,24},{20,28},{24,16},{28,20},{1,9},{5... | collective-permute-start | bytes 294920 | tf_op jit(solution)/shard_map/ppermute | solution.py:349
  58.4 5.5 %collective-permute-start.13 = (bf16[48,1024]{1,0:T(8,128)(2,1)S(1)}, bf16[48,1024]{1,0:T(8,128)(2,1)S(1)}, u32[]{:S(2)}, u32[]{:S(2)}) collective-permute-start(bf16[48,1024]{1,0:T(8,128)(2,1)S(1)} %get-tuple-element.50), channel_id=1, source_target_pairs={{0,12},{4,8},{8,4},{12,0},{16,28},{20,24},{24,20},{28,16},{1,13},{... | collective-permute-start | bytes 294920 | tf_op jit(solution)/shard_map/ppermute | solution.py:349

commit v3 on v2

--- a/solution.py
+++ b/solution.py
@@ -3,6 +3,7 @@
 
 import jax
 import jax.numpy as jnp
+import numpy as np
 from jax import lax
 from jax.experimental import pallas as pl
 from jax.experimental.pallas import tpu as pltpu
@@ -11,7 +12,9 @@
 H = 16
 LANES = 128
 ROOM = 4 * 1024 * 1024
+WEIGHT = 40
 F32 = jnp.float32
+HUGE = float(np.finfo(np.float32).max)
 BF16 = jnp.bfloat16
 NN = (((1,), (0,)), ((), ()))
 NT = (((1,), (1,)), ((), ()))
@@ -36,7 +39,7 @@
         out_specs=VMEM if single else [VMEM] * len(outs),
         scratch_shapes=list(scratch),
         compiler_params=pltpu.CompilerParams(vmem_limit_bytes=limit or moved + 2 * held + ROOM),
-        cost_estimate=pl.CostEstimate(flops=flops, bytes_accessed=moved, transcendentals=0),
+        cost_estimate=pl.CostEstimate(flops=WEIGHT * flops, bytes_accessed=moved, transcendentals=0),
     )(*operands)
 
 
@@ -56,7 +59,11 @@
 
 def named_rows(send_ref, me_ref, order):
     return jnp.concatenate(
-        [send_ref[0, pl.ds(me_ref[0] ^ mask, 1), :] for mask in order], axis=1
+        [
+            send_ref[0, pl.ds(lax.rem(me_ref[0] + shift, send_ref.shape[1]), 1), :]
+            for shift in order
+        ],
+        axis=1,
     )
 
 
@@ -76,8 +83,11 @@
         out_refs[c][...] = rows[c * step : (c + 1) * step]
 
 
-def query_kernel(head_size, feat_ref, w_ref, out_ref):
+def query_kernel(
+    order, capacity, head_size, feat_ref, w_ref, names_ref, live_ref, me_ref, out_ref, mult_ref
+):
     points, width = feat_ref.shape
+    slots = names_ref.shape[0]
     per = LANES // head_size
     query = dot(feat_ref[...], w_ref[...]).astype(BF16)
     head = lax.broadcasted_iota(jnp.int32, (points, width), 1) // head_size % per
@@ -85,6 +95,14 @@
         out_ref[p * points : (p + 1) * points, :] = jnp.where(
             head == p, query, jnp.zeros_like(query)
         )
+    place = lax.broadcasted_iota(jnp.int32, (capacity, points), 0)
+    owners = [lax.rem(me_ref[0] + len(order) - shift, len(order)) for shift in order]
+    ids = jnp.concatenate([place + owner * capacity for owner in owners], axis=0)
+    mult = jnp.zeros(ids.shape, F32)
+    for k in range(slots):
+        name = jnp.where(live_ref[...] > k, names_ref[k : k + 1, :], -1)
+        mult = mult + jnp.where(ids == name, 1.0, 0.0)
+    mult_ref[...] = mult
 
 
 def project(rows, wk_ref, wv_ref, k_scr, v_ref, offset, members, chunks, capacity):
@@ -102,9 +120,11 @@
             )
 
 
-def raised_scores(k_scr, qm_ref, m, j, factor, bias):
+def raised_scores(k_scr, qm_ref, m, j, factor, bias, mult):
     cols = slice(j * LANES, (j + 1) * LANES)
-    return jnp.exp2(dot(k_scr[m, :, cols], qm_ref[:, cols], NT) * factor + bias)
+    raised = jnp.exp2(dot(k_scr[m, :, cols], qm_ref[:, cols], NT) * factor + bias)
+    raised = jnp.minimum(mult * raised, HUGE)
+    return raised, jnp.sum(raised, axis=0, keepdims=True)
 
 
 def exponent(head_size):
@@ -112,15 +132,18 @@
 
 
 def near_kernel(members, chunks, capacity, head_size, qm_ref, wk_ref, wv_ref, mult_ref, *refs):
-    raised_ref, v_ref, k_scr = refs[chunks:]
+    raised_ref, total_ref, v_ref, k_scr = refs[chunks:]
     groups = wk_ref.shape[0] // LANES
     rows = jnp.concatenate([r[...] for r in refs[:chunks]], axis=0)
     project(rows, wk_ref, wv_ref, k_scr, v_ref, 0, members, chunks, capacity)
-    mult = jnp.concatenate([mult_ref[...]] * (LANES // head_size), axis=1)
+    mult = mult_ref[: k_scr.shape[1], :]
+    mult = jnp.concatenate([mult] * (LANES // head_size), axis=1)
     bias = jnp.where(mult > 0.0, 0.0, -jnp.inf)
     for m in range(members):
         for j in range(groups):
-            raised_ref[m, j] = raised_scores(k_scr, qm_ref, m, j, exponent(head_size), bias)
+            raised_ref[m, j], total_ref[m, j] = raised_scores(
+                k_scr, qm_ref, m, j, exponent(head_size), bias, mult
+            )
 
 
 def forward_kernel(
@@ -134,6 +157,7 @@
     wout_ref,
     mult_ref,
     raised_ref,
+    total_ref,
     v_near_ref,
     *refs,
 ):
@@ -145,16 +169,19 @@
     rows = jnp.concatenate([r[...] for r in refs[:chunks]], axis=0)
     v_ref[:, :done, :] = v_near_ref[...]
     project(rows, wk_ref, wv_ref, k_scr, v_ref, done, members, chunks, capacity)
-    mult = jnp.concatenate([mult_ref[...]] * per, axis=1)
-    bias = jnp.where(mult[done:] > 0.0, 0.0, -jnp.inf)
+    mult = jnp.concatenate([mult_ref[done:, :]] * per, axis=1)
+    bias = jnp.where(mult > 0.0, 0.0, -jnp.inf)
     steps = [(m, j) for m in range(members) for j in range(groups)]
-    ahead = raised_scores(k_scr, qm_ref, *steps[0], exponent(head_size), bias)
+    ahead = raised_scores(k_scr, qm_ref, *steps[0], exponent(head_size), bias, mult)
     for i, (m, j) in enumerate(steps):
-        raised = jnp.concatenate([raised_ref[m, j], ahead], axis=0)
+        late, late_total = ahead
+        raised = jnp.concatenate([raised_ref[m, j], late], axis=0)
+        root = lax.rsqrt(total_ref[m, j] + late_total)
         if i + 1 < len(steps):
-            ahead = raised_scores(k_scr, qm_ref, *steps[i + 1], exponent(head_size), bias)
-        root = lax.rsqrt(jnp.sum(mult * raised, axis=0, keepdims=True))
-        weights = (raised * root * root * mult).astype(BF16)
+            ahead = raised_scores(
+                k_scr, qm_ref, *steps[i + 1], exponent(head_size), bias, mult
+            )
+        weights = (raised * root * root).astype(BF16)
         weight_ref[m, j] = weights
         both = dot(v_ref[m, :, j * LANES : (j + 1) * LANES], weights, TN)
         for p in range(per):
@@ -166,13 +193,18 @@
             pred_ref[m] = dot(wout_ref[...], att_scr[...])
 
 
-def return_rows(dk, dv, wk_ref, wv_ref, out_refs):
-    width = wk_ref.shape[0]
+def transpose_kernel(a_ref, b_ref, at_ref, bt_ref):
+    at_ref[...] = a_ref[...].T
+    bt_ref[...] = b_ref[...].T
+
+
+def return_rows(dk, dv, wkt_ref, wvt_ref, out_refs):
+    width = wkt_ref.shape[1]
     tile = 2 * LANES
     step = out_refs[0].shape[0]
     for t in range(width // tile):
         cols = slice(t * tile, (t + 1) * tile)
-        rows = dot(dk, wk_ref[cols, :], NT) + dot(dv, wv_ref[cols, :], NT)
+        rows = dot(dk, wkt_ref[:, cols]) + dot(dv, wvt_ref[:, cols])
         rows = rows.astype(BF16)
         for c, out_ref in enumerate(out_refs):
             out_ref[:, cols] = rows[c * step : (c + 1) * step]
@@ -185,10 +217,9 @@
     capacity,
     head_size,
     qm_ref,
-    wk_ref,
-    wv_ref,
+    wkt_ref,
+    wvt_ref,
     wout_ref,
-    every_ref,
     mine_ref,
     truth_ref,
     area_ref,
@@ -197,24 +228,31 @@
     v_ref,
     *refs,
 ):
-    out_refs = refs[: len(early)]
-    dk_ref, dv_ref, da_scr, dk_scr, dv_scr = refs[len(early) :]
-    width = wk_ref.shape[0]
+    other_refs = refs[: len(refs) - len(early) - 5]
+    out_refs = refs[len(other_refs) : -5]
+    dk_ref, dv_ref, da_scr, dk_scr, dv_scr = refs[-5:]
+    width = wkt_ref.shape[1]
     points = truth_ref.shape[1]
-    total = every_ref.shape[0]
+    every_refs = (mine_ref, *other_refs)
+    total = sum(r.shape[0] for r in every_refs)
     per = LANES // head_size
     groups = width // LANES
     scale = head_size ** (-0.5)
-    factor = area_ref[...] * var_ref[...]
+    variables = var_ref.shape[1]
+    wide = -variables % LANES
+    var = jnp.concatenate([var_ref[...], jnp.zeros((1, wide), F32)], axis=1)
+    var = jnp.broadcast_to(var, (LANES, variables + wide)).T[:variables, :1]
+    factor = area_ref[...] * var
     head = lax.broadcasted_iota(jnp.int32, (points, width), 1) // head_size % per
     for m in range(members):
         mine = mine_ref[m]
         miss = mine - truth_ref[...]
         first = miss * lax.rsqrt(1.0 + miss * miss) / total
         second = jnp.zeros_like(mine)
-        for f in range(total):
-            paired = mine - every_ref[f]
-            second = second + paired * lax.rsqrt(1.0 + paired * paired)
+        for every_ref in every_refs:
+            for f in range(every_ref.shape[0]):
+                paired = mine - every_ref[f]
+                second = second + paired * lax.rsqrt(1.0 + paired * paired)
         dpred = (factor * (first - second / (total * (total - 1)))).astype(BF16)
         d_attended = dot(dpred, wout_ref[...], TN).astype(BF16)
         for p in range(per):
@@ -236,8 +274,8 @@
             ahead = probs_grad(*steps[i + 1])
         weights = weight_ref[m, j].astype(F32)
         inner = jnp.sum(weights * d_probs, axis=0, keepdims=True)
-        d_scores = (weights * scale * (d_probs - inner)).astype(BF16)
-        d_keys.append(dot(d_scores, qm_ref[:, cols]))
+        d_scores = (weights * (d_probs - inner)).astype(BF16)
+        d_keys.append(dot(d_scores, qm_ref[:, cols]) * scale)
         d_values.append(dot(weight_ref[m, j], da_scr[m, :, cols]))
         if m == members - 1:
             dk_scr[:, cols] = by_chunk(d_keys, early, capacity).astype(BF16)
@@ -245,11 +283,11 @@
             dk_ref[:, cols] = by_chunk(d_keys, late, capacity).astype(BF16)
             dv_ref[:, cols] = by_chunk(d_values, late, capacity).astype(BF16)
             d_keys, d_values = [], []
-    return_rows(dk_scr[...], dv_scr[...], wk_ref, wv_ref, out_refs)
-
-
-def late_rows_kernel(wk_ref, wv_ref, dk_ref, dv_ref, *out_refs):
-    return_rows(dk_ref[...], dv_ref[...], wk_ref, wv_ref, out_refs)
+    return_rows(dk_scr[...], dv_scr[...], wkt_ref, wvt_ref, out_refs)
+
+
+def late_rows_kernel(wkt_ref, wvt_ref, dk_ref, dv_ref, *out_refs):
+    return_rows(dk_ref[...], dv_ref[...], wkt_ref, wvt_ref, out_refs)
 
 
 def first_sum_kernel(members, order, capacity, send_ref, me_ref, *refs):
@@ -311,8 +349,13 @@
     )(send_rows, me, before, *blocks)
 
 
+def shifts_from(chunks, first):
+    return tuple(dict.fromkeys([0, *(s % chunks for s in first), *range(chunks)]))
+
+
 def on_device(
     chunks,
+    ensembles,
     latent,
     grid_feat,
     w_query,
@@ -336,18 +379,19 @@
     step = members * capacity
     received = chunks * capacity
     me = lax.axis_index("grid")
-    half, quarter = chunks // 2, chunks // 4
-    order = tuple(range(chunks))
+    half = chunks // 2
+    order = shifts_from(chunks, (1, -1, half, half - 1, half + 1, 2, -2))
     near, far = order[:half], order[half:]
-    early = (0, *far[:quarter], *near[1 : max(quarter, 1)])
-    late = tuple(s for s in [*far, *near] if s not in early)
+    leave = shifts_from(chunks, (half, half - 1, half + 1, 1, 2, -2, -1))
+    early, late = leave[:half], leave[half:]
     here = me[None]
-    partners = jnp.bitwise_xor(me, jnp.arange(chunks, dtype=jnp.int32))
-
-    def exchanged(blocks, masks):
+
+    def exchanged(blocks, shifts, sign):
         return [
-            b if s == 0 else lax.ppermute(b, "grid", [(i, i ^ s) for i in range(chunks)])
-            for s, b in zip(masks, blocks)
+            b
+            if s == 0
+            else lax.ppermute(b, "grid", [(i, (i + sign * s) % chunks) for i in range(chunks)])
+            for s, b in zip(shifts, blocks)
         ]
 
     chunk_shape = jax.ShapeDtypeStruct((step, width), BF16)
@@ -359,62 +403,74 @@
         scalars=(2,),
         limit=40 * 1024 * 1024,
     )
-    arrived_near = exchanged(outgoing[:half], near)
-    arrived_far = exchanged(outgoing[half:], far)
-    query = call(
-        functools.partial(query_kernel, head_size),
-        jax.ShapeDtypeStruct((per * points, width), BF16),
-        [grid_feat, w_query],
+    arrived_near = exchanged(outgoing[: len(near)], near, 1)
+    arrived_far = exchanged(outgoing[len(near) :], far, 1)
+    query, mult = call(
+        functools.partial(query_kernel, order, capacity, head_size),
+        [
+            jax.ShapeDtypeStruct((per * points, width), BF16),
+            jax.ShapeDtypeStruct((received, points), F32),
+        ],
+        [grid_feat, w_query, neighbours.T, live_count[None, :], here],
         flops=2 * points * width * width,
-    )
-    row_ids = (partners[:, None] * capacity + jnp.arange(capacity, dtype=jnp.int32)).reshape(-1)
-    live = jnp.arange(slots)[:, None] < live_count[None, :]
-    names = jnp.where(live, neighbours.T, -1)
-    mult = jnp.sum((row_ids[None, :, None] == names[:, None, :]).astype(F32), axis=0)
-
-    raised, values_near = call(
-        functools.partial(near_kernel, members, half, capacity, head_size),
+        scalars=(4,),
+    )
+
+    raised, totals, values_near = call(
+        functools.partial(near_kernel, members, len(near), capacity, head_size),
         [
-            jax.ShapeDtypeStruct((members, groups, half * capacity, per * points), F32),
-            jax.ShapeDtypeStruct((members, half * capacity, width), BF16),
-        ],
-        [query, w_key, w_value, mult[: half * capacity], *arrived_near],
-        scratch=[pltpu.VMEM((members, half * capacity, width), BF16)],
-        flops=4 * members * half * capacity * width * width,
+            jax.ShapeDtypeStruct((members, groups, len(near) * capacity, per * points), F32),
+            jax.ShapeDtypeStruct((members, groups, 1, per * points), F32),
+            jax.ShapeDtypeStruct((members, len(near) * capacity, width), BF16),
+        ],
+        [query, w_key, w_value, mult, *arrived_near],
+        scratch=[pltpu.VMEM((members, len(near) * capacity, width), BF16)],
+        flops=4 * members * len(near) * capacity * width * width,
     )
     predicted, weights, values = call(
-        functools.partial(forward_kernel, members, (chunks - half), capacity, head_size),
+        functools.partial(forward_kernel, members, len(far), capacity, head_size),
         [
             jax.ShapeDtypeStruct((members, variables, points), F32),
             jax.ShapeDtypeStruct((members, groups, received, per * points), BF16),
             jax.ShapeDtypeStruct((members, received, width), BF16),
         ],
-        [query, w_key, w_value, w_out, mult, raised, values_near, *arrived_far],
+        [query, w_key, w_value, w_out, mult, raised, totals, values_near, *arrived_far],
         scratch=[
-            pltpu.VMEM((members, (chunks - half) * capacity, width), BF16),
+            pltpu.VMEM((members, len(far) * capacity, width), BF16),
             pltpu.VMEM((width, points), BF16),
         ],
-        flops=4 * members * (chunks - half) * capacity * width * width,
-    )
-    everyone = lax.all_gather(predicted, "member", axis=0, tiled=True)
+        flops=4 * members * len(far) * capacity * width * width,
+    )
+    everyone = [predicted]
+    bit = ensembles // 2
+    while bit:
+        pairs = [(i, i ^ bit) for i in range(ensembles)]
+        everyone += [lax.ppermute(p, "member", pairs) for p in everyone]
+        bit //= 2
+    w_key_t, w_value_t = call(
+        transpose_kernel,
+        [jax.ShapeDtypeStruct((width, width), BF16)] * 2,
+        [w_key, w_value],
+        flops=width * width,
+    )
     late_grad = jax.ShapeDtypeStruct((len(late) * step, width), BF16)
     *leaving_early, d_keys, d_values = call(
         functools.partial(
-            backward_kernel, members, early, late, capacity, head_size
+            backward_kernel, members, [order.index(c) for c in early], [order.index(c) for c in late], capacity, head_size
         ),
         [chunk_shape] * len(early) + [late_grad] * 2,
         [
             query,
-            w_key,
-            w_value,
+            w_key_t,
+            w_value_t,
             w_out,
-            everyone,
             predicted,
             truth,
             area[None, :],
-            var_weight[:, None],
+            var_weight[None, :],
             weights,
             values,
+            *everyone[1:],
         ],
         scratch=[
             pltpu.VMEM((members, per * points, width), BF16),
@@ -423,14 +479,14 @@
         ],
         flops=4 * members * received * width * width,
     )
-    returned_early = exchanged(leaving_early, early)
+    returned_early = exchanged(leaving_early, early, -1)
     leaving_late = call(
         late_rows_kernel,
         [chunk_shape] * len(late),
-        [w_key, w_value, d_keys, d_values],
+        [w_key_t, w_value_t, d_keys, d_values],
         flops=4 * len(late) * step * width * width,
     )
-    returned_late = exchanged(leaving_late, late)
+    returned_late = exchanged(leaving_late, late, -1)
     before = call(
         functools.partial(first_sum_kernel, members, early, capacity),
         jax.ShapeDtypeStruct((members, own_rows, width), F32),
@@ -443,7 +499,7 @@
 
 def solution(mesh):
     return jax.shard_map(
-        functools.partial(on_device, mesh.shape["grid"]),
+        functools.partial(on_device, mesh.shape["grid"], mesh.shape["member"]),
         mesh=mesh,
         in_specs=(
             P("member", "grid", None),

time: 66.1 us -> 60.6 us (0.917)
  blocking collectives: 6.45 us -> 0 us
  starting transfers between devices: 23.1 us -> 29.5 us
  local copies, waits for them, and re-layouts: 6.2 us -> 2.05 us
  other arithmetic: 1 us -> 0 us
    all_gather x1 -> x0, blocking collectives: 6.45 us -> none  [on_device(): everyone = lax.all_gather(predicted, 'member', axis=0, tiled=True)]
    ppermute x14 -> x17, starting transfers between devices: 23.1 us -> 29.5 us  [the longest x14 27.9 us: exchanged(): lax.ppermute(b, 'grid', [(i, (i + sign * s) % chunks) for i in range(chun...]
    unnamed x22 -> x24, local copies, waits for them, and re-layouts: 5.21 us -> 2.05 us
    broadcast_in_dim x1 -> x0, local copies, waits for them, and re-layouts: 0.9 us -> none  [on_device(): var_weight[:, None]]
    select_n x1 -> x0, other arithmetic: 0.7 us -> none  [on_device(): names = jnp.where(live, neighbours.T, -1)]
    pallas_call x7 -> x8, Pallas kernels: 11.7 us -> 11.4 us  [call(): pl.pallas_call(kernel, out_shape=out_shape, in_specs=[SMEM if i in scalar...]
    ppermute x14 -> x17, waiting for transfers between devices: 15.3 us -> 15.5 us  [the longest x14 12.3 us: exchanged(): lax.ppermute(b, 'grid', [(i, (i + sign * s) % chunks) for i in range(chun...]
  transfers between devices with their start and end apart: 14 -> 17, of which waited for: 5 -> 7; matrix products, arithmetic and copies ran while one was open for 3% -> 0% of each run, Pallas kernels for 6% -> 8%
where the time goes in v3:
time: 60.6 us; the launch traced here: 60.5 us
  starting transfers between devices  29.5 us (49%)
  waiting for transfers between devices  15.5 us (26%)
  Pallas kernels  13.2 us (22%)
  local copies, waits for them, and re-layouts  2.05 us (3%)
    ppermute x14, starting transfers between devices, exchanged(): lax.ppermute(b, 'grid', [(i, (i + sign * s) % chunks) for i in range(chun...  27.9 us
    ppermute x14, waiting for transfers between devices, exchanged(): lax.ppermute(b, 'grid', [(i, (i + sign * s) % chunks) for i in range(chun...  12.3 us
    pallas_call x8, Pallas kernels, call(): pl.pallas_call(kernel, out_shape=out_shape, in_specs=[SMEM if i in scalar...  11.4 us
    ppermute x3, waiting for transfers between devices, on_device(): everyone += [lax.ppermute(p, 'member', pairs) for p in everyone]  3.2 us
    unnamed x24, local copies, waits for them, and re-layouts  2.05 us
    pallas_call x1, Pallas kernels, last_sum(): pl.pallas_call(functools.partial(last_sum_kernel, members, order, capacit...  1.86 us
    ppermute x3, starting transfers between devices, on_device(): everyone += [lax.ppermute(p, 'member', pairs) for p in everyone]  1.54 us
  transfers between devices with their start and end apart: 17, of which 7 were waited for; matrix products, arithmetic and copies ran while one was open for 0% of the time, Pallas kernels for 8%

profile of v3, /device:TPU:0, one launch (start us, length us, event | category | flops | bytes accessed | tf_op | source)
XLA Modules:
  0.0 60.5 jit_solution(851064738884092936)
XLA Ops:
  0.0 0.7 %copy-done.2 = s32[1,8,24]{2,1,0:T(8,128)S(1)} copy-done((s32[1,8,24]{2,1,0:T(8,128)S(1)}, s32[1,8,24]{2,1,0:T(8,128)}, u32[]{:S(2)}) %copy-start.2) | copy-done | bytes 792
  0.7 1.3 %copy-done.4 = bf16[2,320,1024]{2,1,0:T(8,128)(2,1)S(1)} copy-done((bf16[2,320,1024]{2,1,0:T(8,128)(2,1)S(1)}, bf16[2,320,1024]{2,1,0:T(8,128)(2,1)}, u32[]{:S(2)}) %copy-start.4) | copy-done | bytes 1310744
  2.0 0.7 %shard_map.120 = (bf16[48,1024]{1,0:T(8,128)(2,1)S(1)}, bf16[48,1024]{1,0:T(8,128)(2,1)S(1)}, bf16[48,1024]{1,0:T(8,128)(2,1)S(1)}, bf16[48,1024]{1,0:T(8,128)(2...) custom-call(bf16[2,320,1024]{2,1,0:T(8,128)(2,1)S(1)} %copy-done.4, ...), custom_call_target="tpu_custom_call" | custom-call | flops 10066329600 | bytes 2097924 | tf_op jit(solution)/shard_map/pallas_call | solution.py:35
  2.7 3.0 %collective-permute-start = (bf16[48,1024]{1,0:T(8,128)(2,1)S(1)}, bf16[48,1024]{1,0:T(8,128)(2,1)S(1)}, u32[]{:S(2)}, u32[]{:S(2)}) collective-permute-start(bf16[48,1024]{1,0:T(8,128)(2,1)S(1)} %get-tuple-element.38), channel_id=1, source_target_pairs={{0,4},{4,8},{8,12},{12,16},{16,20},{20,24},{24,28},{28,0},{1,5},{5... | collective-permute-start | bytes 294920 | tf_op jit(solution)/shard_map/ppermute | solution.py:393
  5.7 3.1 %collective-permute-start.1 = (bf16[48,1024]{1,0:T(8,128)(2,1)S(1)}, bf16[48,1024]{1,0:T(8,128)(2,1)S(1)}, u32[]{:S(2)}, u32[]{:S(2)}) collective-permute-start(bf16[48,1024]{1,0:T(8,128)(2,1)S(1)} %get-tuple-element.39), channel_id=1, source_target_pairs={{0,28},{4,0},{8,4},{12,8},{16,12},{20,16},{24,20},{28,24},{1,29},{... | collective-permute-start | bytes 294920 | tf_op jit(solution)/shard_map/ppermute | solution.py:393
  8.8 0.9 %collective-permute-start.2 = (bf16[48,1024]{1,0:T(8,128)(2,1)S(1)}, bf16[48,1024]{1,0:T(8,128)(2,1)S(1)}, u32[]{:S(2)}, u32[]{:S(2)}) collective-permute-start(bf16[48,1024]{1,0:T(8,128)(2,1)S(1)} %get-tuple-element.40), channel_id=1, source_target_pairs={{0,16},{4,20},{8,24},{12,28},{16,0},{20,4},{24,8},{28,12},{1,17},{... | collective-permute-start | bytes 294920 | tf_op jit(solution)/shard_map/ppermute | solution.py:393
  9.7 1.6 %collective-permute-start.3 = (bf16[48,1024]{1,0:T(8,128)(2,1)S(1)}, bf16[48,1024]{1,0:T(8,128)(2,1)S(1)}, u32[]{:S(2)}, u32[]{:S(2)}) collective-permute-start(bf16[48,1024]{1,0:T(8,128)(2,1)S(1)} %get-tuple-element.44), channel_id=1, source_target_pairs={{0,12},{4,16},{8,20},{12,24},{16,28},{20,0},{24,4},{28,8},{1,13},{... | collective-permute-start | bytes 294920 | tf_op jit(solution)/shard_map/ppermute | solution.py:393
  11.3 2.2 %collective-permute-start.4 = (bf16[48,1024]{1,0:T(8,128)(2,1)S(1)}, bf16[48,1024]{1,0:T(8,128)(2,1)S(1)}, u32[]{:S(2)}, u32[]{:S(2)}) collective-permute-start(bf16[48,1024]{1,0:T(8,128)(2,1)S(1)} %get-tuple-element.45), channel_id=1, source_target_pairs={{0,20},{4,24},{8,28},{12,0},{16,4},{20,8},{24,12},{28,16},{1,21},{... | collective-permute-start | bytes 294920 | tf_op jit(solution)/shard_map/ppermute | solution.py:393
  13.6 0.5 shard_map.118
  14.1 1.6 %collective-permute-start.5 = (bf16[48,1024]{1,0:T(8,128)(2,1)S(1)}, bf16[48,1024]{1,0:T(8,128)(2,1)S(1)}, u32[]{:S(2)}, u32[]{:S(2)}) collective-permute-start(bf16[48,1024]{1,0:T(8,128)(2,1)S(1)} %get-tuple-element.46), channel_id=1, source_target_pairs={{0,8},{4,12},{8,16},{12,20},{16,24},{20,28},{24,0},{28,4},{1,9},{5... | collective-permute-start | bytes 294920 | tf_op jit(solution)/shard_map/ppermute | solution.py:393
  15.7 2.2 %collective-permute-start.6 = (bf16[48,1024]{1,0:T(8,128)(2,1)S(1)}, bf16[48,1024]{1,0:T(8,128)(2,1)S(1)}, u32[]{:S(2)}, u32[]{:S(2)}) collective-permute-start(bf16[48,1024]{1,0:T(8,128)(2,1)S(1)} %get-tuple-element.47), channel_id=1, source_target_pairs={{0,24},{4,28},{8,0},{12,4},{16,8},{20,12},{24,16},{28,20},{1,25},{... | collective-permute-start | bytes 294920 | tf_op jit(solution)/shard_map/ppermute | solution.py:393
  18.0 5.4 %collective-permute-done.2.refs_3_ = bf16[48,1024]{1,0:T(8,128)(2,1)S(1)} collective-permute-done((bf16[48,1024]{1,0:T(8,128)(2,1)S(1)}, bf16[48,1024]{1,0:T(8,128)(2,1)S(1)}, u32[]{:S(2)}, u32[]{:S(2)}) %collective-permute-start.2) | collective-permute-done | bytes 98336 | tf_op jit(solution)/shard_map/ppermute | solution.py:393
  23.4 1.5 %shard_map.121 = (f32[2,8,96,256]{3,2,1,0:T(8,128)S(1)}, f32[2,8,1,256]{3,2,1,0:T(1,128)S(1)}, bf16[2,96,1024]{2,1,0:T(8,128)(2,1)S(1)}) custom-call(bf16[256,1024]{1,0:T(8,128)(2,1)S(1)} %get-tuple-element.33.qm_ref, bf16[1024,1024]{1,0:T(8,128)(2,1)S(1)} %copy-done, bf16[1024,1024]{1,0:T(8,128)(2,1)S(1)} %copy-done.1, ...), custom_call_target="tpu_custom_call" | custom-call | flops 32212254720 | bytes 7192576 | tf_op jit(solution)/shard_map/pallas_call | solution.py:35
  24.9 0.3 collective-permute-done.6.refs_3_
  25.2 2.5 %shard_map.122 = (f32[2,96,128]{2,1,0:T(8,128)S(1)}, bf16[2,8,192,256]{3,2,1,0:T(8,128)(2,1)S(1)}, bf16[2,192,1024]{2,1,0:T(8,128)(2,1)S(1)}) custom-call(bf16[256,1024]{1,0:T(8,128)(2,1)S(1)} %get-tuple-element.33.qm_ref, bf16[1024,1024]{1,0:T(8,128)(2,1)S(1)} %copy-done, bf16[1024,1024]{1,0:T(8,128)(2,1)S(1)} %copy-done.1, bf16[96,1024]{1,0:T(8,128)(2,1)S(1)} %copy-done.6, ...), custom_call_target="tpu_custom_call" | custom-call | flops 32212254720 | bytes 9846784 | tf_op jit(solution)/shard_map/pallas_call | solution.py:35
  27.7 1.5 %collective-permute-start.7 = (f32[2,96,128]{2,1,0:T(8,128)S(1)}, f32[2,96,128]{2,1,0:T(8,128)S(1)}, u32[]{:S(2)}, u32[]{:S(2)}) collective-permute-start(f32[2,96,128]{2,1,0:T(8,128)S(1)} %get-tuple-element.48.mine_ref), channel_id=1, source_target_pairs={{0,2},{1,3},{2,0},{3,1},{4,6},{5,7},{6,4},{7,5},{8,10},{9,11},{10,... | collective-permute-start | bytes 294920 | tf_op jit(solution)/shard_map/ppermute | solution.py:448
  29.3 3.1 %collective-permute-done.7.refs_0_ = f32[2,96,128]{2,1,0:T(8,128)S(1)} collective-permute-done((f32[2,96,128]{2,1,0:T(8,128)S(1)}, f32[2,96,128]{2,1,0:T(8,128)S(1)}, u32[]{:S(2)}, u32[]{:S(2)}) %collective-permute-start.7) | collective-permute-done | bytes 98336 | tf_op jit(solution)/shard_map/ppermute | solution.py:448
  32.4 1.2 %shard_map.119 = (bf16[1024,1024]{1,0:T(8,128)(2,1)S(1)}, bf16[1024,1024]{1,0:T(8,128)(2,1)S(1)}) custom-call(bf16[1024,1024]{1,0:T(8,128)(2,1)S(1)} %copy-done, bf16[1024,1024]{1,0:T(8,128)(2,1)S(1)} %copy-done.1), custom_call_target="tpu_custom_call" | custom-call | flops 41943040 | bytes 8388608 | tf_op jit(solution)/shard_map/pallas_call | solution.py:35
  33.7 0.1 collective-permute-done.9.refs_2_
  33.7 3.4 %shard_map.123 = (bf16[48,1024]{1,0:T(8,128)(2,1)S(1)}, bf16[48,1024]{1,0:T(8,128)(2,1)S(1)}, bf16[48,1024]{1,0:T(8,128)(2,1)S(1)}, bf16[48,1024]{1,0:T(8,128)(2...) custom-call(bf16[256,1024]{1,0:T(8,128)(2,1)S(1)} %get-tuple-element.33.qm_ref, ...), custom_call_target="tpu_custom_call" | custom-call | flops 64424509440 | bytes 8897408 | tf_op jit(solution)/shard_map/pallas_call | solution.py:35
  37.2 4.0 %collective-permute-start.10 = (bf16[48,1024]{1,0:T(8,128)(2,1)S(1)}, bf16[48,1024]{1,0:T(8,128)(2,1)S(1)}, u32[]{:S(2)}, u32[]{:S(2)}) collective-permute-start(bf16[48,1024]{1,0:T(8,128)(2,1)S(1)} %get-tuple-element.52), channel_id=1, source_target_pairs={{0,16},{4,20},{8,24},{12,28},{16,0},{20,4},{24,8},{28,12},{1,17},{... | collective-permute-start | bytes 294920 | tf_op jit(solution)/shard_map/ppermute | solution.py:393
  41.2 0.2 collective-permute-start.11
  41.3 2.8 %collective-permute-start.12 = (bf16[48,1024]{1,0:T(8,128)(2,1)S(1)}, bf16[48,1024]{1,0:T(8,128)(2,1)S(1)}, u32[]{:S(2)}, u32[]{:S(2)}) collective-permute-start(bf16[48,1024]{1,0:T(8,128)(2,1)S(1)} %get-tuple-element.54), channel_id=1, source_target_pairs={{0,12},{4,16},{8,20},{12,24},{16,28},{20,0},{24,4},{28,8},{1,13},{... | collective-permute-start | bytes 294920 | tf_op jit(solution)/shard_map/ppermute | solution.py:393
  44.1 1.0 %shard_map.125 = (bf16[48,1024]{1,0:T(8,128)(2,1)S(1)}, bf16[48,1024]{1,0:T(8,128)(2,1)S(1)}, bf16[48,1024]{1,0:T(8,128)(2,1)S(1)}, bf16[48,1024]{1,0:T(8,128)(2,1)S(1)}) custom-call(bf16[1024,1024]{1,0:T(8,128)(2,1)S(1)} %get-tuple-element.34.wkt_ref, bf16[1024,1024]{1,0:T(8,128)(2,1)S(1)} %get-tuple-element.35.wvt_ref, ...), custom_call_target="tpu_custom_call" | custom-call | flops 32212254720 | bytes 5373952 | tf_op jit(solution)/shard_map/pallas_call | solution.py:35
  45.1 1.2 %collective-permute-start.13 = (bf16[48,1024]{1,0:T(8,128)(2,1)S(1)}, bf16[48,1024]{1,0:T(8,128)(2,1)S(1)}, u32[]{:S(2)}, u32[]{:S(2)}) collective-permute-start(bf16[48,1024]{1,0:T(8,128)(2,1)S(1)} %get-tuple-element.57), channel_id=1, source_target_pairs={{0,28},{4,0},{8,4},{12,8},{16,12},{20,16},{24,20},{28,24},{1,29},{... | collective-permute-start | bytes 294920 | tf_op jit(solution)/shard_map/ppermute | solution.py:393
  46.3 1.6 %collective-permute-start.14 = (bf16[48,1024]{1,0:T(8,128)(2,1)S(1)}, bf16[48,1024]{1,0:T(8,128)(2,1)S(1)}, u32[]{:S(2)}, u32[]{:S(2)}) collective-permute-start(bf16[48,1024]{1,0:T(8,128)(2,1)S(1)} %get-tuple-element.58), channel_id=1, source_target_pairs={{0,24},{4,28},{8,0},{12,4},{16,8},{20,12},{24,16},{28,20},{1,25},{... | collective-permute-start | bytes 294920 | tf_op jit(solution)/shard_map/ppermute | solution.py:393
  47.9 3.3 %collective-permute-done.10.refs_1_ = bf16[48,1024]{1,0:T(8,128)(2,1)S(1)} collective-permute-done((bf16[48,1024]{1,0:T(8,128)(2,1)S(1)}, bf16[48,1024]{1,0:T(8,128)(2,1)S(1)}, u32[]{:S(2)}, u32[]{:S(2)}) %collective-permute-start.10) | collective-permute-done | bytes 98336 | tf_op jit(solution)/shard_map/ppermute | solution.py:393
  51.2 3.5 %collective-permute-start.16 = (bf16[48,1024]{1,0:T(8,128)(2,1)S(1)}, bf16[48,1024]{1,0:T(8,128)(2,1)S(1)}, u32[]{:S(2)}, u32[]{:S(2)}) collective-permute-start(bf16[48,1024]{1,0:T(8,128)(2,1)S(1)} %get-tuple-element.60), channel_id=1, source_target_pairs={{0,4},{4,8},{8,12},{12,16},{16,20},{20,24},{24,28},{28,0},{1,5},{5... | collective-permute-start | bytes 294920 | tf_op jit(solution)/shard_map/ppermute | solution.py:393
  54.7 0.5 shard_map.124.before_ref
  55.3 3.2 %collective-permute-done.14.refs_1_ = bf16[48,1024]{1,0:T(8,128)(2,1)S(1)} collective-permute-done((bf16[48,1024]{1,0:T(8,128)(2,1)S(1)}, bf16[48,1024]{1,0:T(8,128)(2,1)S(1)}, u32[]{:S(2)}, u32[]{:S(2)}) %collective-permute-start.14) | collective-permute-done | bytes 98336 | tf_op jit(solution)/shard_map/ppermute | solution.py:393
  58.5 0.1 collective-permute-done.16.refs_3_
  58.6 1.9 %shard_map.126 = f32[2,320,1024]{2,1,0:T(8,128)} custom-call(s32[1,8,24]{2,1,0:T(8,128)S(1)} %copy-done.2, s32[1]{0:T(128)} %bitcast.me_ref, f32[2,320,1024]{2,1,0:T(8,128)S(1)} %shard_map.124.before_ref, bf16[48,1024]{1,0:T(8,128)(2,1)S(1)} %collective-permute-done.13.refs_0_, bf16[48,1024]{1,0:T(8,128)(2,1)S(1)} %collective-permute-done.14.refs_1_, ...), custom_call_target="tpu_custom_call" | custom-call | flops 125829120 | bytes 5636096 | tf_op jit(solution)/shard_map/pallas_call | solution.py:334
  (35 shorter events, 0.1 us)
Async XLA Ops:
  0.0 0.7 %copy-start.2 = (s32[1,8,24]{2,1,0:T(8,128)S(1)}, s32[1,8,24]{2,1,0:T(8,128)}, u32[]{:S(2)}) copy-start(s32[1,8,24]{2,1,0:T(8,128)} %send_ref.5) | copy-start | bytes 2308
  0.7 1.3 %copy-start.4 = (bf16[2,320,1024]{2,1,0:T(8,128)(2,1)S(1)}, bf16[2,320,1024]{2,1,0:T(8,128)(2,1)}, u32[]{:S(2)}) copy-start(bf16[2,320,1024]{2,1,0:T(8,128)(2,1)} %latent_ref.1) | copy-start | bytes 3932164
  2.0 11.5 %copy-start.3 = (bf16[1024,1024]{1,0:T(8,128)(2,1)S(1)}, bf16[1024,1024]{1,0:T(8,128)(2,1)}, u32[]{:S(2)}) copy-start(bf16[1024,1024]{1,0:T(8,128)(2,1)} %w_ref.1) | copy-start | bytes 6291460
  2.0 11.5 %copy-start.5 = (bf16[128,1024]{1,0:T(8,128)(2,1)S(1)}, bf16[128,1024]{1,0:T(8,128)(2,1)}, u32[]{:S(2)}) copy-start(bf16[128,1024]{1,0:T(8,128)(2,1)} %feat_ref.1) | copy-start | bytes 786436
  2.0 11.5 %copy-start.8 = (s32[128,16]{0,1:T(8,128)S(1)}, s32[128,16]{0,1:T(8,128)}, u32[]{:S(2)}) copy-start(s32[128,16]{0,1:T(8,128)} %param.22) | copy-start | bytes 24580
  2.0 11.5 %copy-start.9 = (s32[128]{0:T(128)S(1)}, s32[128]{0:T(128)}, u32[]{:S(2)}) copy-start(s32[128]{0:T(128)} %param.23) | copy-start | bytes 1540
  2.7 11.4 %collective-permute-start = (bf16[48,1024]{1,0:T(8,128)(2,1)S(1)}, bf16[48,1024]{1,0:T(8,128)(2,1)S(1)}, u32[]{:S(2)}, u32[]{:S(2)}) collective-permute-start(bf16[48,1024]{1,0:T(8,128)(2,1)S(1)} %get-tuple-element.38), channel_id=1, source_target_pairs={{0,4},{4,8},{8,12},{12,16},{16,20},{20,24},{24,28},{28,0},{1,5},{5... | collective-permute-start | bytes 294920 | tf_op jit(solution)/shard_map/ppermute | solution.py:393
  5.7 10.0 %collective-permute-start.1 = (bf16[48,1024]{1,0:T(8,128)(2,1)S(1)}, bf16[48,1024]{1,0:T(8,128)(2,1)S(1)}, u32[]{:S(2)}, u32[]{:S(2)}) collective-permute-start(bf16[48,1024]{1,0:T(8,128)(2,1)S(1)} %get-tuple-element.39), channel_id=1, source_target_pairs={{0,28},{4,0},{8,4},{12,8},{16,12},{20,16},{24,20},{28,24},{1,29},{... | collective-permute-start | bytes 294920 | tf_op jit(solution)/shard_map/ppermute | solution.py:393
  8.8 14.5 %collective-permute-start.2 = (bf16[48,1024]{1,0:T(8,128)(2,1)S(1)}, bf16[48,1024]{1,0:T(8,128)(2,1)S(1)}, u32[]{:S(2)}, u32[]{:S(2)}) collective-permute-start(bf16[48,1024]{1,0:T(8,128)(2,1)S(1)} %get-tuple-element.40), channel_id=1, source_target_pairs={{0,16},{4,20},{8,24},{12,28},{16,0},{20,4},{24,8},{28,12},{1,17},{... | collective-permute-start | bytes 294920 | tf_op jit(solution)/shard_map/ppermute | solution.py:393
  9.7 15.1 %collective-permute-start.3 = (bf16[48,1024]{1,0:T(8,128)(2,1)S(1)}, bf16[48,1024]{1,0:T(8,128)(2,1)S(1)}, u32[]{:S(2)}, u32[]{:S(2)}) collective-permute-start(bf16[48,1024]{1,0:T(8,128)(2,1)S(1)} %get-tuple-element.44), channel_id=1, source_target_pairs={{0,12},{4,16},{8,20},{12,24},{16,28},{20,0},{24,4},{28,8},{1,13},{... | collective-permute-start | bytes 294920 | tf_op jit(solution)/shard_map/ppermute | solution.py:393
  11.3 13.5 %collective-permute-start.4 = (bf16[48,1024]{1,0:T(8,128)(2,1)S(1)}, bf16[48,1024]{1,0:T(8,128)(2,1)S(1)}, u32[]{:S(2)}, u32[]{:S(2)}) collective-permute-start(bf16[48,1024]{1,0:T(8,128)(2,1)S(1)} %get-tuple-element.45), channel_id=1, source_target_pairs={{0,20},{4,24},{8,28},{12,0},{16,4},{20,8},{24,12},{28,16},{1,21},{... | collective-permute-start | bytes 294920 | tf_op jit(solution)/shard_map/ppermute | solution.py:393
  13.6 9.8 %copy-start = (bf16[1024,1024]{1,0:T(8,128)(2,1)S(1)}, bf16[1024,1024]{1,0:T(8,128)(2,1)}, u32[]{:S(2)}) copy-start(bf16[1024,1024]{1,0:T(8,128)(2,1)} %wk_ref.3) | copy-start | bytes 6291460
  13.6 9.8 %copy-start.1 = (bf16[1024,1024]{1,0:T(8,128)(2,1)S(1)}, bf16[1024,1024]{1,0:T(8,128)(2,1)}, u32[]{:S(2)}) copy-start(bf16[1024,1024]{1,0:T(8,128)(2,1)} %wv_ref.3) | copy-start | bytes 6291460
  14.1 10.8 %collective-permute-start.5 = (bf16[48,1024]{1,0:T(8,128)(2,1)S(1)}, bf16[48,1024]{1,0:T(8,128)(2,1)S(1)}, u32[]{:S(2)}, u32[]{:S(2)}) collective-permute-start(bf16[48,1024]{1,0:T(8,128)(2,1)S(1)} %get-tuple-element.46), channel_id=1, source_target_pairs={{0,8},{4,12},{8,16},{12,20},{16,24},{20,28},{24,0},{28,4},{1,9},{5... | collective-permute-start | bytes 294920 | tf_op jit(solution)/shard_map/ppermute | solution.py:393
  15.7 9.4 %collective-permute-start.6 = (bf16[48,1024]{1,0:T(8,128)(2,1)S(1)}, bf16[48,1024]{1,0:T(8,128)(2,1)S(1)}, u32[]{:S(2)}, u32[]{:S(2)}) collective-permute-start(bf16[48,1024]{1,0:T(8,128)(2,1)S(1)} %get-tuple-element.47), channel_id=1, source_target_pairs={{0,24},{4,28},{8,0},{12,4},{16,8},{20,12},{24,16},{28,20},{1,25},{... | collective-permute-start | bytes 294920 | tf_op jit(solution)/shard_map/ppermute | solution.py:393
  23.4 1.8 %copy-start.6 = (bf16[96,1024]{1,0:T(8,128)(2,1)S(1)}, bf16[96,1024]{1,0:T(8,128)(2,1)}, u32[]{:S(2)}) copy-start(bf16[96,1024]{1,0:T(8,128)(2,1)} %wout_ref.3) | copy-start | bytes 589828
  27.7 6.0 %copy-start.7 = (f32[96,128]{1,0:T(8,128)S(1)}, f32[96,128]{1,0:T(8,128)}, u32[]{:S(2)}) copy-start(f32[96,128]{1,0:T(8,128)} %truth_ref.1) | copy-start | bytes 147460
  27.7 6.0 %copy-start.10 = (f32[128]{0:T(128)S(1)}, f32[128]{0:T(128)}, u32[]{:S(2)}) copy-start(f32[128]{0:T(128)} %param.19) | copy-start | bytes 1540
  27.7 6.0 %copy-start.11 = (f32[96]{0:T(128)S(1)}, f32[96]{0:T(128)}, u32[]{:S(2)}) copy-start(f32[96]{0:T(128)} %param.20) | copy-start | bytes 1156
  27.7 4.7 %collective-permute-start.7 = (f32[2,96,128]{2,1,0:T(8,128)S(1)}, f32[2,96,128]{2,1,0:T(8,128)S(1)}, u32[]{:S(2)}, u32[]{:S(2)}) collective-permute-start(f32[2,96,128]{2,1,0:T(8,128)S(1)} %get-tuple-element.48.mine_ref), channel_id=1, source_target_pairs={{0,2},{1,3},{2,0},{3,1},{4,6},{5,7},{6,4},{7,5},{8,10},{9,11},{10,... | collective-permute-start | bytes 294920 | tf_op jit(solution)/shard_map/ppermute | solution.py:448
  29.3 4.4 %collective-permute-start.8 = (f32[2,96,128]{2,1,0:T(8,128)S(1)}, f32[2,96,128]{2,1,0:T(8,128)S(1)}, u32[]{:S(2)}, u32[]{:S(2)}) collective-permute-start(f32[2,96,128]{2,1,0:T(8,128)S(1)} %get-tuple-element.48.mine_ref), channel_id=1, source_target_pairs={{0,1},{1,0},{2,3},{3,2},{4,5},{5,4},{6,7},{7,6},{8,9},{9,8},{10,11... | collective-permute-start | bytes 294920 | tf_op jit(solution)/shard_map/ppermute | solution.py:448
  32.4 1.3 %collective-permute-start.9 = (f32[2,96,128]{2,1,0:T(8,128)S(1)}, f32[2,96,128]{2,1,0:T(8,128)S(1)}, u32[]{:S(2)}, u32[]{:S(2)}) collective-permute-start(f32[2,96,128]{2,1,0:T(8,128)S(1)} %collective-permute-done.7.refs_0_), channel_id=1, source_target_pairs={{0,1},{1,0},{2,3},{3,2},{4,5},{5,4},{6,7},{7,6},{8,9},{9,8},{10,11... | collective-permute-start | bytes 294920 | tf_op jit(solution)/shard_map/ppermute | solution.py:448
  37.2 14.1 %collective-permute-start.10 = (bf16[48,1024]{1,0:T(8,128)(2,1)S(1)}, bf16[48,1024]{1,0:T(8,128)(2,1)S(1)}, u32[]{:S(2)}, u32[]{:S(2)}) collective-permute-start(bf16[48,1024]{1,0:T(8,128)(2,1)S(1)} %get-tuple-element.52), channel_id=1, source_target_pairs={{0,16},{4,20},{8,24},{12,28},{16,0},{20,4},{24,8},{28,12},{1,17},{... | collective-permute-start | bytes 294920 | tf_op jit(solution)/shard_map/ppermute | solution.py:393
  41.2 10.1 %collective-permute-start.11 = (bf16[48,1024]{1,0:T(8,128)(2,1)S(1)}, bf16[48,1024]{1,0:T(8,128)(2,1)S(1)}, u32[]{:S(2)}, u32[]{:S(2)}) collective-permute-start(bf16[48,1024]{1,0:T(8,128)(2,1)S(1)} %get-tuple-element.53), channel_id=1, source_target_pairs={{0,20},{4,24},{8,28},{12,0},{16,4},{20,8},{24,12},{28,16},{1,21},{... | collective-permute-start | bytes 294920 | tf_op jit(solution)/shard_map/ppermute | solution.py:393
  41.3 13.4 %collective-permute-start.12 = (bf16[48,1024]{1,0:T(8,128)(2,1)S(1)}, bf16[48,1024]{1,0:T(8,128)(2,1)S(1)}, u32[]{:S(2)}, u32[]{:S(2)}) collective-permute-start(bf16[48,1024]{1,0:T(8,128)(2,1)S(1)} %get-tuple-element.54), channel_id=1, source_target_pairs={{0,12},{4,16},{8,20},{12,24},{16,28},{20,0},{24,4},{28,8},{1,13},{... | collective-permute-start | bytes 294920 | tf_op jit(solution)/shard_map/ppermute | solution.py:393
  45.1 10.2 %collective-permute-start.13 = (bf16[48,1024]{1,0:T(8,128)(2,1)S(1)}, bf16[48,1024]{1,0:T(8,128)(2,1)S(1)}, u32[]{:S(2)}, u32[]{:S(2)}) collective-permute-start(bf16[48,1024]{1,0:T(8,128)(2,1)S(1)} %get-tuple-element.57), channel_id=1, source_target_pairs={{0,28},{4,0},{8,4},{12,8},{16,12},{20,16},{24,20},{28,24},{1,29},{... | collective-permute-start | bytes 294920 | tf_op jit(solution)/shard_map/ppermute | solution.py:393
  46.3 12.1 %collective-permute-start.14 = (bf16[48,1024]{1,0:T(8,128)(2,1)S(1)}, bf16[48,1024]{1,0:T(8,128)(2,1)S(1)}, u32[]{:S(2)}, u32[]{:S(2)}) collective-permute-start(bf16[48,1024]{1,0:T(8,128)(2,1)S(1)} %get-tuple-element.58), channel_id=1, source_target_pairs={{0,24},{4,28},{8,0},{12,4},{16,8},{20,12},{24,16},{28,20},{1,25},{... | collective-permute-start | bytes 294920 | tf_op jit(solution)/shard_map/ppermute | solution.py:393
  51.2 7.2 %collective-permute-start.15 = (bf16[48,1024]{1,0:T(8,128)(2,1)S(1)}, bf16[48,1024]{1,0:T(8,128)(2,1)S(1)}, u32[]{:S(2)}, u32[]{:S(2)}) collective-permute-start(bf16[48,1024]{1,0:T(8,128)(2,1)S(1)} %get-tuple-element.59), channel_id=1, source_target_pairs={{0,8},{4,12},{8,16},{12,20},{16,24},{20,28},{24,0},{28,4},{1,9},{5... | collective-permute-start | bytes 294920 | tf_op jit(solution)/shard_map/ppermute | solution.py:393
  51.2 7.4 %collective-permute-start.16 = (bf16[48,1024]{1,0:T(8,128)(2,1)S(1)}, bf16[48,1024]{1,0:T(8,128)(2,1)S(1)}, u32[]{:S(2)}, u32[]{:S(2)}) collective-permute-start(bf16[48,1024]{1,0:T(8,128)(2,1)S(1)} %get-tuple-element.60), channel_id=1, source_target_pairs={{0,4},{4,8},{8,12},{12,16},{16,20},{20,24},{24,28},{28,0},{1,5},{5... | collective-permute-start | bytes 294920 | tf_op jit(solution)/shard_map/ppermute | solution.py:393

commit v4 on v3

--- a/solution.py
+++ b/solution.py
@@ -73,10 +73,28 @@
     return (rows == ids).astype(F32).astype(BF16)
 
 
-def gather_kernel(members, order, capacity, latent_ref, send_ref, me_ref, *out_refs):
-    chunks = len(order)
-    pick = one_hot(send_ref, me_ref, order, latent_ref.shape[1])
-    picked = [dot(pick, latent_ref[m], TN) for m in range(members)]
+def of_chunks(block, chunks, capacity):
+    return jnp.concatenate(
+        [block[c * capacity : (c + 1) * capacity] for c in chunks], axis=0
+    )
+
+
+def ids_kernel(out_ref):
+    out_ref[...] = lax.broadcasted_iota(jnp.int32, out_ref.shape, 0)
+
+
+def pick_kernel(order, send_ref, me_ref, ids_ref, out_ref):
+    rows = named_rows(send_ref, me_ref, order)
+    out_ref[...] = (rows == ids_ref[...]).astype(F32).astype(BF16)
+
+
+def one_hot_kernel(orders, send_ref, me_ref, *out_refs):
+    for order, out_ref in zip(orders, out_refs):
+        out_ref[...] = one_hot(send_ref, me_ref, order, out_ref.shape[0])
+
+
+def gather_kernel(members, chunks, capacity, latent_ref, pick_ref, *out_refs):
+    picked = [dot(pick_ref[...], latent_ref[m], TN) for m in range(members)]
     step = members * capacity
     rows = by_chunk(picked, range(chunks), capacity).astype(BF16)
     for c in range(chunks):
@@ -131,12 +149,14 @@
     return head_size ** (-0.5) * math.log2(math.e)
 
 
-def near_kernel(members, chunks, capacity, head_size, qm_ref, wk_ref, wv_ref, mult_ref, *refs):
+def near_kernel(
+    members, chunks, capacity, head_size, before, qm_ref, wk_ref, wv_ref, mult_ref, *refs
+):
     raised_ref, total_ref, v_ref, k_scr = refs[chunks:]
     groups = wk_ref.shape[0] // LANES
     rows = jnp.concatenate([r[...] for r in refs[:chunks]], axis=0)
     project(rows, wk_ref, wv_ref, k_scr, v_ref, 0, members, chunks, capacity)
-    mult = mult_ref[: k_scr.shape[1], :]
+    mult = mult_ref[before : before + k_scr.shape[1], :]
     mult = jnp.concatenate([mult] * (LANES // head_size), axis=1)
     bias = jnp.where(mult > 0.0, 0.0, -jnp.inf)
     for m in range(members):
@@ -156,18 +176,20 @@
     wv_ref,
     wout_ref,
     mult_ref,
-    raised_ref,
-    total_ref,
-    v_near_ref,
     *refs,
 ):
-    pred_ref, weight_ref, v_ref, k_scr, att_scr = refs[chunks:]
+    pred_ref, weight_ref, v_ref, k_scr, att_scr = refs[-5:]
+    chunk_refs = refs[-5 - chunks : -5]
+    parts = refs[: -5 - chunks]
+    raised_refs, total_refs, v_refs = parts[0::3], parts[1::3], parts[2::3]
     points = mult_ref.shape[1]
     per = LANES // head_size
     groups = wk_ref.shape[0] // LANES
-    done = v_near_ref.shape[1]
-    rows = jnp.concatenate([r[...] for r in refs[:chunks]], axis=0)
-    v_ref[:, :done, :] = v_near_ref[...]
+    done = 0
+    for v_part in v_refs:
+        v_ref[:, done : done + v_part.shape[1], :] = v_part[...]
+        done += v_part.shape[1]
+    rows = jnp.concatenate([r[...] for r in chunk_refs], axis=0)
     project(rows, wk_ref, wv_ref, k_scr, v_ref, done, members, chunks, capacity)
     mult = jnp.concatenate([mult_ref[done:, :]] * per, axis=1)
     bias = jnp.where(mult > 0.0, 0.0, -jnp.inf)
@@ -175,8 +197,8 @@
     ahead = raised_scores(k_scr, qm_ref, *steps[0], exponent(head_size), bias, mult)
     for i, (m, j) in enumerate(steps):
         late, late_total = ahead
-        raised = jnp.concatenate([raised_ref[m, j], late], axis=0)
-        root = lax.rsqrt(total_ref[m, j] + late_total)
+        raised = jnp.concatenate([r[m, j] for r in raised_refs] + [late], axis=0)
+        root = lax.rsqrt(sum([t[m, j] for t in total_refs], late_total))
         if i + 1 < len(steps):
             ahead = raised_scores(
                 k_scr, qm_ref, *steps[i + 1], exponent(head_size), bias, mult
@@ -193,9 +215,14 @@
             pred_ref[m] = dot(wout_ref[...], att_scr[...])
 
 
-def transpose_kernel(a_ref, b_ref, at_ref, bt_ref):
-    at_ref[...] = a_ref[...].T
-    bt_ref[...] = b_ref[...].T
+def first_kernel(sizes, orders, qm_ref, wk_ref, wv_ref, mult_ref, send_ref, me_ref, *refs):
+    *refs, k_scr = refs
+    last = len(refs) - 2 - len(orders)
+    wkt_ref, wvt_ref, *place_refs = refs[last:]
+    near_kernel(*sizes, qm_ref, wk_ref, wv_ref, mult_ref, *refs[:last], k_scr)
+    wkt_ref[...] = wk_ref[...].T
+    wvt_ref[...] = wv_ref[...].T
+    one_hot_kernel(orders, send_ref, me_ref, *place_refs)
 
 
 def return_rows(dk, dv, wkt_ref, wvt_ref, out_refs):
@@ -230,7 +257,7 @@
 ):
     other_refs = refs[: len(refs) - len(early) - 5]
     out_refs = refs[len(other_refs) : -5]
-    dk_ref, dv_ref, da_scr, dk_scr, dv_scr = refs[-5:]
+    ds_ref, w_ref, da_ref, dk_scr, dv_scr = refs[-5:]
     width = wkt_ref.shape[1]
     points = truth_ref.shape[1]
     every_refs = (mine_ref, *other_refs)
@@ -256,13 +283,13 @@
         dpred = (factor * (first - second / (total * (total - 1)))).astype(BF16)
         d_attended = dot(dpred, wout_ref[...], TN).astype(BF16)
         for p in range(per):
-            da_scr[m, p * points : (p + 1) * points, :] = jnp.where(
+            da_ref[m, p * points : (p + 1) * points, :] = jnp.where(
                 head == p, d_attended, jnp.zeros_like(d_attended)
             )
 
     def probs_grad(m, j):
         cols = slice(j * LANES, (j + 1) * LANES)
-        return dot(v_ref[m, :, cols], da_scr[m, :, cols], NT)
+        return dot(v_ref[m, :, cols], da_ref[m, :, cols], NT)
 
     steps = [(m, j) for j in range(groups) for m in range(members)]
     ahead = probs_grad(*steps[0])
@@ -274,39 +301,51 @@
             ahead = probs_grad(*steps[i + 1])
         weights = weight_ref[m, j].astype(F32)
         inner = jnp.sum(weights * d_probs, axis=0, keepdims=True)
-        d_scores = (weights * (d_probs - inner)).astype(BF16)
-        d_keys.append(dot(d_scores, qm_ref[:, cols]) * scale)
-        d_values.append(dot(weight_ref[m, j], da_scr[m, :, cols]))
+        d_scores = weights * (d_probs - inner)
+        ds_ref[m, j] = of_chunks(d_scores, late, capacity).astype(BF16)
+        w_ref[m, j] = of_chunks(weights, late, capacity).astype(BF16)
+        now = of_chunks(d_scores, early, capacity).astype(BF16)
+        d_keys.append(dot(now, qm_ref[:, cols]) * scale)
+        now = of_chunks(weights, early, capacity).astype(BF16)
+        d_values.append(dot(now, da_ref[m, :, cols]))
         if m == members - 1:
-            dk_scr[:, cols] = by_chunk(d_keys, early, capacity).astype(BF16)
-            dv_scr[:, cols] = by_chunk(d_values, early, capacity).astype(BF16)
-            dk_ref[:, cols] = by_chunk(d_keys, late, capacity).astype(BF16)
-            dv_ref[:, cols] = by_chunk(d_values, late, capacity).astype(BF16)
+            dk_scr[:, cols] = by_chunk(d_keys, range(len(early)), capacity).astype(BF16)
+            dv_scr[:, cols] = by_chunk(d_values, range(len(early)), capacity).astype(BF16)
             d_keys, d_values = [], []
     return_rows(dk_scr[...], dv_scr[...], wkt_ref, wvt_ref, out_refs)
 
 
-def late_rows_kernel(wkt_ref, wvt_ref, dk_ref, dv_ref, *out_refs):
-    return_rows(dk_ref[...], dv_ref[...], wkt_ref, wvt_ref, out_refs)
-
-
-def first_sum_kernel(members, order, capacity, send_ref, me_ref, *refs):
-    chunks = len(order)
-    out_ref = refs[chunks]
-    place = one_hot(send_ref, me_ref, order, out_ref.shape[1])
+def late_rows_kernel(
+    chunks, capacity, head_size, qm_ref, wkt_ref, wvt_ref, ds_ref, w_ref, da_ref, *refs
+):
+    out_refs = refs[:chunks]
+    dk_scr, dv_scr = refs[chunks:]
+    members, groups = ds_ref.shape[:2]
+    scale = head_size ** (-0.5)
+    for j in range(groups):
+        cols = slice(j * LANES, (j + 1) * LANES)
+        d_keys = [dot(ds_ref[m, j], qm_ref[:, cols]) * scale for m in range(members)]
+        d_values = [dot(w_ref[m, j], da_ref[m, :, cols]) for m in range(members)]
+        dk_scr[:, cols] = by_chunk(d_keys, range(chunks), capacity).astype(BF16)
+        dv_scr[:, cols] = by_chunk(d_values, range(chunks), capacity).astype(BF16)
+    return_rows(dk_scr[...], dv_scr[...], wkt_ref, wvt_ref, out_refs)
+
+
+def first_sum_kernel(members, capacity, place_ref, *refs):
+    *_, out_ref = refs
+    chunks = len(refs) - 1
+    place = place_ref[...]
     back = jnp.concatenate([r[...] for r in refs[:chunks]], axis=0).astype(F32)
     for m in range(members):
         mine = of_member(back, m, members, chunks, capacity).astype(BF16)
         out_ref[m] = dot(place, mine)
 
 
-def last_sum_kernel(members, order, capacity, send_ref, me_ref, before_ref, *refs):
-    chunks = len(order)
+def last_sum_kernel(members, capacity, place_ref, before_ref, *refs):
+    chunks = len(refs) - 3
     out_ref, sum_scr, sems = refs[chunks:]
-    own_rows, width = out_ref.shape[1:]
     parts = sems.shape[1]
-    part = width // parts
-    place = one_hot(send_ref, me_ref, order, own_rows)
+    part = out_ref.shape[1] // parts
     back = jnp.concatenate([r[...] for r in refs[:chunks]], axis=0).astype(F32)
     mine = [
         of_member(back, m, members, chunks, capacity).astype(BF16) for m in range(members)
@@ -314,11 +353,11 @@
     sends = []
     for m in range(members):
         for p in range(parts):
-            cols = slice(p * part, (p + 1) * part)
-            sum_scr[m, :, cols] = before_ref[m, :, cols] + dot(place, mine[m][:, cols])
+            rows = slice(p * part, (p + 1) * part)
+            sum_scr[m, rows, :] = before_ref[m, rows, :] + dot(place_ref[rows, :], mine[m])
             there = pl.ds(p * part, part)
             send = pltpu.make_async_copy(
-                sum_scr.at[m, :, there], out_ref.at[m, :, there], sems.at[m, p]
+                sum_scr.at[m, there], out_ref.at[m, there], sems.at[m, p]
             )
             send.start()
             sends.append(send)
@@ -326,15 +365,15 @@
         send.wait()
 
 
-def last_sum(members, order, capacity, send_rows, me, before, blocks):
+def last_sum(members, capacity, place, before, blocks):
     step, width = blocks[0].shape
     own_rows = before.shape[1]
-    parts = 4 if width % (4 * LANES) == 0 else 1
-    moved = len(order) * step * width * 2 + 2 * members * own_rows * width * 4
+    parts = next(p for p in (5, 4, 2, 1) if own_rows % (p * 16) == 0)
+    moved = len(blocks) * step * width * 2 + 2 * members * own_rows * width * 4
     return pl.pallas_call(
-        functools.partial(last_sum_kernel, members, order, capacity),
+        functools.partial(last_sum_kernel, members, capacity),
         out_shape=jax.ShapeDtypeStruct((members, own_rows, width), F32),
-        in_specs=[VMEM, SMEM] + [VMEM] * (1 + len(order)),
+        in_specs=[VMEM] * (2 + len(blocks)),
         out_specs=pl.BlockSpec(memory_space=pltpu.HBM),
         scratch_shapes=[
             pltpu.VMEM((members, own_rows, width), F32),
@@ -342,11 +381,11 @@
         ],
         compiler_params=pltpu.CompilerParams(vmem_limit_bytes=2 * moved + 2 * ROOM),
         cost_estimate=pl.CostEstimate(
-            flops=2 * len(order) * step * own_rows * width,
+            flops=2 * len(blocks) * step * own_rows * width,
             bytes_accessed=moved,
             transcendentals=0,
         ),
-    )(send_rows, me, before, *blocks)
+    )(place, before, *blocks)
 
 
 def shifts_from(chunks, first):
@@ -380,8 +419,8 @@
     received = chunks * capacity
     me = lax.axis_index("grid")
     half = chunks // 2
-    order = shifts_from(chunks, (1, -1, half, half - 1, half + 1, 2, -2))
-    near, far = order[:half], order[half:]
+    order = shifts_from(chunks, (half, 1, -1, half - 1, half + 1, 2, -2))
+    groups_in = [order[:half], order[half:]]
     leave = shifts_from(chunks, (half, half - 1, half + 1, 1, 2, -2, -1))
     early, late = leave[:half], leave[half:]
     here = me[None]
@@ -395,16 +434,29 @@
         ]
 
     chunk_shape = jax.ShapeDtypeStruct((step, width), BF16)
+    ids = call(
+        ids_kernel,
+        jax.ShapeDtypeStruct((own_rows, received), jnp.int32),
+        [],
+        flops=members * received * own_rows * width,
+    )
+    pick = call(
+        functools.partial(pick_kernel, order),
+        jax.ShapeDtypeStruct((own_rows, received), BF16),
+        [send_rows, here, ids],
+        flops=members * received * own_rows * width,
+        scalars=(1,),
+    )
     outgoing = call(
-        functools.partial(gather_kernel, members, order, capacity),
+        functools.partial(gather_kernel, members, chunks, capacity),
         [chunk_shape] * chunks,
-        [latent, send_rows, here],
+        [latent, pick],
         flops=2 * members * received * own_rows * width,
-        scalars=(2,),
         limit=40 * 1024 * 1024,
     )
-    arrived_near = exchanged(outgoing[: len(near)], near, 1)
-    arrived_far = exchanged(outgoing[len(near) :], far, 1)
+    arrived_first, arrived_last = [
+        exchanged([outgoing[order.index(s)] for s in group], group, 1) for group in groups_in
+    ]
     query, mult = call(
         functools.partial(query_kernel, order, capacity, head_size),
         [
@@ -416,30 +468,37 @@
         scalars=(4,),
     )
 
-    raised, totals, values_near = call(
-        functools.partial(near_kernel, members, len(near), capacity, head_size),
+    before = len(arrived_first) * capacity
+    *parts, w_key_t, w_value_t, place_early, place_late = call(
+        functools.partial(
+            first_kernel, (members, len(arrived_first), capacity, head_size, 0), [early, late]
+        ),
         [
-            jax.ShapeDtypeStruct((members, groups, len(near) * capacity, per * points), F32),
+            jax.ShapeDtypeStruct((members, groups, before, per * points), F32),
             jax.ShapeDtypeStruct((members, groups, 1, per * points), F32),
-            jax.ShapeDtypeStruct((members, len(near) * capacity, width), BF16),
-        ],
-        [query, w_key, w_value, mult, *arrived_near],
-        scratch=[pltpu.VMEM((members, len(near) * capacity, width), BF16)],
-        flops=4 * members * len(near) * capacity * width * width,
-    )
+            jax.ShapeDtypeStruct((members, before, width), BF16),
+        ]
+        + [jax.ShapeDtypeStruct((width, width), BF16)] * 2
+        + [jax.ShapeDtypeStruct((own_rows, len(s) * capacity), BF16) for s in (early, late)],
+        [query, w_key, w_value, mult, send_rows, here, *arrived_first],
+        scratch=[pltpu.VMEM((members, before, width), BF16)],
+        flops=4 * members * before * width * width,
+        scalars=(5,),
+    )
+    rows_here = len(arrived_last) * capacity
     predicted, weights, values = call(
-        functools.partial(forward_kernel, members, len(far), capacity, head_size),
+        functools.partial(forward_kernel, members, len(arrived_last), capacity, head_size),
         [
             jax.ShapeDtypeStruct((members, variables, points), F32),
             jax.ShapeDtypeStruct((members, groups, received, per * points), BF16),
             jax.ShapeDtypeStruct((members, received, width), BF16),
         ],
-        [query, w_key, w_value, w_out, mult, raised, totals, values_near, *arrived_far],
+        [query, w_key, w_value, w_out, mult, *parts, *arrived_last],
         scratch=[
-            pltpu.VMEM((members, len(far) * capacity, width), BF16),
+            pltpu.VMEM((members, rows_here, width), BF16),
             pltpu.VMEM((width, points), BF16),
         ],
-        flops=4 * members * len(far) * capacity * width * width,
+        flops=4 * members * rows_here * width * width,
     )
     everyone = [predicted]
     bit = ensembles // 2
@@ -447,18 +506,21 @@
         pairs = [(i, i ^ bit) for i in range(ensembles)]
         everyone += [lax.ppermute(p, "member", pairs) for p in everyone]
         bit //= 2
-    w_key_t, w_value_t = call(
-        transpose_kernel,
-        [jax.ShapeDtypeStruct((width, width), BF16)] * 2,
-        [w_key, w_value],
-        flops=width * width,
-    )
-    late_grad = jax.ShapeDtypeStruct((len(late) * step, width), BF16)
-    *leaving_early, d_keys, d_values = call(
+    late_grad = jax.ShapeDtypeStruct(
+        (members, groups, len(late) * capacity, per * points), BF16
+    )
+    *leaving_early, d_scores, late_weights, d_attended = call(
         functools.partial(
-            backward_kernel, members, [order.index(c) for c in early], [order.index(c) for c in late], capacity, head_size
+            backward_kernel,
+            members,
+            [order.index(c) for c in early],
+            [order.index(c) for c in late],
+            capacity,
+            head_size,
         ),
-        [chunk_shape] * len(early) + [late_grad] * 2,
+        [chunk_shape] * len(early)
+        + [late_grad] * 2
+        + [jax.ShapeDtypeStruct((members, per * points, width), BF16)],
         [
             query,
             w_key_t,
@@ -472,29 +534,25 @@
             values,
             *everyone[1:],
         ],
-        scratch=[
-            pltpu.VMEM((members, per * points, width), BF16),
-            pltpu.VMEM((len(early) * step, width), BF16),
-            pltpu.VMEM((len(early) * step, width), BF16),
-        ],
+        scratch=[pltpu.VMEM((len(early) * step, width), BF16)] * 2,
         flops=4 * members * received * width * width,
     )
     returned_early = exchanged(leaving_early, early, -1)
     leaving_late = call(
-        late_rows_kernel,
+        functools.partial(late_rows_kernel, len(late), capacity, head_size),
         [chunk_shape] * len(late),
-        [w_key_t, w_value_t, d_keys, d_values],
+        [query, w_key_t, w_value_t, d_scores, late_weights, d_attended],
+        scratch=[pltpu.VMEM((len(late) * step, width), BF16)] * 2,
         flops=4 * len(late) * step * width * width,
     )
     returned_late = exchanged(leaving_late, late, -1)
     before = call(
-        functools.partial(first_sum_kernel, members, early, capacity),
+        functools.partial(first_sum_kernel, members, capacity),
         jax.ShapeDtypeStruct((members, own_rows, width), F32),
-        [send_rows, here, *returned_early],
+        [place_early, *returned_early],
         flops=2 * len(early) * step * own_rows * width,
-        scalars=(1,),
-    )
-    return last_sum(members, late, capacity, send_rows, here, before, returned_late)
+    )
+    return last_sum(members, capacity, place_late, before, returned_late)
 
 
 def solution(mesh):

time: 60.6 us -> 59.3 us (0.979)
  waiting for transfers between devices: 15.5 us -> 12.8 us
  starting transfers between devices: 29.5 us -> 31.8 us
  Pallas kernels: 13.2 us -> 12.5 us
    ppermute x14, waiting for transfers between devices: 12.3 us -> 8.35 us  [exchanged(): lax.ppermute(b, 'grid', [(i, (i + sign * s) % chunks) for i in range(chun...]
    ppermute x14, starting transfers between devices: 27.9 us -> 30.2 us  [exchanged(): lax.ppermute(b, 'grid', [(i, (i + sign * s) % chunks) for i in range(chun...]
    ppermute x3, waiting for transfers between devices: 3.2 us -> 4.41 us  [on_device(): everyone += [lax.ppermute(p, 'member', pairs) for p in everyone]]
    pallas_call x8 -> x9, Pallas kernels: 11.4 us -> 10.8 us  [call(): pl.pallas_call(kernel, out_shape=out_shape, in_specs=[SMEM if i in scalar...]
  transfers between devices with their start and end apart: 17 -> 17, of which waited for: 7 -> 7; matrix products, arithmetic and copies ran while one was open for 0% -> 0% of each run, Pallas kernels for 8% -> 7%
where the time goes in v4:
time: 59.3 us; the launch traced here: 59.1 us
  starting transfers between devices  31.8 us (54%)
  waiting for transfers between devices  12.8 us (22%)
  Pallas kernels  12.5 us (21%)
  local copies, waits for them, and re-layouts  1.89 us (3%)
    ppermute x14, starting transfers between devices, exchanged(): lax.ppermute(b, 'grid', [(i, (i + sign * s) % chunks) for i in range(chun...  30.2 us
    pallas_call x9, Pallas kernels, call(): pl.pallas_call(kernel, out_shape=out_shape, in_specs=[SMEM if i in scalar...  10.8 us
    ppermute x14, waiting for transfers between devices, exchanged(): lax.ppermute(b, 'grid', [(i, (i + sign * s) % chunks) for i in range(chun...  8.35 us
    ppermute x3, waiting for transfers between devices, on_device(): everyone += [lax.ppermute(p, 'member', pairs) for p in everyone]  4.41 us
    unnamed x24, local copies, waits for them, and re-layouts  1.89 us
    pallas_call x1, Pallas kernels, last_sum(): pl.pallas_call(functools.partial(last_sum_kernel, members, capacity), out...  1.75 us
    ppermute x3, starting transfers between devices, on_device(): everyone += [lax.ppermute(p, 'member', pairs) for p in everyone]  1.57 us
  transfers between devices with their start and end apart: 17, of which 7 were waited for; matrix products, arithmetic and copies ran while one was open for 0% of the time, Pallas kernels for 7%

profile of v4, /device:TPU:0, one launch (start us, length us, event | category | flops | bytes accessed | tf_op | source)
XLA Modules:
  0.0 59.1 jit_solution(12494260282433043368)
XLA Ops:
  0.0 0.7 %copy-done.8 = s32[1,8,24]{2,1,0:T(8,128)S(1)} copy-done((s32[1,8,24]{2,1,0:T(8,128)S(1)}, s32[1,8,24]{2,1,0:T(8,128)}, u32[]{:S(2)}) %copy-start.8) | copy-done | bytes 792
  0.7 0.1 shard_map.120.pick_ref
  0.8 1.2 %copy-done.3 = bf16[2,320,1024]{2,1,0:T(8,128)(2,1)S(1)} copy-done((bf16[2,320,1024]{2,1,0:T(8,128)(2,1)S(1)}, bf16[2,320,1024]{2,1,0:T(8,128)(2,1)}, u32[]{:S(2)}) %copy-start.3) | copy-done | bytes 1310744
  2.0 0.6 shard_map.121
  2.6 4.1 %collective-permute-start = (bf16[48,1024]{1,0:T(8,128)(2,1)S(1)}, bf16[48,1024]{1,0:T(8,128)(2,1)S(1)}, u32[]{:S(2)}, u32[]{:S(2)}) collective-permute-start(bf16[48,1024]{1,0:T(8,128)(2,1)S(1)} %get-tuple-element.39), channel_id=1, source_target_pairs={{0,16},{4,20},{8,24},{12,28},{16,0},{20,4},{24,8},{28,12},{1,17},{... | collective-permute-start | bytes 294920 | tf_op jit(solution)/shard_map/ppermute | solution.py:432
  6.7 1.5 %collective-permute-start.1 = (bf16[48,1024]{1,0:T(8,128)(2,1)S(1)}, bf16[48,1024]{1,0:T(8,128)(2,1)S(1)}, u32[]{:S(2)}, u32[]{:S(2)}) collective-permute-start(bf16[48,1024]{1,0:T(8,128)(2,1)S(1)} %get-tuple-element.40), channel_id=1, source_target_pairs={{0,4},{4,8},{8,12},{12,16},{16,20},{20,24},{24,28},{28,0},{1,5},{5... | collective-permute-start | bytes 294920 | tf_op jit(solution)/shard_map/ppermute | solution.py:432
  8.2 3.2 %collective-permute-start.2 = (bf16[48,1024]{1,0:T(8,128)(2,1)S(1)}, bf16[48,1024]{1,0:T(8,128)(2,1)S(1)}, u32[]{:S(2)}, u32[]{:S(2)}) collective-permute-start(bf16[48,1024]{1,0:T(8,128)(2,1)S(1)} %get-tuple-element.41), channel_id=1, source_target_pairs={{0,28},{4,0},{8,4},{12,8},{16,12},{20,16},{24,20},{28,24},{1,29},{... | collective-permute-start | bytes 294920 | tf_op jit(solution)/shard_map/ppermute | solution.py:432
  11.5 3.8 %collective-permute-start.4 = (bf16[48,1024]{1,0:T(8,128)(2,1)S(1)}, bf16[48,1024]{1,0:T(8,128)(2,1)S(1)}, u32[]{:S(2)}, u32[]{:S(2)}) collective-permute-start(bf16[48,1024]{1,0:T(8,128)(2,1)S(1)} %get-tuple-element.50), channel_id=1, source_target_pairs={{0,20},{4,24},{8,28},{12,0},{16,4},{20,8},{24,12},{28,16},{1,21},{... | collective-permute-start | bytes 294920 | tf_op jit(solution)/shard_map/ppermute | solution.py:432
  15.3 0.5 shard_map.118
  15.8 0.1 collective-permute-start.5
  15.9 3.8 %collective-permute-start.6 = (bf16[48,1024]{1,0:T(8,128)(2,1)S(1)}, bf16[48,1024]{1,0:T(8,128)(2,1)S(1)}, u32[]{:S(2)}, u32[]{:S(2)}) collective-permute-start(bf16[48,1024]{1,0:T(8,128)(2,1)S(1)} %get-tuple-element.52), channel_id=1, source_target_pairs={{0,24},{4,28},{8,0},{12,4},{16,8},{20,12},{24,16},{28,20},{1,25},{... | collective-permute-start | bytes 294920 | tf_op jit(solution)/shard_map/ppermute | solution.py:432
  19.7 0.0 copy-start.5
  19.7 1.8 %shard_map.122 = (f32[2,8,96,256]{3,2,1,0:T(8,128)S(1)}, f32[2,8,1,256]{3,2,1,0:T(1,128)S(1)}, bf16[2,96,1024]{2,1,0:T(8,128)(2,1)S(1)}, bf16[1024,1024]{1,0:T(8...) custom-call(bf16[256,1024]{1,0:T(8,128)(2,1)S(1)} %get-tuple-element.36.qm_, ...), custom_call_target="tpu_custom_call" | custom-call | flops 32212254720 | bytes 11510532 | tf_op jit(solution)/shard_map/pallas_call | solution.py:35
  21.6 0.8 %collective-permute-done.5.refs_5_ = bf16[48,1024]{1,0:T(8,128)(2,1)S(1)} collective-permute-done((bf16[48,1024]{1,0:T(8,128)(2,1)S(1)}, bf16[48,1024]{1,0:T(8,128)(2,1)S(1)}, u32[]{:S(2)}, u32[]{:S(2)}) %collective-permute-start.5) | collective-permute-done | bytes 98336 | tf_op jit(solution)/shard_map/ppermute | solution.py:432
  22.4 0.9 %collective-permute-done.6.refs_6_ = bf16[48,1024]{1,0:T(8,128)(2,1)S(1)} collective-permute-done((bf16[48,1024]{1,0:T(8,128)(2,1)S(1)}, bf16[48,1024]{1,0:T(8,128)(2,1)S(1)}, u32[]{:S(2)}, u32[]{:S(2)}) %collective-permute-start.6) | collective-permute-done | bytes 98336 | tf_op jit(solution)/shard_map/ppermute | solution.py:432
  23.3 2.5 %shard_map.123 = (f32[2,96,128]{2,1,0:T(8,128)S(1)}, bf16[2,8,192,256]{3,2,1,0:T(8,128)(2,1)S(1)}, bf16[2,192,1024]{2,1,0:T(8,128)(2,1)S(1)}) custom-call(bf16[256,1024]{1,0:T(8,128)(2,1)S(1)} %get-tuple-element.36.qm_ref, bf16[1024,1024]{1,0:T(8,128)(2,1)S(1)} %copy-done.1, bf16[1024,1024]{1,0:T(8,128)(2,1)S(1)} %copy-done.2, ...), custom_call_target="tpu_custom_call" | custom-call | flops 32212254720 | bytes 9846784 | tf_op jit(solution)/shard_map/pallas_call | solution.py:35
  25.8 1.6 %collective-permute-start.7 = (f32[2,96,128]{2,1,0:T(8,128)S(1)}, f32[2,96,128]{2,1,0:T(8,128)S(1)}, u32[]{:S(2)}, u32[]{:S(2)}) collective-permute-start(f32[2,96,128]{2,1,0:T(8,128)S(1)} %get-tuple-element.53.mine_ref), channel_id=1, source_target_pairs={{0,2},{1,3},{2,0},{3,1},{4,6},{5,7},{6,4},{7,5},{8,10},{9,11},{10,... | collective-permute-start | bytes 294920 | tf_op jit(solution)/shard_map/ppermute | solution.py:507
  27.4 3.1 %collective-permute-done.7.refs_0_ = f32[2,96,128]{2,1,0:T(8,128)S(1)} collective-permute-done((f32[2,96,128]{2,1,0:T(8,128)S(1)}, f32[2,96,128]{2,1,0:T(8,128)S(1)}, u32[]{:S(2)}, u32[]{:S(2)}) %collective-permute-start.7) | collective-permute-done | bytes 98336 | tf_op jit(solution)/shard_map/ppermute | solution.py:507
  30.5 1.3 %collective-permute-done.9.refs_2_ = f32[2,96,128]{2,1,0:T(8,128)S(1)} collective-permute-done((f32[2,96,128]{2,1,0:T(8,128)S(1)}, f32[2,96,128]{2,1,0:T(8,128)S(1)}, u32[]{:S(2)}, u32[]{:S(2)}) %collective-permute-start.9) | collective-permute-done | bytes 98336 | tf_op jit(solution)/shard_map/ppermute | solution.py:507
  31.8 3.2 %shard_map.124 = (bf16[48,1024]{1,0:T(8,128)(2,1)S(1)}, bf16[48,1024]{1,0:T(8,128)(2,1)S(1)}, bf16[48,1024]{1,0:T(8,128)(2,1)S(1)}, bf16[48,1024]{1,0:T(8,128)(2...) custom-call(bf16[256,1024]{1,0:T(8,128)(2,1)S(1)} %get-tuple-element, ...), custom_call_target="tpu_custom_call" | custom-call | flops 64424509440 | bytes 10732416 | tf_op jit(solution)/shard_map/pallas_call | solution.py:35
  35.1 4.1 %collective-permute-start.10 = (bf16[48,1024]{1,0:T(8,128)(2,1)S(1)}, bf16[48,1024]{1,0:T(8,128)(2,1)S(1)}, u32[]{:S(2)}, u32[]{:S(2)}) collective-permute-start(bf16[48,1024]{1,0:T(8,128)(2,1)S(1)} %get-tuple-element.57), channel_id=1, source_target_pairs={{0,16},{4,20},{8,24},{12,28},{16,0},{20,4},{24,8},{28,12},{1,17},{... | collective-permute-start | bytes 294920 | tf_op jit(solution)/shard_map/ppermute | solution.py:432
  39.1 0.8 %collective-permute-start.11 = (bf16[48,1024]{1,0:T(8,128)(2,1)S(1)}, bf16[48,1024]{1,0:T(8,128)(2,1)S(1)}, u32[]{:S(2)}, u32[]{:S(2)}) collective-permute-start(bf16[48,1024]{1,0:T(8,128)(2,1)S(1)} %get-tuple-element.58), channel_id=1, source_target_pairs={{0,20},{4,24},{8,28},{12,0},{16,4},{20,8},{24,12},{28,16},{1,21},{... | collective-permute-start | bytes 294920 | tf_op jit(solution)/shard_map/ppermute | solution.py:432
  39.9 2.1 %collective-permute-start.12 = (bf16[48,1024]{1,0:T(8,128)(2,1)S(1)}, bf16[48,1024]{1,0:T(8,128)(2,1)S(1)}, u32[]{:S(2)}, u32[]{:S(2)}) collective-permute-start(bf16[48,1024]{1,0:T(8,128)(2,1)S(1)} %get-tuple-element.59), channel_id=1, source_target_pairs={{0,12},{4,16},{8,20},{12,24},{16,28},{20,0},{24,4},{28,8},{1,13},{... | collective-permute-start | bytes 294920 | tf_op jit(solution)/shard_map/ppermute | solution.py:432
  42.1 1.5 %shard_map.126 = (bf16[48,1024]{1,0:T(8,128)(2,1)S(1)}, bf16[48,1024]{1,0:T(8,128)(2,1)S(1)}, bf16[48,1024]{1,0:T(8,128)(2,1)S(1)}, bf16[48,1024]{1,0:T(8,128)(2,1)S(1)}) custom-call(bf16[256,1024]{1,0:T(8,128)(2,1)S(1)} %get-tuple-element.36.qm_ref, bf16[1024,1024]{1,0:T(8,128)(2,1)S(1)} %get-tuple-element.44.wkt_ref, ...), custom_call_target="tpu_custom_call" | custom-call | flops 32212254720 | bytes 7733248 | tf_op jit(solution)/shard_map/pallas_call | solution.py:35
  43.6 2.3 %collective-permute-start.13 = (bf16[48,1024]{1,0:T(8,128)(2,1)S(1)}, bf16[48,1024]{1,0:T(8,128)(2,1)S(1)}, u32[]{:S(2)}, u32[]{:S(2)}) collective-permute-start(bf16[48,1024]{1,0:T(8,128)(2,1)S(1)} %get-tuple-element.63), channel_id=1, source_target_pairs={{0,28},{4,0},{8,4},{12,8},{16,12},{20,16},{24,20},{28,24},{1,29},{... | collective-permute-start | bytes 294920 | tf_op jit(solution)/shard_map/ppermute | solution.py:432
  45.9 0.9 %collective-permute-start.14 = (bf16[48,1024]{1,0:T(8,128)(2,1)S(1)}, bf16[48,1024]{1,0:T(8,128)(2,1)S(1)}, u32[]{:S(2)}, u32[]{:S(2)}) collective-permute-start(bf16[48,1024]{1,0:T(8,128)(2,1)S(1)} %get-tuple-element.64), channel_id=1, source_target_pairs={{0,24},{4,28},{8,0},{12,4},{16,8},{20,12},{24,16},{28,20},{1,25},{... | collective-permute-start | bytes 294920 | tf_op jit(solution)/shard_map/ppermute | solution.py:432
  46.8 2.4 %collective-permute-done.10.refs_1_ = bf16[48,1024]{1,0:T(8,128)(2,1)S(1)} collective-permute-done((bf16[48,1024]{1,0:T(8,128)(2,1)S(1)}, bf16[48,1024]{1,0:T(8,128)(2,1)S(1)}, u32[]{:S(2)}, u32[]{:S(2)}) %collective-permute-start.10) | collective-permute-done | bytes 98336 | tf_op jit(solution)/shard_map/ppermute | solution.py:432
  49.1 3.5 %collective-permute-start.16 = (bf16[48,1024]{1,0:T(8,128)(2,1)S(1)}, bf16[48,1024]{1,0:T(8,128)(2,1)S(1)}, u32[]{:S(2)}, u32[]{:S(2)}) collective-permute-start(bf16[48,1024]{1,0:T(8,128)(2,1)S(1)} %get-tuple-element.66), channel_id=1, source_target_pairs={{0,4},{4,8},{8,12},{12,16},{16,20},{20,24},{24,28},{28,0},{1,5},{5... | collective-permute-start | bytes 294920 | tf_op jit(solution)/shard_map/ppermute | solution.py:432
  52.7 0.5 shard_map.125.before_ref
  53.1 3.8 %collective-permute-done.14.refs_1_ = bf16[48,1024]{1,0:T(8,128)(2,1)S(1)} collective-permute-done((bf16[48,1024]{1,0:T(8,128)(2,1)S(1)}, bf16[48,1024]{1,0:T(8,128)(2,1)S(1)}, u32[]{:S(2)}, u32[]{:S(2)}) %collective-permute-start.14) | collective-permute-done | bytes 98336 | tf_op jit(solution)/shard_map/ppermute | solution.py:432
  57.0 0.4 collective-permute-done.16.refs_3_
  57.4 1.7 %shard_map.127 = f32[2,320,1024]{2,1,0:T(8,128)} custom-call(bf16[320,96]{1,0:T(8,128)(2,1)S(1)} %get-tuple-element.42.place_ref, f32[2,320,1024]{2,1,0:T(8,128)S(1)} %shard_map.125.before_ref, bf16[48,1024]{1,0:T(8,128)(2,1)S(1)} %collective-permute-done.13.refs_0_, bf16[48,1024]{1,0:T(8,128)(2,1)S(1)} %collective-permute-done.14.refs_1_, ...), custom_call_target="tpu_custom_call" | custom-call | flops 125829120 | bytes 5636096 | tf_op jit(solution)/shard_map/pallas_call | solution.py:373
  (36 shorter events, 0.1 us)
Async XLA Ops:
  0.0 0.7 %copy-start.8 = (s32[1,8,24]{2,1,0:T(8,128)S(1)}, s32[1,8,24]{2,1,0:T(8,128)}, u32[]{:S(2)}) copy-start(s32[1,8,24]{2,1,0:T(8,128)} %send_ref.3) | copy-start | bytes 2308
  0.7 1.3 %copy-start.3 = (bf16[2,320,1024]{2,1,0:T(8,128)(2,1)S(1)}, bf16[2,320,1024]{2,1,0:T(8,128)(2,1)}, u32[]{:S(2)}) copy-start(bf16[2,320,1024]{2,1,0:T(8,128)(2,1)} %latent_ref.1) | copy-start | bytes 3932164
  2.0 13.3 %copy-start = (bf16[1024,1024]{1,0:T(8,128)(2,1)S(1)}, bf16[1024,1024]{1,0:T(8,128)(2,1)}, u32[]{:S(2)}) copy-start(bf16[1024,1024]{1,0:T(8,128)(2,1)} %w_ref.1) | copy-start | bytes 6291460
  2.0 13.3 %copy-start.4 = (bf16[128,1024]{1,0:T(8,128)(2,1)S(1)}, bf16[128,1024]{1,0:T(8,128)(2,1)}, u32[]{:S(2)}) copy-start(bf16[128,1024]{1,0:T(8,128)(2,1)} %feat_ref.1) | copy-start | bytes 786436
  2.0 13.3 %copy-start.7 = (s32[128,16]{0,1:T(8,128)S(1)}, s32[128,16]{0,1:T(8,128)}, u32[]{:S(2)}) copy-start(s32[128,16]{0,1:T(8,128)} %param.22) | copy-start | bytes 24580
  2.0 13.3 %copy-start.9 = (s32[128]{0:T(128)S(1)}, s32[128]{0:T(128)}, u32[]{:S(2)}) copy-start(s32[128]{0:T(128)} %param.23) | copy-start | bytes 1540
  2.6 13.2 %collective-permute-start = (bf16[48,1024]{1,0:T(8,128)(2,1)S(1)}, bf16[48,1024]{1,0:T(8,128)(2,1)S(1)}, u32[]{:S(2)}, u32[]{:S(2)}) collective-permute-start(bf16[48,1024]{1,0:T(8,128)(2,1)S(1)} %get-tuple-element.39), channel_id=1, source_target_pairs={{0,16},{4,20},{8,24},{12,28},{16,0},{20,4},{24,8},{28,12},{1,17},{... | collective-permute-start | bytes 294920 | tf_op jit(solution)/shard_map/ppermute | solution.py:432
  6.7 9.2 %collective-permute-start.1 = (bf16[48,1024]{1,0:T(8,128)(2,1)S(1)}, bf16[48,1024]{1,0:T(8,128)(2,1)S(1)}, u32[]{:S(2)}, u32[]{:S(2)}) collective-permute-start(bf16[48,1024]{1,0:T(8,128)(2,1)S(1)} %get-tuple-element.40), channel_id=1, source_target_pairs={{0,4},{4,8},{8,12},{12,16},{16,20},{20,24},{24,28},{28,0},{1,5},{5... | collective-permute-start | bytes 294920 | tf_op jit(solution)/shard_map/ppermute | solution.py:432
  8.2 11.5 %collective-permute-start.2 = (bf16[48,1024]{1,0:T(8,128)(2,1)S(1)}, bf16[48,1024]{1,0:T(8,128)(2,1)S(1)}, u32[]{:S(2)}, u32[]{:S(2)}) collective-permute-start(bf16[48,1024]{1,0:T(8,128)(2,1)S(1)} %get-tuple-element.41), channel_id=1, source_target_pairs={{0,28},{4,0},{8,4},{12,8},{16,12},{20,16},{24,20},{28,24},{1,29},{... | collective-permute-start | bytes 294920 | tf_op jit(solution)/shard_map/ppermute | solution.py:432
  11.4 10.1 %collective-permute-start.3 = (bf16[48,1024]{1,0:T(8,128)(2,1)S(1)}, bf16[48,1024]{1,0:T(8,128)(2,1)S(1)}, u32[]{:S(2)}, u32[]{:S(2)}) collective-permute-start(bf16[48,1024]{1,0:T(8,128)(2,1)S(1)} %get-tuple-element.49), channel_id=1, source_target_pairs={{0,12},{4,16},{8,20},{12,24},{16,28},{20,0},{24,4},{28,8},{1,13},{... | collective-permute-start | bytes 294920 | tf_op jit(solution)/shard_map/ppermute | solution.py:432
  11.5 10.1 %collective-permute-start.4 = (bf16[48,1024]{1,0:T(8,128)(2,1)S(1)}, bf16[48,1024]{1,0:T(8,128)(2,1)S(1)}, u32[]{:S(2)}, u32[]{:S(2)}) collective-permute-start(bf16[48,1024]{1,0:T(8,128)(2,1)S(1)} %get-tuple-element.50), channel_id=1, source_target_pairs={{0,20},{4,24},{8,28},{12,0},{16,4},{20,8},{24,12},{28,16},{1,21},{... | collective-permute-start | bytes 294920 | tf_op jit(solution)/shard_map/ppermute | solution.py:432
  15.3 4.4 %copy-start.1 = (bf16[1024,1024]{1,0:T(8,128)(2,1)S(1)}, bf16[1024,1024]{1,0:T(8,128)(2,1)}, u32[]{:S(2)}) copy-start(bf16[1024,1024]{1,0:T(8,128)(2,1)} %wk_ref.3) | copy-start | bytes 6291460
  15.3 4.4 %copy-start.2 = (bf16[1024,1024]{1,0:T(8,128)(2,1)S(1)}, bf16[1024,1024]{1,0:T(8,128)(2,1)}, u32[]{:S(2)}) copy-start(bf16[1024,1024]{1,0:T(8,128)(2,1)} %wv_ref.3) | copy-start | bytes 6291460
  15.8 6.5 %collective-permute-start.5 = (bf16[48,1024]{1,0:T(8,128)(2,1)S(1)}, bf16[48,1024]{1,0:T(8,128)(2,1)S(1)}, u32[]{:S(2)}, u32[]{:S(2)}) collective-permute-start(bf16[48,1024]{1,0:T(8,128)(2,1)S(1)} %get-tuple-element.51), channel_id=1, source_target_pairs={{0,8},{4,12},{8,16},{12,20},{16,24},{20,28},{24,0},{28,4},{1,9},{5... | collective-permute-start | bytes 294920 | tf_op jit(solution)/shard_map/ppermute | solution.py:432
  15.9 7.4 %collective-permute-start.6 = (bf16[48,1024]{1,0:T(8,128)(2,1)S(1)}, bf16[48,1024]{1,0:T(8,128)(2,1)S(1)}, u32[]{:S(2)}, u32[]{:S(2)}) collective-permute-start(bf16[48,1024]{1,0:T(8,128)(2,1)S(1)} %get-tuple-element.52), channel_id=1, source_target_pairs={{0,24},{4,28},{8,0},{12,4},{16,8},{20,12},{24,16},{28,20},{1,25},{... | collective-permute-start | bytes 294920 | tf_op jit(solution)/shard_map/ppermute | solution.py:432
  19.7 3.6 %copy-start.5 = (bf16[96,1024]{1,0:T(8,128)(2,1)S(1)}, bf16[96,1024]{1,0:T(8,128)(2,1)}, u32[]{:S(2)}) copy-start(bf16[96,1024]{1,0:T(8,128)(2,1)} %wout_ref.3) | copy-start | bytes 589828
  23.3 8.5 %copy-start.6 = (f32[96,128]{1,0:T(8,128)S(1)}, f32[96,128]{1,0:T(8,128)}, u32[]{:S(2)}) copy-start(f32[96,128]{1,0:T(8,128)} %truth_ref.1) | copy-start | bytes 147460
  23.3 8.5 %copy-start.10 = (f32[128]{0:T(128)S(1)}, f32[128]{0:T(128)}, u32[]{:S(2)}) copy-start(f32[128]{0:T(128)} %param.19) | copy-start | bytes 1540
  23.3 8.5 %copy-start.11 = (f32[96]{0:T(128)S(1)}, f32[96]{0:T(128)}, u32[]{:S(2)}) copy-start(f32[96]{0:T(128)} %param.20) | copy-start | bytes 1156
  25.8 4.7 %collective-permute-start.7 = (f32[2,96,128]{2,1,0:T(8,128)S(1)}, f32[2,96,128]{2,1,0:T(8,128)S(1)}, u32[]{:S(2)}, u32[]{:S(2)}) collective-permute-start(f32[2,96,128]{2,1,0:T(8,128)S(1)} %get-tuple-element.53.mine_ref), channel_id=1, source_target_pairs={{0,2},{1,3},{2,0},{3,1},{4,6},{5,7},{6,4},{7,5},{8,10},{9,11},{10,... | collective-permute-start | bytes 294920 | tf_op jit(solution)/shard_map/ppermute | solution.py:507
  27.4 3.1 %collective-permute-start.8 = (f32[2,96,128]{2,1,0:T(8,128)S(1)}, f32[2,96,128]{2,1,0:T(8,128)S(1)}, u32[]{:S(2)}, u32[]{:S(2)}) collective-permute-start(f32[2,96,128]{2,1,0:T(8,128)S(1)} %get-tuple-element.53.mine_ref), channel_id=1, source_target_pairs={{0,1},{1,0},{2,3},{3,2},{4,5},{5,4},{6,7},{7,6},{8,9},{9,8},{10,11... | collective-permute-start | bytes 294920 | tf_op jit(solution)/shard_map/ppermute | solution.py:507
  30.5 1.3 %collective-permute-start.9 = (f32[2,96,128]{2,1,0:T(8,128)S(1)}, f32[2,96,128]{2,1,0:T(8,128)S(1)}, u32[]{:S(2)}, u32[]{:S(2)}) collective-permute-start(f32[2,96,128]{2,1,0:T(8,128)S(1)} %collective-permute-done.7.refs_0_), channel_id=1, source_target_pairs={{0,1},{1,0},{2,3},{3,2},{4,5},{5,4},{6,7},{7,6},{8,9},{9,8},{10,11... | collective-permute-start | bytes 294920 | tf_op jit(solution)/shard_map/ppermute | solution.py:507
  35.1 14.1 %collective-permute-start.10 = (bf16[48,1024]{1,0:T(8,128)(2,1)S(1)}, bf16[48,1024]{1,0:T(8,128)(2,1)S(1)}, u32[]{:S(2)}, u32[]{:S(2)}) collective-permute-start(bf16[48,1024]{1,0:T(8,128)(2,1)S(1)} %get-tuple-element.57), channel_id=1, source_target_pairs={{0,16},{4,20},{8,24},{12,28},{16,0},{20,4},{24,8},{28,12},{1,17},{... | collective-permute-start | bytes 294920 | tf_op jit(solution)/shard_map/ppermute | solution.py:432
  39.1 10.0 %collective-permute-start.11 = (bf16[48,1024]{1,0:T(8,128)(2,1)S(1)}, bf16[48,1024]{1,0:T(8,128)(2,1)S(1)}, u32[]{:S(2)}, u32[]{:S(2)}) collective-permute-start(bf16[48,1024]{1,0:T(8,128)(2,1)S(1)} %get-tuple-element.58), channel_id=1, source_target_pairs={{0,20},{4,24},{8,28},{12,0},{16,4},{20,8},{24,12},{28,16},{1,21},{... | collective-permute-start | bytes 294920 | tf_op jit(solution)/shard_map/ppermute | solution.py:432
  39.9 12.7 %collective-permute-start.12 = (bf16[48,1024]{1,0:T(8,128)(2,1)S(1)}, bf16[48,1024]{1,0:T(8,128)(2,1)S(1)}, u32[]{:S(2)}, u32[]{:S(2)}) collective-permute-start(bf16[48,1024]{1,0:T(8,128)(2,1)S(1)} %get-tuple-element.59), channel_id=1, source_target_pairs={{0,12},{4,16},{8,20},{12,24},{16,28},{20,0},{24,4},{28,8},{1,13},{... | collective-permute-start | bytes 294920 | tf_op jit(solution)/shard_map/ppermute | solution.py:432
  43.6 9.6 %collective-permute-start.13 = (bf16[48,1024]{1,0:T(8,128)(2,1)S(1)}, bf16[48,1024]{1,0:T(8,128)(2,1)S(1)}, u32[]{:S(2)}, u32[]{:S(2)}) collective-permute-start(bf16[48,1024]{1,0:T(8,128)(2,1)S(1)} %get-tuple-element.63), channel_id=1, source_target_pairs={{0,28},{4,0},{8,4},{12,8},{16,12},{20,16},{24,20},{28,24},{1,29},{... | collective-permute-start | bytes 294920 | tf_op jit(solution)/shard_map/ppermute | solution.py:432
  45.9 11.1 %collective-permute-start.14 = (bf16[48,1024]{1,0:T(8,128)(2,1)S(1)}, bf16[48,1024]{1,0:T(8,128)(2,1)S(1)}, u32[]{:S(2)}, u32[]{:S(2)}) collective-permute-start(bf16[48,1024]{1,0:T(8,128)(2,1)S(1)} %get-tuple-element.64), channel_id=1, source_target_pairs={{0,24},{4,28},{8,0},{12,4},{16,8},{20,12},{24,16},{28,20},{1,25},{... | collective-permute-start | bytes 294920 | tf_op jit(solution)/shard_map/ppermute | solution.py:432
  49.1 7.9 %collective-permute-start.15 = (bf16[48,1024]{1,0:T(8,128)(2,1)S(1)}, bf16[48,1024]{1,0:T(8,128)(2,1)S(1)}, u32[]{:S(2)}, u32[]{:S(2)}) collective-permute-start(bf16[48,1024]{1,0:T(8,128)(2,1)S(1)} %get-tuple-element.65), channel_id=1, source_target_pairs={{0,8},{4,12},{8,16},{12,20},{16,24},{20,28},{24,0},{28,4},{1,9},{5... | collective-permute-start | bytes 294920 | tf_op jit(solution)/shard_map/ppermute | solution.py:432
  49.1 8.3 %collective-permute-start.16 = (bf16[48,1024]{1,0:T(8,128)(2,1)S(1)}, bf16[48,1024]{1,0:T(8,128)(2,1)S(1)}, u32[]{:S(2)}, u32[]{:S(2)}) collective-permute-start(bf16[48,1024]{1,0:T(8,128)(2,1)S(1)} %get-tuple-element.66), channel_id=1, source_target_pairs={{0,4},{4,8},{8,12},{12,16},{16,20},{20,24},{24,28},{28,0},{1,5},{5... | collective-permute-start | bytes 294920 | tf_op jit(solution)/shard_map/ppermute | solution.py:432

commit v5 on v4

--- a/solution.py
+++ b/solution.py
@@ -73,12 +73,6 @@
     return (rows == ids).astype(F32).astype(BF16)
 
 
-def of_chunks(block, chunks, capacity):
-    return jnp.concatenate(
-        [block[c * capacity : (c + 1) * capacity] for c in chunks], axis=0
-    )
-
-
 def ids_kernel(out_ref):
     out_ref[...] = lax.broadcasted_iota(jnp.int32, out_ref.shape, 0)
 
@@ -102,8 +96,9 @@
 
 
 def query_kernel(
-    order, capacity, head_size, feat_ref, w_ref, names_ref, live_ref, me_ref, out_ref, mult_ref
+    order, capacity, head_size, feat_ref, w_ref, names_ref, live_ref, me_ref, *out_refs
 ):
+    out_ref, turned_ref, mult_ref = out_refs
     points, width = feat_ref.shape
     slots = names_ref.shape[0]
     per = LANES // head_size
@@ -111,6 +106,12 @@
     head = lax.broadcasted_iota(jnp.int32, (points, width), 1) // head_size % per
     for p in range(per):
         out_ref[p * points : (p + 1) * points, :] = jnp.where(
+            head == p, query, jnp.zeros_like(query)
+        )
+    query = query.T
+    head = lax.broadcasted_iota(jnp.int32, (width, points), 0) // head_size % per
+    for p in range(per):
+        turned_ref[:, p * points : (p + 1) * points] = jnp.where(
             head == p, query, jnp.zeros_like(query)
         )
     place = lax.broadcasted_iota(jnp.int32, (capacity, points), 0)
@@ -123,11 +124,10 @@
     mult_ref[...] = mult
 
 
-def project(rows, wk_ref, wv_ref, k_scr, v_ref, offset, members, chunks, capacity):
-    width = wk_ref.shape[0]
+def project(rows, wk_ref, wv_ref, k_scr, v_ref, offset, members, chunks, capacity, tiles):
     tile = 2 * LANES
     rows_here = pl.ds(offset, chunks * capacity)
-    for t in range(width // tile):
+    for t in tiles:
         cols = slice(t * tile, (t + 1) * tile)
         keys = dot(rows, wk_ref[:, cols])
         values = dot(rows, wv_ref[:, cols])
@@ -138,11 +138,17 @@
             )
 
 
-def raised_scores(k_scr, qm_ref, m, j, factor, bias, mult):
+def raised_scores(k_scr, qmt_ref, j, factor, bias, mult):
+    members, rows = k_scr.shape[:2]
     cols = slice(j * LANES, (j + 1) * LANES)
-    raised = jnp.exp2(dot(k_scr[m, :, cols], qm_ref[:, cols], NT) * factor + bias)
-    raised = jnp.minimum(mult * raised, HUGE)
-    return raised, jnp.sum(raised, axis=0, keepdims=True)
+    keys = jnp.concatenate([k_scr[m, :, cols] for m in range(members)], axis=0)
+    scores = dot(keys, qmt_ref[cols, :])
+    both = []
+    for m in range(members):
+        raised = jnp.exp2(scores[m * rows : (m + 1) * rows] * factor + bias)
+        raised = jnp.minimum(mult * raised, HUGE)
+        both.append((raised, jnp.sum(raised, axis=0, keepdims=True)))
+    return both
 
 
 def exponent(head_size):
@@ -150,20 +156,21 @@
 
 
 def near_kernel(
-    members, chunks, capacity, head_size, before, qm_ref, wk_ref, wv_ref, mult_ref, *refs
+    members, chunks, capacity, head_size, before, qmt_ref, wk_ref, wv_ref, mult_ref, *refs
 ):
     raised_ref, total_ref, v_ref, k_scr = refs[chunks:]
     groups = wk_ref.shape[0] // LANES
     rows = jnp.concatenate([r[...] for r in refs[:chunks]], axis=0)
-    project(rows, wk_ref, wv_ref, k_scr, v_ref, 0, members, chunks, capacity)
+    tiles = range(wk_ref.shape[0] // (2 * LANES))
+    project(rows, wk_ref, wv_ref, k_scr, v_ref, 0, members, chunks, capacity, tiles)
     mult = mult_ref[before : before + k_scr.shape[1], :]
     mult = jnp.concatenate([mult] * (LANES // head_size), axis=1)
     bias = jnp.where(mult > 0.0, 0.0, -jnp.inf)
-    for m in range(members):
-        for j in range(groups):
-            raised_ref[m, j], total_ref[m, j] = raised_scores(
-                k_scr, qm_ref, m, j, exponent(head_size), bias, mult
-            )
+    for j in range(groups):
+        both = raised_scores(k_scr, qmt_ref, j, exponent(head_size), bias, mult)
+        for m, (raised, total) in enumerate(both):
+            raised_ref[m, j] = raised
+            total_ref[m, j] = total
 
 
 def forward_kernel(
@@ -171,7 +178,7 @@
     chunks,
     capacity,
     head_size,
-    qm_ref,
+    qmt_ref,
     wk_ref,
     wv_ref,
     wout_ref,
@@ -190,36 +197,41 @@
         v_ref[:, done : done + v_part.shape[1], :] = v_part[...]
         done += v_part.shape[1]
     rows = jnp.concatenate([r[...] for r in chunk_refs], axis=0)
-    project(rows, wk_ref, wv_ref, k_scr, v_ref, done, members, chunks, capacity)
+    work = (rows, wk_ref, wv_ref, k_scr, v_ref, done, members, chunks, capacity)
+    tiles = groups // 2
+    project(*work, [0])
     mult = jnp.concatenate([mult_ref[done:, :]] * per, axis=1)
     bias = jnp.where(mult > 0.0, 0.0, -jnp.inf)
-    steps = [(m, j) for m in range(members) for j in range(groups)]
-    ahead = raised_scores(k_scr, qm_ref, *steps[0], exponent(head_size), bias, mult)
-    for i, (m, j) in enumerate(steps):
-        late, late_total = ahead
-        raised = jnp.concatenate([r[m, j] for r in raised_refs] + [late], axis=0)
-        root = lax.rsqrt(sum([t[m, j] for t in total_refs], late_total))
-        if i + 1 < len(steps):
-            ahead = raised_scores(
-                k_scr, qm_ref, *steps[i + 1], exponent(head_size), bias, mult
-            )
-        weights = (raised * root * root).astype(BF16)
-        weight_ref[m, j] = weights
-        both = dot(v_ref[m, :, j * LANES : (j + 1) * LANES], weights, TN)
-        for p in range(per):
-            first = p * head_size
-            att_scr[pl.ds(j * LANES + first, head_size), :] = both[
-                first : first + head_size, p * points : (p + 1) * points
-            ].astype(BF16)
-        if j == groups - 1:
-            pred_ref[m] = dot(wout_ref[...], att_scr[...])
-
-
-def first_kernel(sizes, orders, qm_ref, wk_ref, wv_ref, mult_ref, send_ref, me_ref, *refs):
+    factor = exponent(head_size)
+    for t in range(tiles):
+        steps = [(m, j) for j in (2 * t, 2 * t + 1) for m in range(members)]
+        ahead = [
+            one
+            for j in (2 * t, 2 * t + 1)
+            for one in raised_scores(k_scr, qmt_ref, j, factor, bias, mult)
+        ]
+        if t + 1 < tiles:
+            project(*work, [t + 1])
+        for (m, j), (late, late_total) in zip(steps, ahead):
+            raised = jnp.concatenate([r[m, j] for r in raised_refs] + [late], axis=0)
+            root = lax.rsqrt(sum([s[m, j] for s in total_refs], late_total))
+            weights = (raised * root * root).astype(BF16)
+            weight_ref[m, j] = weights
+            both = dot(v_ref[m, :, j * LANES : (j + 1) * LANES], weights, TN)
+            for p in range(per):
+                first = p * head_size
+                att_scr[m, pl.ds(j * LANES + first, head_size), :] = both[
+                    first : first + head_size, p * points : (p + 1) * points
+                ].astype(BF16)
+    for m in range(members):
+        pred_ref[m] = dot(wout_ref[...], att_scr[m])
+
+
+def first_kernel(sizes, orders, qmt_ref, wk_ref, wv_ref, mult_ref, send_ref, me_ref, *refs):
     *refs, k_scr = refs
     last = len(refs) - 2 - len(orders)
     wkt_ref, wvt_ref, *place_refs = refs[last:]
-    near_kernel(*sizes, qm_ref, wk_ref, wv_ref, mult_ref, *refs[:last], k_scr)
+    near_kernel(*sizes, qmt_ref, wk_ref, wv_ref, mult_ref, *refs[:last], k_scr)
     wkt_ref[...] = wk_ref[...].T
     wvt_ref[...] = wv_ref[...].T
     one_hot_kernel(orders, send_ref, me_ref, *place_refs)
@@ -239,8 +251,7 @@
 
 def backward_kernel(
     members,
-    early,
-    late,
+    chunks,
     capacity,
     head_size,
     qm_ref,
@@ -255,9 +266,10 @@
     v_ref,
     *refs,
 ):
-    other_refs = refs[: len(refs) - len(early) - 5]
-    out_refs = refs[len(other_refs) : -5]
-    ds_ref, w_ref, da_ref, dk_scr, dv_scr = refs[-5:]
+    other_refs = refs[: len(refs) - chunks - 6]
+    out_refs = refs[len(other_refs) : -6]
+    ds_ref, da_ref, dk_scr, dv_scr, sum_scr, dat_scr = refs[-6:]
+    now = chunks * capacity
     width = wkt_ref.shape[1]
     points = truth_ref.shape[1]
     every_refs = (mine_ref, *other_refs)
@@ -270,7 +282,9 @@
     var = jnp.concatenate([var_ref[...], jnp.zeros((1, wide), F32)], axis=1)
     var = jnp.broadcast_to(var, (LANES, variables + wide)).T[:variables, :1]
     factor = area_ref[...] * var
-    head = lax.broadcasted_iota(jnp.int32, (points, width), 1) // head_size % per
+    head = lax.broadcasted_iota(jnp.int32, (points, 2 * LANES), 1) // head_size % per
+    turned = lax.broadcasted_iota(jnp.int32, (2 * LANES, points), 0) // head_size % per
+    dpreds = []
     for m in range(members):
         mine = mine_ref[m]
         miss = mine - truth_ref[...]
@@ -281,38 +295,65 @@
                 paired = mine - every_ref[f]
                 second = second + paired * lax.rsqrt(1.0 + paired * paired)
         dpred = (factor * (first - second / (total * (total - 1)))).astype(BF16)
-        d_attended = dot(dpred, wout_ref[...], TN).astype(BF16)
-        for p in range(per):
-            da_ref[m, p * points : (p + 1) * points, :] = jnp.where(
-                head == p, d_attended, jnp.zeros_like(d_attended)
-            )
+        dpreds.append(dpred)
+    tile = 2 * LANES
+    tiles = width // tile
+
+    def attended_grad(t):
+        cols = slice(t * tile, (t + 1) * tile)
+        for m in range(members):
+            grad = dot(dpreds[m], wout_ref[:, cols], TN).astype(BF16)
+            for p in range(per):
+                da_ref[m, p * points : (p + 1) * points, cols] = jnp.where(
+                    head == p, grad, jnp.zeros_like(grad)
+                )
+            grad = dot(wout_ref[:, cols], dpreds[m], TN).astype(BF16)
+            for p in range(per):
+                dat_scr[m, cols, p * points : (p + 1) * points] = jnp.where(
+                    turned == p, grad, jnp.zeros_like(grad)
+                )
 
     def probs_grad(m, j):
         cols = slice(j * LANES, (j + 1) * LANES)
-        return dot(v_ref[m, :, cols], da_ref[m, :, cols], NT)
-
-    steps = [(m, j) for j in range(groups) for m in range(members)]
-    ahead = probs_grad(*steps[0])
-    d_keys, d_values = [], []
-    for i, (m, j) in enumerate(steps):
-        cols = slice(j * LANES, (j + 1) * LANES)
-        d_probs = ahead
-        if i + 1 < len(steps):
-            ahead = probs_grad(*steps[i + 1])
-        weights = weight_ref[m, j].astype(F32)
-        inner = jnp.sum(weights * d_probs, axis=0, keepdims=True)
-        d_scores = weights * (d_probs - inner)
-        ds_ref[m, j] = of_chunks(d_scores, late, capacity).astype(BF16)
-        w_ref[m, j] = of_chunks(weights, late, capacity).astype(BF16)
-        now = of_chunks(d_scores, early, capacity).astype(BF16)
-        d_keys.append(dot(now, qm_ref[:, cols]) * scale)
-        now = of_chunks(weights, early, capacity).astype(BF16)
-        d_values.append(dot(now, da_ref[m, :, cols]))
-        if m == members - 1:
-            dk_scr[:, cols] = by_chunk(d_keys, range(len(early)), capacity).astype(BF16)
-            dv_scr[:, cols] = by_chunk(d_values, range(len(early)), capacity).astype(BF16)
-            d_keys, d_values = [], []
-    return_rows(dk_scr[...], dv_scr[...], wkt_ref, wvt_ref, out_refs)
+        return dot(v_ref[m, :, cols], dat_scr[m, cols, :])
+
+    attended_grad(0)
+    for t in range(tiles):
+        steps = [(j, m) for j in (2 * t, 2 * t + 1) for m in range(members)]
+        ahead = [probs_grad(m, j) for j, m in steps]
+        if t + 1 < tiles:
+            attended_grad(t + 1)
+        if t > 0:
+            before = slice((t - 1) * tile, t * tile)
+            more = dot(dk_scr[:, before], wkt_ref[before, :])
+            more = more + dot(dv_scr[:, before], wvt_ref[before, :])
+            sum_scr[...] = more if t == 1 else sum_scr[...] + more
+        d_keys, d_values = [], []
+        for (j, m), d_probs in zip(steps, ahead):
+            cols = slice(j * LANES, (j + 1) * LANES)
+            weights = weight_ref[m, j].astype(F32)
+            inner = jnp.sum(weights * d_probs, axis=0, keepdims=True)
+            d_scores = (weights * (d_probs - inner)).astype(BF16)
+            ds_ref[m, j] = d_scores[now:]
+            d_keys.append(d_scores[:now])
+            d_values.append(dot(weight_ref[m, j, :now, :], da_ref[m, :, cols]))
+            if m == members - 1:
+                both = dot(jnp.concatenate(d_keys, axis=0), qm_ref[:, cols]) * scale
+                d_keys = [both[i * now : (i + 1) * now] for i in range(members)]
+                dk_scr[:, cols] = by_chunk(d_keys, range(chunks), capacity).astype(BF16)
+                dv_scr[:, cols] = by_chunk(d_values, range(chunks), capacity).astype(BF16)
+                d_keys, d_values = [], []
+    last = slice((tiles - 1) * tile, width)
+    step = out_refs[0].shape[0]
+    for t in range(tiles):
+        cols = slice(t * tile, (t + 1) * tile)
+        rows = dot(dk_scr[:, last], wkt_ref[last, cols])
+        rows = rows + dot(dv_scr[:, last], wvt_ref[last, cols])
+        if tiles > 1:
+            rows = rows + sum_scr[:, cols]
+        rows = rows.astype(BF16)
+        for c, out_ref in enumerate(out_refs):
+            out_ref[:, cols] = rows[c * step : (c + 1) * step]
 
 
 def late_rows_kernel(
@@ -320,12 +361,15 @@
 ):
     out_refs = refs[:chunks]
     dk_scr, dv_scr = refs[chunks:]
-    members, groups = ds_ref.shape[:2]
+    members, groups, rows = ds_ref.shape[:3]
+    done = w_ref.shape[2] - rows
     scale = head_size ** (-0.5)
     for j in range(groups):
         cols = slice(j * LANES, (j + 1) * LANES)
-        d_keys = [dot(ds_ref[m, j], qm_ref[:, cols]) * scale for m in range(members)]
-        d_values = [dot(w_ref[m, j], da_ref[m, :, cols]) for m in range(members)]
+        both = jnp.concatenate([ds_ref[m, j] for m in range(members)], axis=0)
+        both = dot(both, qm_ref[:, cols]) * scale
+        d_keys = [both[m * rows : (m + 1) * rows] for m in range(members)]
+        d_values = [dot(w_ref[m, j, done:, :], da_ref[m, :, cols]) for m in range(members)]
         dk_scr[:, cols] = by_chunk(d_keys, range(chunks), capacity).astype(BF16)
         dv_scr[:, cols] = by_chunk(d_values, range(chunks), capacity).astype(BF16)
     return_rows(dk_scr[...], dv_scr[...], wkt_ref, wvt_ref, out_refs)
@@ -420,9 +464,7 @@
     me = lax.axis_index("grid")
     half = chunks // 2
     order = shifts_from(chunks, (half, 1, -1, half - 1, half + 1, 2, -2))
-    groups_in = [order[:half], order[half:]]
-    leave = shifts_from(chunks, (half, half - 1, half + 1, 1, 2, -2, -1))
-    early, late = leave[:half], leave[half:]
+    early, late = order[:half], order[half:]
     here = me[None]
 
     def exchanged(blocks, shifts, sign):
@@ -444,7 +486,6 @@
         functools.partial(pick_kernel, order),
         jax.ShapeDtypeStruct((own_rows, received), BF16),
         [send_rows, here, ids],
-        flops=members * received * own_rows * width,
         scalars=(1,),
     )
     outgoing = call(
@@ -455,12 +496,13 @@
         limit=40 * 1024 * 1024,
     )
     arrived_first, arrived_last = [
-        exchanged([outgoing[order.index(s)] for s in group], group, 1) for group in groups_in
+        exchanged([outgoing[order.index(s)] for s in group], group, 1) for group in (early, late)
     ]
-    query, mult = call(
+    query, query_t, mult = call(
         functools.partial(query_kernel, order, capacity, head_size),
         [
             jax.ShapeDtypeStruct((per * points, width), BF16),
+            jax.ShapeDtypeStruct((width, per * points), BF16),
             jax.ShapeDtypeStruct((received, points), F32),
         ],
         [grid_feat, w_query, neighbours.T, live_count[None, :], here],
@@ -480,7 +522,7 @@
         ]
         + [jax.ShapeDtypeStruct((width, width), BF16)] * 2
         + [jax.ShapeDtypeStruct((own_rows, len(s) * capacity), BF16) for s in (early, late)],
-        [query, w_key, w_value, mult, send_rows, here, *arrived_first],
+        [query_t, w_key, w_value, mult, send_rows, here, *arrived_first],
         scratch=[pltpu.VMEM((members, before, width), BF16)],
         flops=4 * members * before * width * width,
         scalars=(5,),
@@ -493,10 +535,10 @@
             jax.ShapeDtypeStruct((members, groups, received, per * points), BF16),
             jax.ShapeDtypeStruct((members, received, width), BF16),
         ],
-        [query, w_key, w_value, w_out, mult, *parts, *arrived_last],
+        [query_t, w_key, w_value, w_out, mult, *parts, *arrived_last],
         scratch=[
             pltpu.VMEM((members, rows_here, width), BF16),
-            pltpu.VMEM((width, points), BF16),
+            pltpu.VMEM((members, width, points), BF16),
         ],
         flops=4 * members * rows_here * width * width,
     )
@@ -509,18 +551,10 @@
     late_grad = jax.ShapeDtypeStruct(
         (members, groups, len(late) * capacity, per * points), BF16
     )
-    *leaving_early, d_scores, late_weights, d_attended = call(
-        functools.partial(
-            backward_kernel,
-            members,
-            [order.index(c) for c in early],
-            [order.index(c) for c in late],
-            capacity,
-            head_size,
-        ),
+    *leaving_early, d_scores, d_attended = call(
+        functools.partial(backward_kernel, members, len(early), capacity, head_size),
         [chunk_shape] * len(early)
-        + [late_grad] * 2
-        + [jax.ShapeDtypeStruct((members, per * points, width), BF16)],
+        + [late_grad, jax.ShapeDtypeStruct((members, per * points, width), BF16)],
         [
             query,
             w_key_t,
@@ -534,14 +568,18 @@
             values,
             *everyone[1:],
         ],
-        scratch=[pltpu.VMEM((len(early) * step, width), BF16)] * 2,
+        scratch=[pltpu.VMEM((len(early) * step, width), BF16)] * 2
+        + [
+            pltpu.VMEM((len(early) * step, width), F32),
+            pltpu.VMEM((members, width, per * points), BF16),
+        ],
         flops=4 * members * received * width * width,
     )
     returned_early = exchanged(leaving_early, early, -1)
     leaving_late = call(
         functools.partial(late_rows_kernel, len(late), capacity, head_size),
         [chunk_shape] * len(late),
-        [query, w_key_t, w_value_t, d_scores, late_weights, d_attended],
+        [query, w_key_t, w_value_t, d_scores, weights, d_attended],
         scratch=[pltpu.VMEM((len(late) * step, width), BF16)] * 2,
         flops=4 * len(late) * step * width * width,
     )

time: 59.3 us -> 56.6 us (0.954)
  starting transfers between devices: 31.8 us -> 30 us
  local copies, waits for them, and re-layouts: 1.89 us -> 1.22 us
    ppermute x14, starting transfers between devices: 30.2 us -> 28.5 us  [exchanged(): lax.ppermute(b, 'grid', [(i, (i + sign * s) % chunks) for i in range(chun...]
    unnamed x24, local copies, waits for them, and re-layouts: 1.89 us -> 1.22 us
  transfers between devices with their start and end apart: 17 -> 17, of which waited for: 7 -> 8; matrix products, arithmetic and copies ran while one was open for 0% -> 0% of each run, Pallas kernels for 7% -> 7%
where the time goes in v5:
time: 56.6 us; the launch traced here: 56.4 us
  starting transfers between devices  30 us (53%)
  waiting for transfers between devices  12.8 us (23%)
  Pallas kernels  12.2 us (22%)
  local copies, waits for them, and re-layouts  1.22 us (2%)
    ppermute x14, starting transfers between devices, exchanged(): lax.ppermute(b, 'grid', [(i, (i + sign * s) % chunks) for i in range(chun...  28.5 us
    pallas_call x9, Pallas kernels, call(): pl.pallas_call(kernel, out_shape=out_shape, in_specs=[SMEM if i in scalar...  10.4 us
    ppermute x14, waiting for transfers between devices, exchanged(): lax.ppermute(b, 'grid', [(i, (i + sign * s) % chunks) for i in range(chun...  8.43 us
    ppermute x3, waiting for transfers between devices, on_device(): everyone += [lax.ppermute(p, 'member', pairs) for p in everyone]  4.42 us
    pallas_call x1, Pallas kernels, last_sum(): pl.pallas_call(functools.partial(last_sum_kernel, members, capacity), out...  1.75 us
    ppermute x3, starting transfers between devices, on_device(): everyone += [lax.ppermute(p, 'member', pairs) for p in everyone]  1.56 us
    unnamed x24, local copies, waits for them, and re-layouts  1.22 us
  transfers between devices with their start and end apart: 17, of which 8 were waited for; matrix products, arithmetic and copies ran while one was open for 0% of the time, Pallas kernels for 7%

profile of v5, /device:TPU:0, one launch (start us, length us, event | category | flops | bytes accessed | tf_op | source)
XLA Modules:
  0.0 56.4 jit_solution(12007551164285278169)
XLA Ops:
  0.0 0.7 %copy-done = s32[1,8,24]{2,1,0:T(8,128)S(1)} copy-done((s32[1,8,24]{2,1,0:T(8,128)S(1)}, s32[1,8,24]{2,1,0:T(8,128)}, u32[]{:S(2)}) %copy-start) | copy-done | bytes 792
  0.7 0.1 shard_map.120.pick_ref
  0.8 0.5 copy-done.4
  1.3 0.6 %shard_map.121 = (bf16[48,1024]{1,0:T(8,128)(2,1)S(1)}, bf16[48,1024]{1,0:T(8,128)(2,1)S(1)}, bf16[48,1024]{1,0:T(8,128)(2,1)S(1)}, bf16[48,1024]{1,0:T(8,128)(2...) custom-call(bf16[2,320,1024]{2,1,0:T(8,128)(2,1)S(1)} %copy-done.4, ...), custom_call_target="tpu_custom_call" | custom-call | flops 10066329600 | bytes 2220032 | tf_op jit(solution)/shard_map/pallas_call | solution.py:35
  2.0 4.1 %collective-permute-start = (bf16[48,1024]{1,0:T(8,128)(2,1)S(1)}, bf16[48,1024]{1,0:T(8,128)(2,1)S(1)}, u32[]{:S(2)}, u32[]{:S(2)}) collective-permute-start(bf16[48,1024]{1,0:T(8,128)(2,1)S(1)} %get-tuple-element.39), channel_id=1, source_target_pairs={{0,16},{4,20},{8,24},{12,28},{16,0},{20,4},{24,8},{28,12},{1,17},{... | collective-permute-start | bytes 294920 | tf_op jit(solution)/shard_map/ppermute | solution.py:474
  6.0 1.5 %collective-permute-start.1 = (bf16[48,1024]{1,0:T(8,128)(2,1)S(1)}, bf16[48,1024]{1,0:T(8,128)(2,1)S(1)}, u32[]{:S(2)}, u32[]{:S(2)}) collective-permute-start(bf16[48,1024]{1,0:T(8,128)(2,1)S(1)} %get-tuple-element.40), channel_id=1, source_target_pairs={{0,4},{4,8},{8,12},{12,16},{16,20},{20,24},{24,28},{28,0},{1,5},{5... | collective-permute-start | bytes 294920 | tf_op jit(solution)/shard_map/ppermute | solution.py:474
  7.6 3.2 %collective-permute-start.2 = (bf16[48,1024]{1,0:T(8,128)(2,1)S(1)}, bf16[48,1024]{1,0:T(8,128)(2,1)S(1)}, u32[]{:S(2)}, u32[]{:S(2)}) collective-permute-start(bf16[48,1024]{1,0:T(8,128)(2,1)S(1)} %get-tuple-element.41), channel_id=1, source_target_pairs={{0,28},{4,0},{8,4},{12,8},{16,12},{20,16},{24,20},{28,24},{1,29},{... | collective-permute-start | bytes 294920 | tf_op jit(solution)/shard_map/ppermute | solution.py:474
  10.8 3.8 %collective-permute-start.4 = (bf16[48,1024]{1,0:T(8,128)(2,1)S(1)}, bf16[48,1024]{1,0:T(8,128)(2,1)S(1)}, u32[]{:S(2)}, u32[]{:S(2)}) collective-permute-start(bf16[48,1024]{1,0:T(8,128)(2,1)S(1)} %get-tuple-element.51), channel_id=1, source_target_pairs={{0,20},{4,24},{8,28},{12,0},{16,4},{20,8},{24,12},{28,16},{1,21},{... | collective-permute-start | bytes 294920 | tf_op jit(solution)/shard_map/ppermute | solution.py:474
  14.6 0.6 %shard_map.118 = (bf16[256,1024]{1,0:T(8,128)(2,1)S(1)}, bf16[1024,256]{1,0:T(8,128)(2,1)S(1)}, f32[192,128]{1,0:T(8,128)S(1)}) custom-call(bf16[128,1024]{1,0:T(8,128)(2,1)S(1)} %copy-done.5, bf16[1024,1024]{1,0:T(8,128)(2,1)S(1)} %copy-done.1, s32[16,128]{1,0:T(8,128)S(1)} %bitcast.5, s32[1,128]{1,0:T(1,128)S(1)} %bitcast.6, s32[1]{0:T(128)} %bitcast.2.me_ref), custom_call_target="tpu_custom_call" | custom-call | flops 10737418240 | bytes 3514884 | tf_op jit(solution)/shard_map/pallas_call | solution.py:35
  15.2 0.1 collective-permute-start.5
  15.3 3.8 %collective-permute-start.6 = (bf16[48,1024]{1,0:T(8,128)(2,1)S(1)}, bf16[48,1024]{1,0:T(8,128)(2,1)S(1)}, u32[]{:S(2)}, u32[]{:S(2)}) collective-permute-start(bf16[48,1024]{1,0:T(8,128)(2,1)S(1)} %get-tuple-element.53), channel_id=1, source_target_pairs={{0,24},{4,28},{8,0},{12,4},{16,8},{20,12},{24,16},{28,20},{1,25},{... | collective-permute-start | bytes 294920 | tf_op jit(solution)/shard_map/ppermute | solution.py:474
  19.1 1.7 %shard_map.122 = (f32[2,8,96,256]{3,2,1,0:T(8,128)S(1)}, f32[2,8,1,256]{3,2,1,0:T(1,128)S(1)}, bf16[2,96,1024]{2,1,0:T(8,128)(2,1)S(1)}, bf16[1024,1024]{1,0:T(8...) custom-call(bf16[1024,256]{1,0:T(8,128)(2,1)S(1)} %get-tuple-element.36.qmt, ...), custom_call_target="tpu_custom_call" | custom-call | flops 32212254720 | bytes 11510532 | tf_op jit(solution)/shard_map/pallas_call | solution.py:35
  20.9 0.9 %collective-permute-done.5.refs_5_ = bf16[48,1024]{1,0:T(8,128)(2,1)S(1)} collective-permute-done((bf16[48,1024]{1,0:T(8,128)(2,1)S(1)}, bf16[48,1024]{1,0:T(8,128)(2,1)S(1)}, u32[]{:S(2)}, u32[]{:S(2)}) %collective-permute-start.5) | collective-permute-done | bytes 98336 | tf_op jit(solution)/shard_map/ppermute | solution.py:474
  21.8 0.9 %collective-permute-done.6.refs_6_ = bf16[48,1024]{1,0:T(8,128)(2,1)S(1)} collective-permute-done((bf16[48,1024]{1,0:T(8,128)(2,1)S(1)}, bf16[48,1024]{1,0:T(8,128)(2,1)S(1)}, u32[]{:S(2)}, u32[]{:S(2)}) %collective-permute-start.6) | collective-permute-done | bytes 98336 | tf_op jit(solution)/shard_map/ppermute | solution.py:474
  22.7 2.4 %shard_map.123 = (f32[2,96,128]{2,1,0:T(8,128)S(1)}, bf16[2,8,192,256]{3,2,1,0:T(8,128)(2,1)S(1)}, bf16[2,192,1024]{2,1,0:T(8,128)(2,1)S(1)}) custom-call(bf16[1024,256]{1,0:T(8,128)(2,1)S(1)} %get-tuple-element.36.qmt_ref, bf16[1024,1024]{1,0:T(8,128)(2,1)S(1)} %copy-done.2, bf16[1024,1024]{1,0:T(8,128)(2,1)S(1)} %copy-done.3, ...), custom_call_target="tpu_custom_call" | custom-call | flops 32212254720 | bytes 9846784 | tf_op jit(solution)/shard_map/pallas_call | solution.py:35
  25.1 1.6 %collective-permute-start.7 = (f32[2,96,128]{2,1,0:T(8,128)S(1)}, f32[2,96,128]{2,1,0:T(8,128)S(1)}, u32[]{:S(2)}, u32[]{:S(2)}) collective-permute-start(f32[2,96,128]{2,1,0:T(8,128)S(1)} %get-tuple-element.54.mine_ref), channel_id=1, source_target_pairs={{0,2},{1,3},{2,0},{3,1},{4,6},{5,7},{6,4},{7,5},{8,10},{9,11},{10,... | collective-permute-start | bytes 294920 | tf_op jit(solution)/shard_map/ppermute | solution.py:549
  26.7 3.1 %collective-permute-done.7.refs_0_ = f32[2,96,128]{2,1,0:T(8,128)S(1)} collective-permute-done((f32[2,96,128]{2,1,0:T(8,128)S(1)}, f32[2,96,128]{2,1,0:T(8,128)S(1)}, u32[]{:S(2)}, u32[]{:S(2)}) %collective-permute-start.7) | collective-permute-done | bytes 98336 | tf_op jit(solution)/shard_map/ppermute | solution.py:549
  29.8 1.3 %collective-permute-done.9.refs_2_ = f32[2,96,128]{2,1,0:T(8,128)S(1)} collective-permute-done((f32[2,96,128]{2,1,0:T(8,128)S(1)}, f32[2,96,128]{2,1,0:T(8,128)S(1)}, u32[]{:S(2)}, u32[]{:S(2)}) %collective-permute-start.9) | collective-permute-done | bytes 98336 | tf_op jit(solution)/shard_map/ppermute | solution.py:549
  31.1 3.1 %shard_map.124 = (bf16[48,1024]{1,0:T(8,128)(2,1)S(1)}, bf16[48,1024]{1,0:T(8,128)(2,1)S(1)}, bf16[48,1024]{1,0:T(8,128)(2,1)S(1)}, bf16[48,1024]{1,0:T(8,128)(2...) custom-call(bf16[256,1024]{1,0:T(8,128)(2,1)S(1)} %get-tuple-element.44.qm_ref, ...), custom_call_target="tpu_custom_call" | custom-call | flops 64424509440 | bytes 9945984 | tf_op jit(solution)/shard_map/pallas_call | solution.py:35
  34.2 4.0 %collective-permute-start.10 = (bf16[48,1024]{1,0:T(8,128)(2,1)S(1)}, bf16[48,1024]{1,0:T(8,128)(2,1)S(1)}, u32[]{:S(2)}, u32[]{:S(2)}) collective-permute-start(bf16[48,1024]{1,0:T(8,128)(2,1)S(1)} %get-tuple-element.58), channel_id=1, source_target_pairs={{0,16},{4,20},{8,24},{12,28},{16,0},{20,4},{24,8},{28,12},{1,17},{... | collective-permute-start | bytes 294920 | tf_op jit(solution)/shard_map/ppermute | solution.py:474
  38.2 1.4 %collective-permute-start.11 = (bf16[48,1024]{1,0:T(8,128)(2,1)S(1)}, bf16[48,1024]{1,0:T(8,128)(2,1)S(1)}, u32[]{:S(2)}, u32[]{:S(2)}) collective-permute-start(bf16[48,1024]{1,0:T(8,128)(2,1)S(1)} %get-tuple-element.59), channel_id=1, source_target_pairs={{0,28},{4,0},{8,4},{12,8},{16,12},{20,16},{24,20},{28,24},{1,29},{... | collective-permute-start | bytes 294920 | tf_op jit(solution)/shard_map/ppermute | solution.py:474
  39.5 0.7 %collective-permute-start.12 = (bf16[48,1024]{1,0:T(8,128)(2,1)S(1)}, bf16[48,1024]{1,0:T(8,128)(2,1)S(1)}, u32[]{:S(2)}, u32[]{:S(2)}) collective-permute-start(bf16[48,1024]{1,0:T(8,128)(2,1)S(1)} %get-tuple-element.60), channel_id=1, source_target_pairs={{0,4},{4,8},{8,12},{12,16},{16,20},{20,24},{24,28},{28,0},{1,5},{5... | collective-permute-start | bytes 294920 | tf_op jit(solution)/shard_map/ppermute | solution.py:474
  40.2 1.4 %shard_map.126 = (bf16[48,1024]{1,0:T(8,128)(2,1)S(1)}, bf16[48,1024]{1,0:T(8,128)(2,1)S(1)}, bf16[48,1024]{1,0:T(8,128)(2,1)S(1)}, bf16[48,1024]{1,0:T(8,128)(2,1)S(1)}) custom-call(bf16[256,1024]{1,0:T(8,128)(2,1)S(1)} %get-tuple-element.44.qm_ref, bf16[1024,1024]{1,0:T(8,128)(2,1)S(1)} %get-tuple-element.45.wkt_ref, ...), custom_call_target="tpu_custom_call" | custom-call | flops 32212254720 | bytes 8519680 | tf_op jit(solution)/shard_map/pallas_call | solution.py:35
  41.7 1.7 %collective-permute-start.13 = (bf16[48,1024]{1,0:T(8,128)(2,1)S(1)}, bf16[48,1024]{1,0:T(8,128)(2,1)S(1)}, u32[]{:S(2)}, u32[]{:S(2)}) collective-permute-start(bf16[48,1024]{1,0:T(8,128)(2,1)S(1)} %get-tuple-element.63), channel_id=1, source_target_pairs={{0,20},{4,24},{8,28},{12,0},{16,4},{20,8},{24,12},{28,16},{1,21},{... | collective-permute-start | bytes 294920 | tf_op jit(solution)/shard_map/ppermute | solution.py:474
  43.4 1.2 %collective-permute-start.14 = (bf16[48,1024]{1,0:T(8,128)(2,1)S(1)}, bf16[48,1024]{1,0:T(8,128)(2,1)S(1)}, u32[]{:S(2)}, u32[]{:S(2)}) collective-permute-start(bf16[48,1024]{1,0:T(8,128)(2,1)S(1)} %get-tuple-element.64), channel_id=1, source_target_pairs={{0,12},{4,16},{8,20},{12,24},{16,28},{20,0},{24,4},{28,8},{1,13},{... | collective-permute-start | bytes 294920 | tf_op jit(solution)/shard_map/ppermute | solution.py:474
  44.6 3.0 %collective-permute-start.15 = (bf16[48,1024]{1,0:T(8,128)(2,1)S(1)}, bf16[48,1024]{1,0:T(8,128)(2,1)S(1)}, u32[]{:S(2)}, u32[]{:S(2)}) collective-permute-start(bf16[48,1024]{1,0:T(8,128)(2,1)S(1)} %get-tuple-element.65), channel_id=1, source_target_pairs={{0,24},{4,28},{8,0},{12,4},{16,8},{20,12},{24,16},{28,20},{1,25},{... | collective-permute-start | bytes 294920 | tf_op jit(solution)/shard_map/ppermute | solution.py:474
  47.6 0.2 collective-permute-done.12.refs_3_
  47.8 0.5 shard_map.125.before_ref
  48.3 1.3 %collective-permute-done.13.refs_0_ = bf16[48,1024]{1,0:T(8,128)(2,1)S(1)} collective-permute-done((bf16[48,1024]{1,0:T(8,128)(2,1)S(1)}, bf16[48,1024]{1,0:T(8,128)(2,1)S(1)}, u32[]{:S(2)}, u32[]{:S(2)}) %collective-permute-start.13) | collective-permute-done | bytes 98336 | tf_op jit(solution)/shard_map/ppermute | solution.py:474
  49.6 4.8 %collective-permute-done.14.refs_1_ = bf16[48,1024]{1,0:T(8,128)(2,1)S(1)} collective-permute-done((bf16[48,1024]{1,0:T(8,128)(2,1)S(1)}, bf16[48,1024]{1,0:T(8,128)(2,1)S(1)}, u32[]{:S(2)}, u32[]{:S(2)}) %collective-permute-start.14) | collective-permute-done | bytes 98336 | tf_op jit(solution)/shard_map/ppermute | solution.py:474
  54.4 0.3 collective-permute-done.15.refs_2_
  54.7 1.7 %shard_map.127 = f32[2,320,1024]{2,1,0:T(8,128)} custom-call(bf16[320,96]{1,0:T(8,128)(2,1)S(1)} %get-tuple-element.42.place_ref, f32[2,320,1024]{2,1,0:T(8,128)S(1)} %shard_map.125.before_ref, bf16[48,1024]{1,0:T(8,128)(2,1)S(1)} %collective-permute-done.13.refs_0_, bf16[48,1024]{1,0:T(8,128)(2,1)S(1)} %collective-permute-done.14.refs_1_, ...), custom_call_target="tpu_custom_call" | custom-call | flops 125829120 | bytes 5636096 | tf_op jit(solution)/shard_map/pallas_call | solution.py:417
  (36 shorter events, 0.1 us)
Async XLA Ops:
  0.0 0.7 %copy-start = (s32[1,8,24]{2,1,0:T(8,128)S(1)}, s32[1,8,24]{2,1,0:T(8,128)}, u32[]{:S(2)}) copy-start(s32[1,8,24]{2,1,0:T(8,128)} %send_ref.3) | copy-start | bytes 2308
  0.0 1.3 %copy-start.4 = (bf16[2,320,1024]{2,1,0:T(8,128)(2,1)S(1)}, bf16[2,320,1024]{2,1,0:T(8,128)(2,1)}, u32[]{:S(2)}) copy-start(bf16[2,320,1024]{2,1,0:T(8,128)(2,1)} %latent_ref.1) | copy-start | bytes 3932164
  1.3 13.3 %copy-start.1 = (bf16[1024,1024]{1,0:T(8,128)(2,1)S(1)}, bf16[1024,1024]{1,0:T(8,128)(2,1)}, u32[]{:S(2)}) copy-start(bf16[1024,1024]{1,0:T(8,128)(2,1)} %w_ref.1) | copy-start | bytes 6291460
  1.3 13.3 %copy-start.5 = (bf16[128,1024]{1,0:T(8,128)(2,1)S(1)}, bf16[128,1024]{1,0:T(8,128)(2,1)}, u32[]{:S(2)}) copy-start(bf16[128,1024]{1,0:T(8,128)(2,1)} %feat_ref.1) | copy-start | bytes 786436
  1.3 13.3 %copy-start.8 = (s32[128,16]{0,1:T(8,128)S(1)}, s32[128,16]{0,1:T(8,128)}, u32[]{:S(2)}) copy-start(s32[128,16]{0,1:T(8,128)} %param.22) | copy-start | bytes 24580
  1.3 13.3 %copy-start.9 = (s32[128]{0:T(128)S(1)}, s32[128]{0:T(128)}, u32[]{:S(2)}) copy-start(s32[128]{0:T(128)} %param.23) | copy-start | bytes 1540
  2.0 13.3 %collective-permute-start = (bf16[48,1024]{1,0:T(8,128)(2,1)S(1)}, bf16[48,1024]{1,0:T(8,128)(2,1)S(1)}, u32[]{:S(2)}, u32[]{:S(2)}) collective-permute-start(bf16[48,1024]{1,0:T(8,128)(2,1)S(1)} %get-tuple-element.39), channel_id=1, source_target_pairs={{0,16},{4,20},{8,24},{12,28},{16,0},{20,4},{24,8},{28,12},{1,17},{... | collective-permute-start | bytes 294920 | tf_op jit(solution)/shard_map/ppermute | solution.py:474
  6.0 9.3 %collective-permute-start.1 = (bf16[48,1024]{1,0:T(8,128)(2,1)S(1)}, bf16[48,1024]{1,0:T(8,128)(2,1)S(1)}, u32[]{:S(2)}, u32[]{:S(2)}) collective-permute-start(bf16[48,1024]{1,0:T(8,128)(2,1)S(1)} %get-tuple-element.40), channel_id=1, source_target_pairs={{0,4},{4,8},{8,12},{12,16},{16,20},{20,24},{24,28},{28,0},{1,5},{5... | collective-permute-start | bytes 294920 | tf_op jit(solution)/shard_map/ppermute | solution.py:474
  7.6 11.6 %collective-permute-start.2 = (bf16[48,1024]{1,0:T(8,128)(2,1)S(1)}, bf16[48,1024]{1,0:T(8,128)(2,1)S(1)}, u32[]{:S(2)}, u32[]{:S(2)}) collective-permute-start(bf16[48,1024]{1,0:T(8,128)(2,1)S(1)} %get-tuple-element.41), channel_id=1, source_target_pairs={{0,28},{4,0},{8,4},{12,8},{16,12},{20,16},{24,20},{28,24},{1,29},{... | collective-permute-start | bytes 294920 | tf_op jit(solution)/shard_map/ppermute | solution.py:474
  10.8 10.1 %collective-permute-start.3 = (bf16[48,1024]{1,0:T(8,128)(2,1)S(1)}, bf16[48,1024]{1,0:T(8,128)(2,1)S(1)}, u32[]{:S(2)}, u32[]{:S(2)}) collective-permute-start(bf16[48,1024]{1,0:T(8,128)(2,1)S(1)} %get-tuple-element.50), channel_id=1, source_target_pairs={{0,12},{4,16},{8,20},{12,24},{16,28},{20,0},{24,4},{28,8},{1,13},{... | collective-permute-start | bytes 294920 | tf_op jit(solution)/shard_map/ppermute | solution.py:474
  10.8 10.1 %collective-permute-start.4 = (bf16[48,1024]{1,0:T(8,128)(2,1)S(1)}, bf16[48,1024]{1,0:T(8,128)(2,1)S(1)}, u32[]{:S(2)}, u32[]{:S(2)}) collective-permute-start(bf16[48,1024]{1,0:T(8,128)(2,1)S(1)} %get-tuple-element.51), channel_id=1, source_target_pairs={{0,20},{4,24},{8,28},{12,0},{16,4},{20,8},{24,12},{28,16},{1,21},{... | collective-permute-start | bytes 294920 | tf_op jit(solution)/shard_map/ppermute | solution.py:474
  14.6 4.5 %copy-start.2 = (bf16[1024,1024]{1,0:T(8,128)(2,1)S(1)}, bf16[1024,1024]{1,0:T(8,128)(2,1)}, u32[]{:S(2)}) copy-start(bf16[1024,1024]{1,0:T(8,128)(2,1)} %wk_ref.3) | copy-start | bytes 6291460
  14.6 4.5 %copy-start.3 = (bf16[1024,1024]{1,0:T(8,128)(2,1)S(1)}, bf16[1024,1024]{1,0:T(8,128)(2,1)}, u32[]{:S(2)}) copy-start(bf16[1024,1024]{1,0:T(8,128)(2,1)} %wv_ref.3) | copy-start | bytes 6291460
  15.2 6.5 %collective-permute-start.5 = (bf16[48,1024]{1,0:T(8,128)(2,1)S(1)}, bf16[48,1024]{1,0:T(8,128)(2,1)S(1)}, u32[]{:S(2)}, u32[]{:S(2)}) collective-permute-start(bf16[48,1024]{1,0:T(8,128)(2,1)S(1)} %get-tuple-element.52), channel_id=1, source_target_pairs={{0,8},{4,12},{8,16},{12,20},{16,24},{20,28},{24,0},{28,4},{1,9},{5... | collective-permute-start | bytes 294920 | tf_op jit(solution)/shard_map/ppermute | solution.py:474
  15.3 7.4 %collective-permute-start.6 = (bf16[48,1024]{1,0:T(8,128)(2,1)S(1)}, bf16[48,1024]{1,0:T(8,128)(2,1)S(1)}, u32[]{:S(2)}, u32[]{:S(2)}) collective-permute-start(bf16[48,1024]{1,0:T(8,128)(2,1)S(1)} %get-tuple-element.53), channel_id=1, source_target_pairs={{0,24},{4,28},{8,0},{12,4},{16,8},{20,12},{24,16},{28,20},{1,25},{... | collective-permute-start | bytes 294920 | tf_op jit(solution)/shard_map/ppermute | solution.py:474
  19.1 3.6 %copy-start.6 = (bf16[96,1024]{1,0:T(8,128)(2,1)S(1)}, bf16[96,1024]{1,0:T(8,128)(2,1)}, u32[]{:S(2)}) copy-start(bf16[96,1024]{1,0:T(8,128)(2,1)} %wout_ref.3) | copy-start | bytes 589828
  22.7 8.4 %copy-start.7 = (f32[96,128]{1,0:T(8,128)S(1)}, f32[96,128]{1,0:T(8,128)}, u32[]{:S(2)}) copy-start(f32[96,128]{1,0:T(8,128)} %truth_ref.1) | copy-start | bytes 147460
  22.7 8.4 %copy-start.10 = (f32[128]{0:T(128)S(1)}, f32[128]{0:T(128)}, u32[]{:S(2)}) copy-start(f32[128]{0:T(128)} %param.19) | copy-start | bytes 1540
  22.7 8.4 %copy-start.11 = (f32[96]{0:T(128)S(1)}, f32[96]{0:T(128)}, u32[]{:S(2)}) copy-start(f32[96]{0:T(128)} %param.20) | copy-start | bytes 1156
  25.1 4.7 %collective-permute-start.7 = (f32[2,96,128]{2,1,0:T(8,128)S(1)}, f32[2,96,128]{2,1,0:T(8,128)S(1)}, u32[]{:S(2)}, u32[]{:S(2)}) collective-permute-start(f32[2,96,128]{2,1,0:T(8,128)S(1)} %get-tuple-element.54.mine_ref), channel_id=1, source_target_pairs={{0,2},{1,3},{2,0},{3,1},{4,6},{5,7},{6,4},{7,5},{8,10},{9,11},{10,... | collective-permute-start | bytes 294920 | tf_op jit(solution)/shard_map/ppermute | solution.py:549
  26.7 3.1 %collective-permute-start.8 = (f32[2,96,128]{2,1,0:T(8,128)S(1)}, f32[2,96,128]{2,1,0:T(8,128)S(1)}, u32[]{:S(2)}, u32[]{:S(2)}) collective-permute-start(f32[2,96,128]{2,1,0:T(8,128)S(1)} %get-tuple-element.54.mine_ref), channel_id=1, source_target_pairs={{0,1},{1,0},{2,3},{3,2},{4,5},{5,4},{6,7},{7,6},{8,9},{9,8},{10,11... | collective-permute-start | bytes 294920 | tf_op jit(solution)/shard_map/ppermute | solution.py:549
  29.8 1.3 %collective-permute-start.9 = (f32[2,96,128]{2,1,0:T(8,128)S(1)}, f32[2,96,128]{2,1,0:T(8,128)S(1)}, u32[]{:S(2)}, u32[]{:S(2)}) collective-permute-start(f32[2,96,128]{2,1,0:T(8,128)S(1)} %collective-permute-done.7.refs_0_), channel_id=1, source_target_pairs={{0,1},{1,0},{2,3},{3,2},{4,5},{5,4},{6,7},{7,6},{8,9},{9,8},{10,11... | collective-permute-start | bytes 294920 | tf_op jit(solution)/shard_map/ppermute | solution.py:549
  34.2 10.4 %collective-permute-start.10 = (bf16[48,1024]{1,0:T(8,128)(2,1)S(1)}, bf16[48,1024]{1,0:T(8,128)(2,1)S(1)}, u32[]{:S(2)}, u32[]{:S(2)}) collective-permute-start(bf16[48,1024]{1,0:T(8,128)(2,1)S(1)} %get-tuple-element.58), channel_id=1, source_target_pairs={{0,16},{4,20},{8,24},{12,28},{16,0},{20,4},{24,8},{28,12},{1,17},{... | collective-permute-start | bytes 294920 | tf_op jit(solution)/shard_map/ppermute | solution.py:474
  38.2 9.4 %collective-permute-start.11 = (bf16[48,1024]{1,0:T(8,128)(2,1)S(1)}, bf16[48,1024]{1,0:T(8,128)(2,1)S(1)}, u32[]{:S(2)}, u32[]{:S(2)}) collective-permute-start(bf16[48,1024]{1,0:T(8,128)(2,1)S(1)} %get-tuple-element.59), channel_id=1, source_target_pairs={{0,28},{4,0},{8,4},{12,8},{16,12},{20,16},{24,20},{28,24},{1,29},{... | collective-permute-start | bytes 294920 | tf_op jit(solution)/shard_map/ppermute | solution.py:474
  39.5 8.3 %collective-permute-start.12 = (bf16[48,1024]{1,0:T(8,128)(2,1)S(1)}, bf16[48,1024]{1,0:T(8,128)(2,1)S(1)}, u32[]{:S(2)}, u32[]{:S(2)}) collective-permute-start(bf16[48,1024]{1,0:T(8,128)(2,1)S(1)} %get-tuple-element.60), channel_id=1, source_target_pairs={{0,4},{4,8},{8,12},{12,16},{16,20},{20,24},{24,28},{28,0},{1,5},{5... | collective-permute-start | bytes 294920 | tf_op jit(solution)/shard_map/ppermute | solution.py:474
  41.7 7.9 %collective-permute-start.13 = (bf16[48,1024]{1,0:T(8,128)(2,1)S(1)}, bf16[48,1024]{1,0:T(8,128)(2,1)S(1)}, u32[]{:S(2)}, u32[]{:S(2)}) collective-permute-start(bf16[48,1024]{1,0:T(8,128)(2,1)S(1)} %get-tuple-element.63), channel_id=1, source_target_pairs={{0,20},{4,24},{8,28},{12,0},{16,4},{20,8},{24,12},{28,16},{1,21},{... | collective-permute-start | bytes 294920 | tf_op jit(solution)/shard_map/ppermute | solution.py:474
  43.4 11.0 %collective-permute-start.14 = (bf16[48,1024]{1,0:T(8,128)(2,1)S(1)}, bf16[48,1024]{1,0:T(8,128)(2,1)S(1)}, u32[]{:S(2)}, u32[]{:S(2)}) collective-permute-start(bf16[48,1024]{1,0:T(8,128)(2,1)S(1)} %get-tuple-element.64), channel_id=1, source_target_pairs={{0,12},{4,16},{8,20},{12,24},{16,28},{20,0},{24,4},{28,8},{1,13},{... | collective-permute-start | bytes 294920 | tf_op jit(solution)/shard_map/ppermute | solution.py:474
  44.6 10.0 %collective-permute-start.15 = (bf16[48,1024]{1,0:T(8,128)(2,1)S(1)}, bf16[48,1024]{1,0:T(8,128)(2,1)S(1)}, u32[]{:S(2)}, u32[]{:S(2)}) collective-permute-start(bf16[48,1024]{1,0:T(8,128)(2,1)S(1)} %get-tuple-element.65), channel_id=1, source_target_pairs={{0,24},{4,28},{8,0},{12,4},{16,8},{20,12},{24,16},{28,20},{1,25},{... | collective-permute-start | bytes 294920 | tf_op jit(solution)/shard_map/ppermute | solution.py:474
  47.6 7.1 %collective-permute-start.16 = (bf16[48,1024]{1,0:T(8,128)(2,1)S(1)}, bf16[48,1024]{1,0:T(8,128)(2,1)S(1)}, u32[]{:S(2)}, u32[]{:S(2)}) collective-permute-start(bf16[48,1024]{1,0:T(8,128)(2,1)S(1)} %get-tuple-element.66), channel_id=1, source_target_pairs={{0,8},{4,12},{8,16},{12,20},{16,24},{20,28},{24,0},{28,4},{1,9},{5... | collective-permute-start | bytes 294920 | tf_op jit(solution)/shard_map/ppermute | solution.py:474

commit v6 on v5

--- a/solution.py
+++ b/solution.py
@@ -249,8 +249,33 @@
             out_ref[:, cols] = rows[c * step : (c + 1) * step]
 
 
+def pair_terms(mine, other_refs):
+    total = jnp.zeros_like(mine)
+    for other_ref in other_refs:
+        for f in range(other_ref.shape[0]):
+            paired = mine - other_ref[f]
+            total = total + paired * lax.rsqrt(1.0 + paired * paired)
+    return total
+
+
+def score_kernel(ensemble, mine_ref, truth_ref, area_ref, var_ref, *refs):
+    *other_refs, base_ref, factor_ref = refs
+    variables = var_ref.shape[1]
+    wide = -variables % LANES
+    var = jnp.concatenate([var_ref[...], jnp.zeros((1, wide), F32)], axis=1)
+    var = jnp.broadcast_to(var, (LANES, variables + wide)).T[:variables, :1]
+    factor_ref[...] = area_ref[...] * var
+    for m in range(mine_ref.shape[0]):
+        mine = mine_ref[m]
+        miss = mine - truth_ref[...]
+        first = miss * lax.rsqrt(1.0 + miss * miss) / ensemble
+        second = pair_terms(mine, [mine_ref, *other_refs]) / (ensemble * (ensemble - 1))
+        base_ref[m] = first - second
+
+
 def backward_kernel(
     members,
+    ensemble,
     chunks,
     capacity,
     head_size,
@@ -259,9 +284,8 @@
     wvt_ref,
     wout_ref,
     mine_ref,
-    truth_ref,
-    area_ref,
-    var_ref,
+    base_ref,
+    factor_ref,
     weight_ref,
     v_ref,
     *refs,
@@ -271,30 +295,17 @@
     ds_ref, da_ref, dk_scr, dv_scr, sum_scr, dat_scr = refs[-6:]
     now = chunks * capacity
     width = wkt_ref.shape[1]
-    points = truth_ref.shape[1]
-    every_refs = (mine_ref, *other_refs)
-    total = sum(r.shape[0] for r in every_refs)
+    points = base_ref.shape[2]
     per = LANES // head_size
     groups = width // LANES
     scale = head_size ** (-0.5)
-    variables = var_ref.shape[1]
-    wide = -variables % LANES
-    var = jnp.concatenate([var_ref[...], jnp.zeros((1, wide), F32)], axis=1)
-    var = jnp.broadcast_to(var, (LANES, variables + wide)).T[:variables, :1]
-    factor = area_ref[...] * var
     head = lax.broadcasted_iota(jnp.int32, (points, 2 * LANES), 1) // head_size % per
     turned = lax.broadcasted_iota(jnp.int32, (2 * LANES, points), 0) // head_size % per
     dpreds = []
     for m in range(members):
         mine = mine_ref[m]
-        miss = mine - truth_ref[...]
-        first = miss * lax.rsqrt(1.0 + miss * miss) / total
-        second = jnp.zeros_like(mine)
-        for every_ref in every_refs:
-            for f in range(every_ref.shape[0]):
-                paired = mine - every_ref[f]
-                second = second + paired * lax.rsqrt(1.0 + paired * paired)
-        dpred = (factor * (first - second / (total * (total - 1)))).astype(BF16)
+        more = pair_terms(mine, other_refs) / (ensemble * (ensemble - 1))
+        dpred = (factor_ref[...] * (base_ref[m] - more)).astype(BF16)
         dpreds.append(dpred)
     tile = 2 * LANES
     tiles = width // tile
@@ -548,11 +559,24 @@
         pairs = [(i, i ^ bit) for i in range(ensembles)]
         everyone += [lax.ppermute(p, "member", pairs) for p in everyone]
         bit //= 2
+    total = members * ensembles
+    known = max(len(everyone) - 1, 1)
+    base, factor = call(
+        functools.partial(score_kernel, total),
+        [
+            jax.ShapeDtypeStruct((members, variables, points), F32),
+            jax.ShapeDtypeStruct((variables, points), F32),
+        ],
+        [predicted, truth, area[None, :], var_weight[None, :], *everyone[1:known]],
+        flops=8 * total * members * variables * points,
+    )
     late_grad = jax.ShapeDtypeStruct(
         (members, groups, len(late) * capacity, per * points), BF16
     )
     *leaving_early, d_scores, d_attended = call(
-        functools.partial(backward_kernel, members, len(early), capacity, head_size),
+        functools.partial(
+            backward_kernel, members, total, len(early), capacity, head_size
+        ),
         [chunk_shape] * len(early)
         + [late_grad, jax.ShapeDtypeStruct((members, per * points, width), BF16)],
         [
@@ -561,12 +585,11 @@
             w_value_t,
             w_out,
             predicted,
-            truth,
-            area[None, :],
-            var_weight[None, :],
+            base,
+            factor,
             weights,
             values,
-            *everyone[1:],
+            *everyone[known:],
         ],
         scratch=[pltpu.VMEM((len(early) * step, width), BF16)] * 2
         + [

time: 56.6 us -> 56.2 us (level)
    pallas_call x9 -> x10, Pallas kernels: 10.4 us -> 10.2 us  [call(): pl.pallas_call(kernel, out_shape=out_shape, in_specs=[SMEM if i in scalar...]
  transfers between devices with their start and end apart: 17 -> 17, of which waited for: 8 -> 8; matrix products, arithmetic and copies ran while one was open for 0% -> 0% of each run, Pallas kernels for 7% -> 8%
where the time goes in v6:
time: 56.2 us; the launch traced here: 56 us
  starting transfers between devices  30 us (53%)
  waiting for transfers between devices  12.7 us (23%)
  Pallas kernels  11.9 us (21%)
  local copies, waits for them, and re-layouts  1.22 us (2%)
    ppermute x14, starting transfers between devices, exchanged(): lax.ppermute(b, 'grid', [(i, (i + sign * s) % chunks) for i in range(chun...  28.5 us
    pallas_call x10, Pallas kernels, call(): pl.pallas_call(kernel, out_shape=out_shape, in_specs=[SMEM if i in scalar...  10.2 us
    ppermute x14, waiting for transfers between devices, exchanged(): lax.ppermute(b, 'grid', [(i, (i + sign * s) % chunks) for i in range(chun...  8.52 us
    ppermute x3, waiting for transfers between devices, on_device(): everyone += [lax.ppermute(p, 'member', pairs) for p in everyone]  4.16 us
    pallas_call x1, Pallas kernels, last_sum(): pl.pallas_call(functools.partial(last_sum_kernel, members, capacity), out...  1.75 us
    ppermute x3, starting transfers between devices, on_device(): everyone += [lax.ppermute(p, 'member', pairs) for p in everyone]  1.56 us
    unnamed x24, local copies, waits for them, and re-layouts  1.22 us
  transfers between devices with their start and end apart: 17, of which 8 were waited for; matrix products, arithmetic and copies ran while one was open for 0% of the time, Pallas kernels for 8%

profile of v6, /device:TPU:0, one launch (start us, length us, event | category | flops | bytes accessed | tf_op | source)
XLA Modules:
  0.0 56.0 jit_solution(14214847587838387327)
XLA Ops:
  0.0 0.7 %copy-done.1 = s32[1,8,24]{2,1,0:T(8,128)S(1)} copy-done((s32[1,8,24]{2,1,0:T(8,128)S(1)}, s32[1,8,24]{2,1,0:T(8,128)}, u32[]{:S(2)}) %copy-start.1) | copy-done | bytes 792
  0.7 0.1 shard_map.120.pick_ref
  0.8 0.5 copy-done.7
  1.3 0.6 %shard_map.121 = (bf16[48,1024]{1,0:T(8,128)(2,1)S(1)}, bf16[48,1024]{1,0:T(8,128)(2,1)S(1)}, bf16[48,1024]{1,0:T(8,128)(2,1)S(1)}, bf16[48,1024]{1,0:T(8,128)(2...) custom-call(bf16[2,320,1024]{2,1,0:T(8,128)(2,1)S(1)} %copy-done.7, ...), custom_call_target="tpu_custom_call" | custom-call | flops 10066329600 | bytes 2220032 | tf_op jit(solution)/shard_map/pallas_call | solution.py:35
  2.0 4.1 %collective-permute-start = (bf16[48,1024]{1,0:T(8,128)(2,1)S(1)}, bf16[48,1024]{1,0:T(8,128)(2,1)S(1)}, u32[]{:S(2)}, u32[]{:S(2)}) collective-permute-start(bf16[48,1024]{1,0:T(8,128)(2,1)S(1)} %get-tuple-element.41), channel_id=1, source_target_pairs={{0,16},{4,20},{8,24},{12,28},{16,0},{20,4},{24,8},{28,12},{1,17},{... | collective-permute-start | bytes 294920 | tf_op jit(solution)/shard_map/ppermute | solution.py:485
  6.0 1.5 %collective-permute-start.1 = (bf16[48,1024]{1,0:T(8,128)(2,1)S(1)}, bf16[48,1024]{1,0:T(8,128)(2,1)S(1)}, u32[]{:S(2)}, u32[]{:S(2)}) collective-permute-start(bf16[48,1024]{1,0:T(8,128)(2,1)S(1)} %get-tuple-element.42), channel_id=1, source_target_pairs={{0,4},{4,8},{8,12},{12,16},{16,20},{20,24},{24,28},{28,0},{1,5},{5... | collective-permute-start | bytes 294920 | tf_op jit(solution)/shard_map/ppermute | solution.py:485
  7.6 3.2 %collective-permute-start.2 = (bf16[48,1024]{1,0:T(8,128)(2,1)S(1)}, bf16[48,1024]{1,0:T(8,128)(2,1)S(1)}, u32[]{:S(2)}, u32[]{:S(2)}) collective-permute-start(bf16[48,1024]{1,0:T(8,128)(2,1)S(1)} %get-tuple-element.43), channel_id=1, source_target_pairs={{0,28},{4,0},{8,4},{12,8},{16,12},{20,16},{24,20},{28,24},{1,29},{... | collective-permute-start | bytes 294920 | tf_op jit(solution)/shard_map/ppermute | solution.py:485
  10.8 3.8 %collective-permute-start.4 = (bf16[48,1024]{1,0:T(8,128)(2,1)S(1)}, bf16[48,1024]{1,0:T(8,128)(2,1)S(1)}, u32[]{:S(2)}, u32[]{:S(2)}) collective-permute-start(bf16[48,1024]{1,0:T(8,128)(2,1)S(1)} %get-tuple-element.53), channel_id=1, source_target_pairs={{0,20},{4,24},{8,28},{12,0},{16,4},{20,8},{24,12},{28,16},{1,21},{... | collective-permute-start | bytes 294920 | tf_op jit(solution)/shard_map/ppermute | solution.py:485
  14.6 0.6 %shard_map.118 = (bf16[256,1024]{1,0:T(8,128)(2,1)S(1)}, bf16[1024,256]{1,0:T(8,128)(2,1)S(1)}, f32[192,128]{1,0:T(8,128)S(1)}) custom-call(bf16[128,1024]{1,0:T(8,128)(2,1)S(1)} %copy-done.8, bf16[1024,1024]{1,0:T(8,128)(2,1)S(1)} %copy-done.4, s32[16,128]{1,0:T(8,128)S(1)} %bitcast.7, s32[1,128]{1,0:T(1,128)S(1)} %bitcast.8, s32[1]{0:T(128)} %bitcast.2.me_ref), custom_call_target="tpu_custom_call" | custom-call | flops 10737418240 | bytes 3514884 | tf_op jit(solution)/shard_map/pallas_call | solution.py:35
  15.3 3.8 %collective-permute-start.6 = (bf16[48,1024]{1,0:T(8,128)(2,1)S(1)}, bf16[48,1024]{1,0:T(8,128)(2,1)S(1)}, u32[]{:S(2)}, u32[]{:S(2)}) collective-permute-start(bf16[48,1024]{1,0:T(8,128)(2,1)S(1)} %get-tuple-element.55), channel_id=1, source_target_pairs={{0,24},{4,28},{8,0},{12,4},{16,8},{20,12},{24,16},{28,20},{1,25},{... | collective-permute-start | bytes 294920 | tf_op jit(solution)/shard_map/ppermute | solution.py:485
  19.1 1.6 %shard_map.122 = (f32[2,8,96,256]{3,2,1,0:T(8,128)S(1)}, f32[2,8,1,256]{3,2,1,0:T(1,128)S(1)}, bf16[2,96,1024]{2,1,0:T(8,128)(2,1)S(1)}, bf16[1024,1024]{1,0:T(8...) custom-call(bf16[1024,256]{1,0:T(8,128)(2,1)S(1)} %get-tuple-element.38.qmt, ...), custom_call_target="tpu_custom_call" | custom-call | flops 32212254720 | bytes 11510532 | tf_op jit(solution)/shard_map/pallas_call | solution.py:35
  20.8 0.9 %collective-permute-done.5.refs_5_ = bf16[48,1024]{1,0:T(8,128)(2,1)S(1)} collective-permute-done((bf16[48,1024]{1,0:T(8,128)(2,1)S(1)}, bf16[48,1024]{1,0:T(8,128)(2,1)S(1)}, u32[]{:S(2)}, u32[]{:S(2)}) %collective-permute-start.5) | collective-permute-done | bytes 98336 | tf_op jit(solution)/shard_map/ppermute | solution.py:485
  21.8 0.9 %collective-permute-done.6.refs_6_ = bf16[48,1024]{1,0:T(8,128)(2,1)S(1)} collective-permute-done((bf16[48,1024]{1,0:T(8,128)(2,1)S(1)}, bf16[48,1024]{1,0:T(8,128)(2,1)S(1)}, u32[]{:S(2)}, u32[]{:S(2)}) %collective-permute-start.6) | collective-permute-done | bytes 98336 | tf_op jit(solution)/shard_map/ppermute | solution.py:485
  22.7 2.3 %shard_map.123 = (f32[2,96,128]{2,1,0:T(8,128)S(1)}, bf16[2,8,192,256]{3,2,1,0:T(8,128)(2,1)S(1)}, bf16[2,192,1024]{2,1,0:T(8,128)(2,1)S(1)}) custom-call(bf16[1024,256]{1,0:T(8,128)(2,1)S(1)} %get-tuple-element.38.qmt_ref, bf16[1024,1024]{1,0:T(8,128)(2,1)S(1)} %copy-done.5, bf16[1024,1024]{1,0:T(8,128)(2,1)S(1)} %copy-done.6, ...), custom_call_target="tpu_custom_call" | custom-call | flops 32212254720 | bytes 9846784 | tf_op jit(solution)/shard_map/pallas_call | solution.py:35
  25.1 1.6 %collective-permute-start.7 = (f32[2,96,128]{2,1,0:T(8,128)S(1)}, f32[2,96,128]{2,1,0:T(8,128)S(1)}, u32[]{:S(2)}, u32[]{:S(2)}) collective-permute-start(f32[2,96,128]{2,1,0:T(8,128)S(1)} %get-tuple-element.56.mine_ref), channel_id=1, source_target_pairs={{0,2},{1,3},{2,0},{3,1},{4,6},{5,7},{6,4},{7,5},{8,10},{9,11},{10,... | collective-permute-start | bytes 294920 | tf_op jit(solution)/shard_map/ppermute | solution.py:560
  26.6 3.1 %collective-permute-done.7.refs_0_ = f32[2,96,128]{2,1,0:T(8,128)S(1)} collective-permute-done((f32[2,96,128]{2,1,0:T(8,128)S(1)}, f32[2,96,128]{2,1,0:T(8,128)S(1)}, u32[]{:S(2)}, u32[]{:S(2)}) %collective-permute-start.7) | collective-permute-done | bytes 98336 | tf_op jit(solution)/shard_map/ppermute | solution.py:560
  29.8 0.2 shard_map.124
  30.0 1.0 %collective-permute-done.9.refs_0_ = f32[2,96,128]{2,1,0:T(8,128)S(1)} collective-permute-done((f32[2,96,128]{2,1,0:T(8,128)S(1)}, f32[2,96,128]{2,1,0:T(8,128)S(1)}, u32[]{:S(2)}, u32[]{:S(2)}) %collective-permute-start.9) | collective-permute-done | bytes 98336 | tf_op jit(solution)/shard_map/ppermute | solution.py:560
  31.0 2.8 %shard_map.125 = (bf16[48,1024]{1,0:T(8,128)(2,1)S(1)}, bf16[48,1024]{1,0:T(8,128)(2,1)S(1)}, bf16[48,1024]{1,0:T(8,128)(2,1)S(1)}, bf16[48,1024]{1,0:T(8,128)(2...) custom-call(bf16[256,1024]{1,0:T(8,128)(2,1)S(1)} %get-tuple-element.46.qm_ref, ...), custom_call_target="tpu_custom_call" | custom-call | flops 64424509440 | bytes 9846784 | tf_op jit(solution)/shard_map/pallas_call | solution.py:35
  33.8 4.0 %collective-permute-start.10 = (bf16[48,1024]{1,0:T(8,128)(2,1)S(1)}, bf16[48,1024]{1,0:T(8,128)(2,1)S(1)}, u32[]{:S(2)}, u32[]{:S(2)}) collective-permute-start(bf16[48,1024]{1,0:T(8,128)(2,1)S(1)} %get-tuple-element.62), channel_id=1, source_target_pairs={{0,16},{4,20},{8,24},{12,28},{16,0},{20,4},{24,8},{28,12},{1,17},{... | collective-permute-start | bytes 294920 | tf_op jit(solution)/shard_map/ppermute | solution.py:485
  37.8 1.4 %collective-permute-start.11 = (bf16[48,1024]{1,0:T(8,128)(2,1)S(1)}, bf16[48,1024]{1,0:T(8,128)(2,1)S(1)}, u32[]{:S(2)}, u32[]{:S(2)}) collective-permute-start(bf16[48,1024]{1,0:T(8,128)(2,1)S(1)} %get-tuple-element.63), channel_id=1, source_target_pairs={{0,28},{4,0},{8,4},{12,8},{16,12},{20,16},{24,20},{28,24},{1,29},{... | collective-permute-start | bytes 294920 | tf_op jit(solution)/shard_map/ppermute | solution.py:485
  39.2 0.7 %collective-permute-start.12 = (bf16[48,1024]{1,0:T(8,128)(2,1)S(1)}, bf16[48,1024]{1,0:T(8,128)(2,1)S(1)}, u32[]{:S(2)}, u32[]{:S(2)}) collective-permute-start(bf16[48,1024]{1,0:T(8,128)(2,1)S(1)} %get-tuple-element.64), channel_id=1, source_target_pairs={{0,4},{4,8},{8,12},{12,16},{16,20},{20,24},{24,28},{28,0},{1,5},{5... | collective-permute-start | bytes 294920 | tf_op jit(solution)/shard_map/ppermute | solution.py:485
  39.8 1.4 %shard_map.127 = (bf16[48,1024]{1,0:T(8,128)(2,1)S(1)}, bf16[48,1024]{1,0:T(8,128)(2,1)S(1)}, bf16[48,1024]{1,0:T(8,128)(2,1)S(1)}, bf16[48,1024]{1,0:T(8,128)(2,1)S(1)}) custom-call(bf16[256,1024]{1,0:T(8,128)(2,1)S(1)} %get-tuple-element.46.qm_ref, bf16[1024,1024]{1,0:T(8,128)(2,1)S(1)} %get-tuple-element.47.wkt_ref, ...), custom_call_target="tpu_custom_call" | custom-call | flops 32212254720 | bytes 8519680 | tf_op jit(solution)/shard_map/pallas_call | solution.py:35
  41.2 1.7 %collective-permute-start.13 = (bf16[48,1024]{1,0:T(8,128)(2,1)S(1)}, bf16[48,1024]{1,0:T(8,128)(2,1)S(1)}, u32[]{:S(2)}, u32[]{:S(2)}) collective-permute-start(bf16[48,1024]{1,0:T(8,128)(2,1)S(1)} %get-tuple-element.67), channel_id=1, source_target_pairs={{0,20},{4,24},{8,28},{12,0},{16,4},{20,8},{24,12},{28,16},{1,21},{... | collective-permute-start | bytes 294920 | tf_op jit(solution)/shard_map/ppermute | solution.py:485
  43.0 1.2 %collective-permute-start.14 = (bf16[48,1024]{1,0:T(8,128)(2,1)S(1)}, bf16[48,1024]{1,0:T(8,128)(2,1)S(1)}, u32[]{:S(2)}, u32[]{:S(2)}) collective-permute-start(bf16[48,1024]{1,0:T(8,128)(2,1)S(1)} %get-tuple-element.68), channel_id=1, source_target_pairs={{0,12},{4,16},{8,20},{12,24},{16,28},{20,0},{24,4},{28,8},{1,13},{... | collective-permute-start | bytes 294920 | tf_op jit(solution)/shard_map/ppermute | solution.py:485
  44.2 3.0 %collective-permute-start.15 = (bf16[48,1024]{1,0:T(8,128)(2,1)S(1)}, bf16[48,1024]{1,0:T(8,128)(2,1)S(1)}, u32[]{:S(2)}, u32[]{:S(2)}) collective-permute-start(bf16[48,1024]{1,0:T(8,128)(2,1)S(1)} %get-tuple-element.69), channel_id=1, source_target_pairs={{0,24},{4,28},{8,0},{12,4},{16,8},{20,12},{24,16},{28,20},{1,25},{... | collective-permute-start | bytes 294920 | tf_op jit(solution)/shard_map/ppermute | solution.py:485
  47.2 0.2 collective-permute-done.12.refs_3_
  47.4 0.5 shard_map.126.before_ref
  47.9 1.3 %collective-permute-done.13.refs_0_ = bf16[48,1024]{1,0:T(8,128)(2,1)S(1)} collective-permute-done((bf16[48,1024]{1,0:T(8,128)(2,1)S(1)}, bf16[48,1024]{1,0:T(8,128)(2,1)S(1)}, u32[]{:S(2)}, u32[]{:S(2)}) %collective-permute-start.13) | collective-permute-done | bytes 98336 | tf_op jit(solution)/shard_map/ppermute | solution.py:485
  49.2 4.9 %collective-permute-done.14.refs_1_ = bf16[48,1024]{1,0:T(8,128)(2,1)S(1)} collective-permute-done((bf16[48,1024]{1,0:T(8,128)(2,1)S(1)}, bf16[48,1024]{1,0:T(8,128)(2,1)S(1)}, u32[]{:S(2)}, u32[]{:S(2)}) %collective-permute-start.14) | collective-permute-done | bytes 98336 | tf_op jit(solution)/shard_map/ppermute | solution.py:485
  54.1 0.2 collective-permute-done.15.refs_2_
  54.3 1.7 %shard_map.128 = f32[2,320,1024]{2,1,0:T(8,128)} custom-call(bf16[320,96]{1,0:T(8,128)(2,1)S(1)} %get-tuple-element.44.place_ref, f32[2,320,1024]{2,1,0:T(8,128)S(1)} %shard_map.126.before_ref, bf16[48,1024]{1,0:T(8,128)(2,1)S(1)} %collective-permute-done.13.refs_0_, bf16[48,1024]{1,0:T(8,128)(2,1)S(1)} %collective-permute-done.14.refs_1_, ...), custom_call_target="tpu_custom_call" | custom-call | flops 125829120 | bytes 5636096 | tf_op jit(solution)/shard_map/pallas_call | solution.py:428
  (37 shorter events, 0.2 us)
Async XLA Ops:
  0.0 0.7 %copy-start.1 = (s32[1,8,24]{2,1,0:T(8,128)S(1)}, s32[1,8,24]{2,1,0:T(8,128)}, u32[]{:S(2)}) copy-start(s32[1,8,24]{2,1,0:T(8,128)} %send_ref.3) | copy-start | bytes 2308
  0.0 1.3 %copy-start.7 = (bf16[2,320,1024]{2,1,0:T(8,128)(2,1)S(1)}, bf16[2,320,1024]{2,1,0:T(8,128)(2,1)}, u32[]{:S(2)}) copy-start(bf16[2,320,1024]{2,1,0:T(8,128)(2,1)} %latent_ref.1) | copy-start | bytes 3932164
  1.3 13.3 %copy-start.4 = (bf16[1024,1024]{1,0:T(8,128)(2,1)S(1)}, bf16[1024,1024]{1,0:T(8,128)(2,1)}, u32[]{:S(2)}) copy-start(bf16[1024,1024]{1,0:T(8,128)(2,1)} %w_ref.1) | copy-start | bytes 6291460
  1.3 13.3 %copy-start.8 = (bf16[128,1024]{1,0:T(8,128)(2,1)S(1)}, bf16[128,1024]{1,0:T(8,128)(2,1)}, u32[]{:S(2)}) copy-start(bf16[128,1024]{1,0:T(8,128)(2,1)} %feat_ref.1) | copy-start | bytes 786436
  1.3 13.3 %copy-start.10 = (s32[128,16]{0,1:T(8,128)S(1)}, s32[128,16]{0,1:T(8,128)}, u32[]{:S(2)}) copy-start(s32[128,16]{0,1:T(8,128)} %param.22) | copy-start | bytes 24580
  1.3 13.3 %copy-start.11 = (s32[128]{0:T(128)S(1)}, s32[128]{0:T(128)}, u32[]{:S(2)}) copy-start(s32[128]{0:T(128)} %param.23) | copy-start | bytes 1540
  2.0 13.3 %collective-permute-start = (bf16[48,1024]{1,0:T(8,128)(2,1)S(1)}, bf16[48,1024]{1,0:T(8,128)(2,1)S(1)}, u32[]{:S(2)}, u32[]{:S(2)}) collective-permute-start(bf16[48,1024]{1,0:T(8,128)(2,1)S(1)} %get-tuple-element.41), channel_id=1, source_target_pairs={{0,16},{4,20},{8,24},{12,28},{16,0},{20,4},{24,8},{28,12},{1,17},{... | collective-permute-start | bytes 294920 | tf_op jit(solution)/shard_map/ppermute | solution.py:485
  6.0 9.3 %collective-permute-start.1 = (bf16[48,1024]{1,0:T(8,128)(2,1)S(1)}, bf16[48,1024]{1,0:T(8,128)(2,1)S(1)}, u32[]{:S(2)}, u32[]{:S(2)}) collective-permute-start(bf16[48,1024]{1,0:T(8,128)(2,1)S(1)} %get-tuple-element.42), channel_id=1, source_target_pairs={{0,4},{4,8},{8,12},{12,16},{16,20},{20,24},{24,28},{28,0},{1,5},{5... | collective-permute-start | bytes 294920 | tf_op jit(solution)/shard_map/ppermute | solution.py:485
  7.6 11.6 %collective-permute-start.2 = (bf16[48,1024]{1,0:T(8,128)(2,1)S(1)}, bf16[48,1024]{1,0:T(8,128)(2,1)S(1)}, u32[]{:S(2)}, u32[]{:S(2)}) collective-permute-start(bf16[48,1024]{1,0:T(8,128)(2,1)S(1)} %get-tuple-element.43), channel_id=1, source_target_pairs={{0,28},{4,0},{8,4},{12,8},{16,12},{20,16},{24,20},{28,24},{1,29},{... | collective-permute-start | bytes 294920 | tf_op jit(solution)/shard_map/ppermute | solution.py:485
  10.8 10.0 %collective-permute-start.3 = (bf16[48,1024]{1,0:T(8,128)(2,1)S(1)}, bf16[48,1024]{1,0:T(8,128)(2,1)S(1)}, u32[]{:S(2)}, u32[]{:S(2)}) collective-permute-start(bf16[48,1024]{1,0:T(8,128)(2,1)S(1)} %get-tuple-element.52), channel_id=1, source_target_pairs={{0,12},{4,16},{8,20},{12,24},{16,28},{20,0},{24,4},{28,8},{1,13},{... | collective-permute-start | bytes 294920 | tf_op jit(solution)/shard_map/ppermute | solution.py:485
  10.8 10.0 %collective-permute-start.4 = (bf16[48,1024]{1,0:T(8,128)(2,1)S(1)}, bf16[48,1024]{1,0:T(8,128)(2,1)S(1)}, u32[]{:S(2)}, u32[]{:S(2)}) collective-permute-start(bf16[48,1024]{1,0:T(8,128)(2,1)S(1)} %get-tuple-element.53), channel_id=1, source_target_pairs={{0,20},{4,24},{8,28},{12,0},{16,4},{20,8},{24,12},{28,16},{1,21},{... | collective-permute-start | bytes 294920 | tf_op jit(solution)/shard_map/ppermute | solution.py:485
  14.6 4.5 %copy-start.5 = (bf16[1024,1024]{1,0:T(8,128)(2,1)S(1)}, bf16[1024,1024]{1,0:T(8,128)(2,1)}, u32[]{:S(2)}) copy-start(bf16[1024,1024]{1,0:T(8,128)(2,1)} %wk_ref.3) | copy-start | bytes 6291460
  14.6 4.5 %copy-start.6 = (bf16[1024,1024]{1,0:T(8,128)(2,1)S(1)}, bf16[1024,1024]{1,0:T(8,128)(2,1)}, u32[]{:S(2)}) copy-start(bf16[1024,1024]{1,0:T(8,128)(2,1)} %wv_ref.3) | copy-start | bytes 6291460
  15.2 6.5 %collective-permute-start.5 = (bf16[48,1024]{1,0:T(8,128)(2,1)S(1)}, bf16[48,1024]{1,0:T(8,128)(2,1)S(1)}, u32[]{:S(2)}, u32[]{:S(2)}) collective-permute-start(bf16[48,1024]{1,0:T(8,128)(2,1)S(1)} %get-tuple-element.54), channel_id=1, source_target_pairs={{0,8},{4,12},{8,16},{12,20},{16,24},{20,28},{24,0},{28,4},{1,9},{5... | collective-permute-start | bytes 294920 | tf_op jit(solution)/shard_map/ppermute | solution.py:485
  15.3 7.4 %collective-permute-start.6 = (bf16[48,1024]{1,0:T(8,128)(2,1)S(1)}, bf16[48,1024]{1,0:T(8,128)(2,1)S(1)}, u32[]{:S(2)}, u32[]{:S(2)}) collective-permute-start(bf16[48,1024]{1,0:T(8,128)(2,1)S(1)} %get-tuple-element.55), channel_id=1, source_target_pairs={{0,24},{4,28},{8,0},{12,4},{16,8},{20,12},{24,16},{28,20},{1,25},{... | collective-permute-start | bytes 294920 | tf_op jit(solution)/shard_map/ppermute | solution.py:485
  19.1 3.6 %copy-start.9 = (bf16[96,1024]{1,0:T(8,128)(2,1)S(1)}, bf16[96,1024]{1,0:T(8,128)(2,1)}, u32[]{:S(2)}) copy-start(bf16[96,1024]{1,0:T(8,128)(2,1)} %wout_ref.3) | copy-start | bytes 589828
  22.7 7.0 %copy-start = (f32[96,128]{1,0:T(8,128)S(1)}, f32[96,128]{1,0:T(8,128)}, u32[]{:S(2)}) copy-start(f32[96,128]{1,0:T(8,128)} %truth_ref.1) | copy-start | bytes 147460
  22.7 7.0 %copy-start.2 = (f32[128]{0:T(128)S(1)}, f32[128]{0:T(128)}, u32[]{:S(2)}) copy-start(f32[128]{0:T(128)} %param.19) | copy-start | bytes 1540
  22.7 7.0 %copy-start.3 = (f32[96]{0:T(128)S(1)}, f32[96]{0:T(128)}, u32[]{:S(2)}) copy-start(f32[96]{0:T(128)} %param.20) | copy-start | bytes 1156
  25.1 4.7 %collective-permute-start.7 = (f32[2,96,128]{2,1,0:T(8,128)S(1)}, f32[2,96,128]{2,1,0:T(8,128)S(1)}, u32[]{:S(2)}, u32[]{:S(2)}) collective-permute-start(f32[2,96,128]{2,1,0:T(8,128)S(1)} %get-tuple-element.56.mine_ref), channel_id=1, source_target_pairs={{0,2},{1,3},{2,0},{3,1},{4,6},{5,7},{6,4},{7,5},{8,10},{9,11},{10,... | collective-permute-start | bytes 294920 | tf_op jit(solution)/shard_map/ppermute | solution.py:560
  26.6 3.1 %collective-permute-start.8 = (f32[2,96,128]{2,1,0:T(8,128)S(1)}, f32[2,96,128]{2,1,0:T(8,128)S(1)}, u32[]{:S(2)}, u32[]{:S(2)}) collective-permute-start(f32[2,96,128]{2,1,0:T(8,128)S(1)} %get-tuple-element.56.mine_ref), channel_id=1, source_target_pairs={{0,1},{1,0},{2,3},{3,2},{4,5},{5,4},{6,7},{7,6},{8,9},{9,8},{10,11... | collective-permute-start | bytes 294920 | tf_op jit(solution)/shard_map/ppermute | solution.py:560
  29.7 1.3 %collective-permute-start.9 = (f32[2,96,128]{2,1,0:T(8,128)S(1)}, f32[2,96,128]{2,1,0:T(8,128)S(1)}, u32[]{:S(2)}, u32[]{:S(2)}) collective-permute-start(f32[2,96,128]{2,1,0:T(8,128)S(1)} %collective-permute-done.7.refs_0_), channel_id=1, source_target_pairs={{0,1},{1,0},{2,3},{3,2},{4,5},{5,4},{6,7},{7,6},{8,9},{9,8},{10,11... | collective-permute-start | bytes 294920 | tf_op jit(solution)/shard_map/ppermute | solution.py:560
  33.8 10.4 %collective-permute-start.10 = (bf16[48,1024]{1,0:T(8,128)(2,1)S(1)}, bf16[48,1024]{1,0:T(8,128)(2,1)S(1)}, u32[]{:S(2)}, u32[]{:S(2)}) collective-permute-start(bf16[48,1024]{1,0:T(8,128)(2,1)S(1)} %get-tuple-element.62), channel_id=1, source_target_pairs={{0,16},{4,20},{8,24},{12,28},{16,0},{20,4},{24,8},{28,12},{1,17},{... | collective-permute-start | bytes 294920 | tf_op jit(solution)/shard_map/ppermute | solution.py:485
  37.8 9.4 %collective-permute-start.11 = (bf16[48,1024]{1,0:T(8,128)(2,1)S(1)}, bf16[48,1024]{1,0:T(8,128)(2,1)S(1)}, u32[]{:S(2)}, u32[]{:S(2)}) collective-permute-start(bf16[48,1024]{1,0:T(8,128)(2,1)S(1)} %get-tuple-element.63), channel_id=1, source_target_pairs={{0,28},{4,0},{8,4},{12,8},{16,12},{20,16},{24,20},{28,24},{1,29},{... | collective-permute-start | bytes 294920 | tf_op jit(solution)/shard_map/ppermute | solution.py:485
  39.2 8.3 %collective-permute-start.12 = (bf16[48,1024]{1,0:T(8,128)(2,1)S(1)}, bf16[48,1024]{1,0:T(8,128)(2,1)S(1)}, u32[]{:S(2)}, u32[]{:S(2)}) collective-permute-start(bf16[48,1024]{1,0:T(8,128)(2,1)S(1)} %get-tuple-element.64), channel_id=1, source_target_pairs={{0,4},{4,8},{8,12},{12,16},{16,20},{20,24},{24,28},{28,0},{1,5},{5... | collective-permute-start | bytes 294920 | tf_op jit(solution)/shard_map/ppermute | solution.py:485
  41.2 7.9 %collective-permute-start.13 = (bf16[48,1024]{1,0:T(8,128)(2,1)S(1)}, bf16[48,1024]{1,0:T(8,128)(2,1)S(1)}, u32[]{:S(2)}, u32[]{:S(2)}) collective-permute-start(bf16[48,1024]{1,0:T(8,128)(2,1)S(1)} %get-tuple-element.67), channel_id=1, source_target_pairs={{0,20},{4,24},{8,28},{12,0},{16,4},{20,8},{24,12},{28,16},{1,21},{... | collective-permute-start | bytes 294920 | tf_op jit(solution)/shard_map/ppermute | solution.py:485
  43.0 11.1 %collective-permute-start.14 = (bf16[48,1024]{1,0:T(8,128)(2,1)S(1)}, bf16[48,1024]{1,0:T(8,128)(2,1)S(1)}, u32[]{:S(2)}, u32[]{:S(2)}) collective-permute-start(bf16[48,1024]{1,0:T(8,128)(2,1)S(1)} %get-tuple-element.68), channel_id=1, source_target_pairs={{0,12},{4,16},{8,20},{12,24},{16,28},{20,0},{24,4},{28,8},{1,13},{... | collective-permute-start | bytes 294920 | tf_op jit(solution)/shard_map/ppermute | solution.py:485
  44.2 10.1 %collective-permute-start.15 = (bf16[48,1024]{1,0:T(8,128)(2,1)S(1)}, bf16[48,1024]{1,0:T(8,128)(2,1)S(1)}, u32[]{:S(2)}, u32[]{:S(2)}) collective-permute-start(bf16[48,1024]{1,0:T(8,128)(2,1)S(1)} %get-tuple-element.69), channel_id=1, source_target_pairs={{0,24},{4,28},{8,0},{12,4},{16,8},{20,12},{24,16},{28,20},{1,25},{... | collective-permute-start | bytes 294920 | tf_op jit(solution)/shard_map/ppermute | solution.py:485
  47.2 7.1 %collective-permute-start.16 = (bf16[48,1024]{1,0:T(8,128)(2,1)S(1)}, bf16[48,1024]{1,0:T(8,128)(2,1)S(1)}, u32[]{:S(2)}, u32[]{:S(2)}) collective-permute-start(bf16[48,1024]{1,0:T(8,128)(2,1)S(1)} %get-tuple-element.70), channel_id=1, source_target_pairs={{0,8},{4,12},{8,16},{12,20},{16,24},{20,28},{24,0},{28,4},{1,9},{5... | collective-permute-start | bytes 294920 | tf_op jit(solution)/shard_map/ppermute | solution.py:485
